TPU v7x, 32 devices: a whole 2x2x4 slice. The times are simulated.
32 devices in a mesh: groups: 2 (over y), lat: 4 (over z), width: 4 (over x, core).
Axes of the slice: x: 2, y: 2, z: 4, core: 2. Of those that a mesh axis runs over, the one named last changes fastest.
Arguments:
- activations: bfloat16 [1024, 4096], P(('groups', 'lat'), 'width'), parts along dimension 0, may hold values from -6 to 6
- rest_recon: bfloat16 [1024, 4096], P(('groups', 'lat'), 'width'), parts along dimension 0, may hold values from -6 to 6
- w_enc: bfloat16 [4096, 768], P('width', 'lat'), may hold values from -0.09375 to 0.09375
- b_enc: float32 [768], P('lat'), may hold values from -3 to 3
- w_dec: bfloat16 [768, 4096], P('lat', 'width'), may hold values from -0.21875 to 0.21875
- b_dec: float32 [4096], P('width'), may hold values from -3 to 3
Outputs:
- grad_enc: float32 [8192, 768], P(('groups', 'width'), 'lat'), parts along dimension 0
- grad_benc: float32 [1536], P(('groups', 'lat')), parts along dimension 0
- grad_dec: float32 [1536, 4096], P(('groups', 'lat'), 'width'), parts along dimension 0
- grad_bdec: float32 [8192], P(('groups', 'width')), parts along dimension 0
There are 2 independent parts, one for each index of `groups`. A program takes and returns all parts, laid end to end along the dimension named above; an argument that names none is the same for every part. Nothing has to cross between parts.
All inputs are finite; a program needn't handle non-finite values.
Results may differ from a plain program's by a relative error of at most 0.012.
Values may be sent and summed in bfloat16 or wider, within the bound.
No kernel may reach another device: no remote copies, remote signals or barrier semaphores. Data moves between devices by JAX's collectives and lax.ppermute only.
A program may use at most 64 MiB of HBM per device.

v0:
```python
import jax
import jax.numpy as jnp
from jax import lax
from jax.sharding import PartitionSpec as P

sparsity_coef = 3.0


def shards(activations, rest_recon, w_enc, b_enc, w_dec, b_dec):
    lat_count = lax.axis_size("lat")
    local_rows = activations.shape[0]
    total_rows = local_rows * lat_count
    row_scale = 1.0 / jnp.sqrt(jnp.float32(total_rows))
    centered = (activations.astype(jnp.float32) - b_dec).astype(jnp.bfloat16)
    gathered = lax.all_gather(centered, "lat", axis=0, tiled=True)
    pre_part = jnp.dot(gathered, w_enc, preferred_element_type=jnp.float32)
    dec_float = w_dec.astype(jnp.float32)
    squares = jnp.sum(dec_float * dec_float, axis=1)
    square_sum = lax.psum(squares, "width")
    pre_total = lax.psum(pre_part.astype(jnp.bfloat16), "width").astype(jnp.float32)
    codes = jnp.maximum(pre_total + b_enc, 0.0).astype(jnp.bfloat16)
    norms = jnp.sqrt(square_sum + 1e-06)
    recon = lax.psum_scatter(
        jnp.dot(codes, w_dec, preferred_element_type=jnp.float32).astype(jnp.bfloat16),
        "lat",
        scatter_dimension=0,
        tiled=True,
    ).astype(jnp.float32)
    error_rows = rest_recon.astype(jnp.float32) + recon + b_dec - activations.astype(jnp.float32)
    res_grad = (2.0 * row_scale * error_rows).astype(jnp.bfloat16)
    whole_grad = lax.all_gather(res_grad, "lat", axis=0, tiled=True)
    code_part = lax.dot_general(
        whole_grad, w_dec, (((1,), (1,)), ((), ())), preferred_element_type=jnp.float32
    )
    code_sum = lax.psum(code_part.astype(jnp.bfloat16), "width").astype(jnp.float32)
    pre_grad = jnp.where(codes > 0, code_sum + sparsity_coef * row_scale * norms, 0.0).astype(
        jnp.bfloat16
    )
    grad_enc = lax.dot_general(
        gathered, pre_grad, (((0,), (0,)), ((), ())), preferred_element_type=jnp.float32
    )
    grad_benc = jnp.sum(pre_grad.astype(jnp.float32), axis=0)
    code_total = jnp.sum(codes.astype(jnp.float32), axis=0)
    grad_dec = lax.dot_general(
        codes, whole_grad, (((0,), (0,)), ((), ())), preferred_element_type=jnp.float32
    )
    grad_dec = grad_dec + (sparsity_coef * row_scale * code_total / norms)[:, None] * dec_float
    enc_term = jnp.dot(w_enc.astype(jnp.float32), grad_benc, precision=lax.Precision.HIGHEST)
    enc_total = lax.psum(enc_term, "lat")
    grad_bdec = jnp.sum(whole_grad.astype(jnp.float32), axis=0) - enc_total
    return (grad_enc, grad_benc, grad_dec, grad_bdec)


def solution(mesh):
    placed = (
        P(("groups", "lat"), "width"),
        P(("groups", "lat"), "width"),
        P("width", "lat"),
        P("lat"),
        P("lat", "width"),
        P("width"),
    )
    return jax.shard_map(
        shards,
        mesh=mesh,
        in_specs=placed,
        out_specs=(
            P(("groups", "width"), "lat"),
            P(("groups", "lat")),
            P(("groups", "lat"), "width"),
            P(("groups", "width")),
        ),
        check_vma=False,
    )
```

profile of v0, /device:TPU:0, one launch (start us, length us, event | category | flops | bytes accessed | tf_op | source)
XLA Modules:
  0.0 191.2 jit_solution(9668466926548899682)
XLA Ops:
  7.2 0.0 all-gather.3.cloned.1.call-start
  7.2 1.8 fusion.1
  9.0 0.0 all-reduce.3.cloned.1.call-start
  9.1 31.8 %all-gather.3.cloned.1.call-done = bf16[512,1024]{1,0:T(8,128)(2,1)} async-done(((bf16[128,1024]{1,0:T(8,128)(2,1)}), bf16[512,1024]{1,0:T(8,128)(2,1)}) %all-gather.3.cloned.1.call-update) | async-done | bytes 1048592 | tf_op jit(solution)/shard_map/all_gather | solution.py:15
  40.8 2.4 %convolution_convert_fusion.2 = bf16[512,192]{0,1:T(8,128)(2,1)} fusion(bf16[512,1024]{1,0:T(8,128)(2,1)} %all-gather.3.cloned.1.call-done, bf16[1024,192]{0,1:T(8,128)(2,1)S(1)} %copy-done), kind=kOutput, calls=%fused_computation.4 | convolution fusion | flops 201424896 | bytes 1638400 | tf_op jit(solution)/shard_map/dot_general | solution.py:16
  43.3 0.0 reduce-scatter.2.cloned.1.call-start
  43.3 31.6 %all-reduce.3.cloned.1.call-done = bf16[512,192]{0,1:T(8,128)(2,1)} async-done(((bf16[512,192]{0,1:T(8,128)(2,1)}), bf16[512,192]{0,1:T(8,128)(2,1)}) %all-reduce.3.cloned.1.call-update) | async-done | bytes 196624 | tf_op jit(solution)/shard_map/psum | solution.py:20
  74.9 2.5 %convolution_convert_fusion = bf16[512,1024]{1,0:T(8,128)(2,1)} fusion(bf16[192,1024]{1,0:T(8,128)(2,1)S(1)} %copy-done.2, bf16[512,192]{0,1:T(8,128)(2,1)} %all-reduce.3.cloned.1.call-done, f32[192]{0:T(256)S(1)} %copy-done.7), kind=kOutput, calls=%fused_computation.1 | convolution fusion | flops 202244096 | bytes 1639168 | tf_op jit(solution)/shard_map/dot_general | solution.py:24
  77.5 0.0 all-gather.5.cloned.1.call-start
  77.5 27.2 %reduce-scatter.2.cloned.1.call-done = bf16[128,1024]{1,0:T(8,128)(2,1)} async-done(((bf16[512,1024]{1,0:T(8,128)(2,1)}), bf16[128,1024]{1,0:T(8,128)(2,1)}) %reduce-scatter.2.cloned.1.call-update) | async-done | bytes 262160 | tf_op jit(solution)/shard_map/reduce_scatter | solution.py:23
  104.8 1.8 fusion.3
  106.6 0.0 all-reduce.5.cloned.1.call-start
  106.6 0.2 fusion
  106.8 6.4 %psum.30 = f32[192]{0:T(256)S(1)} all-reduce(f32[192]{0:T(256)S(1)} %fusion), channel_id=1, replica_groups=mesh['groups'=2,'lat'=4,'width'=4] {'width'}, use_global_device_ids=true, to_apply=%region_4.0 | all-reduce | flops 192 | bytes 1536 | tf_op jit(solution)/shard_map/psum | solution.py:19
  113.2 20.2 %all-gather.5.cloned.1.call-done = bf16[512,1024]{1,0:T(8,128)(2,1)} async-done(((bf16[128,1024]{1,0:T(8,128)(2,1)}), bf16[512,1024]{1,0:T(8,128)(2,1)}) %all-gather.5.cloned.1.call-update) | async-done | bytes 1048592 | tf_op jit(solution)/shard_map/all_gather | solution.py:31
  133.4 2.5 %convolution_convert_fusion.1 = bf16[512,192]{0,1:T(8,128)(2,1)} fusion(bf16[512,1024]{1,0:T(8,128)(2,1)} %all-gather.5.cloned.1.call-done, bf16[192,1024]{1,0:T(8,128)(2,1)S(1)} %copy-done.2), kind=kOutput, calls=%fused_computation.3 | convolution fusion | flops 201424896 | bytes 1638400 | tf_op jit(solution)/shard_map/dot_general | solution.py:32
  135.9 0.2 convert_reduce_fusion
  136.1 31.2 %all-reduce.5.cloned.1.call-done = bf16[512,192]{0,1:T(8,128)(2,1)} async-done(((bf16[512,192]{0,1:T(8,128)(2,1)}), bf16[512,192]{0,1:T(8,128)(2,1)}) %all-reduce.5.cloned.1.call-update) | async-done | bytes 196624 | tf_op jit(solution)/shard_map/psum | solution.py:35
  167.3 1.2 convert_reduce_fusion.1
  168.6 0.3 fusion.6
  168.8 11.7 %psum.31 = f32[1024]{0:T(1024)S(1)} all-reduce(f32[1024]{0:T(1024)S(1)} %bitcast.11), channel_id=1, replica_groups=mesh['groups'=2,'lat'=4,'width'=4] {'lat'}, use_global_device_ids=true, to_apply=%region_8.9 | all-reduce | flops 1024 | bytes 8192 | tf_op jit(solution)/shard_map/psum | solution.py:49
  180.5 0.6 sub.17
  181.1 2.2 %fusion.5 = f32[1024,192]{0,1:T(8,128)} fusion(bf16[512,1024]{1,0:T(8,128)(2,1)S(1)} %copy-done.3, bf16[512,192]{0,1:T(8,128)(2,1)} %all-reduce.5.cloned.1.call-done, f32[192]{0:T(256)S(1)} %fusion.4, bf16[512,192]{0,1:T(8,128)(2,1)S(1)} %copy-done.4, f32[192]{0:T(256)S(1)} %copy-done.7), kind=kOutput, calls=%fused_computation.20 | convolution fusion | flops 202211328 | bytes 2229760 | tf_op jit(solution)/shard_map/dot_general | solution.py:39
  183.4 1.3 convolution_add_fusion
  (27 shorter events, 0.2 us)
Async XLA Ops:
  7.2 33.7 %copy-start = (bf16[1024,192]{0,1:T(8,128)(2,1)S(1)}, bf16[1024,192]{0,1:T(8,128)(2,1)}, u32[]{:S(2)}) copy-start(bf16[1024,192]{0,1:T(8,128)(2,1)} %param.8) | copy-start | bytes 1179652
  7.2 33.6 %all-gather.3.cloned.1.call-start = ((), (), s32[]{:S(2)}) async-start(), calls=%async_computation.1 | async-start | bytes 1310720 | tf_op jit(solution)/shard_map/all_gather | solution.py:15
  9.0 65.9 %copy-start.2 = (bf16[192,1024]{1,0:T(8,128)(2,1)S(1)}, bf16[192,1024]{1,0:T(8,128)(2,1)}, u32[]{:S(2)}) copy-start(bf16[192,1024]{1,0:T(8,128)(2,1)} %param.10) | copy-start | bytes 1179652
  9.0 65.9 %copy-start.7 = (f32[192]{0:T(256)S(1)}, f32[192]{0:T(256)}, u32[]{:S(2)}) copy-start(f32[192]{0:T(256)} %param.9) | copy-start | bytes 2308
  9.0 65.9 %all-reduce.3.cloned.1.call-start = ((), (), s32[]{:S(2)}) async-start(), calls=%async_computation.2 | async-start | bytes 393216 | tf_op jit(solution)/shard_map/psum | solution.py:20
  43.3 61.5 %copy-start.5 = (bf16[128,1024]{1,0:T(8,128)(2,1)S(1)}, bf16[128,1024]{1,0:T(8,128)(2,1)}, u32[]{:S(2)}) copy-start(bf16[128,1024]{1,0:T(8,128)(2,1)} %param.6) | copy-start | bytes 786436
  43.3 61.5 %copy-start.6 = (bf16[128,1024]{1,0:T(8,128)(2,1)S(1)}, bf16[128,1024]{1,0:T(8,128)(2,1)}, u32[]{:S(2)}) copy-start(bf16[128,1024]{1,0:T(8,128)(2,1)} %param.7) | copy-start | bytes 786436
  43.3 61.5 %copy-start.8 = (f32[1024]{0:T(1024)S(1)}, f32[1024]{0:T(1024)}, u32[]{:S(2)}) copy-start(f32[1024]{0:T(1024)} %param.11) | copy-start | bytes 12292
  43.3 61.5 %reduce-scatter.2.cloned.1.call-start = ((), (), s32[]{:S(2)}) async-start(), calls=%async_computation.3 | async-start | bytes 1310720 | tf_op jit(solution)/shard_map/reduce_scatter | solution.py:23
  77.5 55.9 %all-gather.5.cloned.1.call-start = ((), (), s32[]{:S(2)}) async-start(), calls=%async_computation.4 | async-start | bytes 1310720 | tf_op jit(solution)/shard_map/all_gather | solution.py:31
  106.6 60.7 %all-reduce.5.cloned.1.call-start = ((), (), s32[]{:S(2)}) async-start(), calls=%async_computation.5 | async-start | bytes 393216 | tf_op jit(solution)/shard_map/psum | solution.py:35
  113.2 54.1 %copy-start.4 = (bf16[512,192]{0,1:T(8,128)(2,1)S(1)}, bf16[512,192]{0,1:T(8,128)(2,1)}, u32[]{:S(2)}) copy-start(bf16[512,192]{0,1:T(8,128)(2,1)} %all-reduce.3.cloned.1.call-done) | copy-start | bytes 589828
  133.4 2.5 %copy-start.1 = (bf16[512,1024]{1,0:T(8,128)(2,1)S(1)}, bf16[512,1024]{1,0:T(8,128)(2,1)}, u32[]{:S(2)}) copy-start(bf16[512,1024]{1,0:T(8,128)(2,1)} %all-gather.5.cloned.1.call-done) | copy-start | bytes 3145732
  135.9 45.2 %copy-start.3 = (bf16[512,1024]{1,0:T(8,128)(2,1)S(1)}, bf16[512,1024]{1,0:T(8,128)(2,1)}, u32[]{:S(2)}) copy-start(bf16[512,1024]{1,0:T(8,128)(2,1)} %all-gather.3.cloned.1.call-done) | copy-start | bytes 3145732
  168.5 14.8 %copy-start.9 = (f32[192]{0:T(256)}, f32[192]{0:T(256)S(1)}, u32[]{:S(2)}) copy-start(f32[192]{0:T(256)S(1)} %get-tuple-element.5) | copy-start | bytes 2308
Sparse Core Ops, SparseCore 0:
  10.2 30.6 all-gather.2
  43.7 31.1 all-reduce.2
  77.6 27.1 reduce-scatter.1
  106.8 26.5 all-gather.4
  136.1 31.1 all-reduce.4
where the time goes:
time: 192 us; the launch traced here: 191 us
  waiting for transfers between devices  142 us (74%)
  blocking collectives  18.1 us (9%)
  between operations  13.8 us (7%)
  matrix products  11.2 us (6%)
  other arithmetic  5.72 us (3%)
    all_gather x1, waiting for transfers between devices, shards(): gathered = lax.all_gather(centered, 'lat', axis=0, tiled=True)  31.8 us
    psum x1, waiting for transfers between devices, shards(): lax.psum(pre_part.astype(jnp.bfloat16), 'width').astype(jnp.float32)  31.6 us
    psum x1, waiting for transfers between devices, shards(): lax.psum(code_part.astype(jnp.bfloat16), 'width').astype(jnp.float32)  31.2 us
    reduce_scatter x1, waiting for transfers between devices, shards(): lax.psum_scatter(jnp.dot(codes, w_dec, preferred_element_type=jnp.float32...  27.2 us
    all_gather x1, waiting for transfers between devices, shards(): whole_grad = lax.all_gather(res_grad, 'lat', axis=0, tiled=True)  20.2 us
    psum x1, blocking collectives, shards(): enc_total = lax.psum(enc_term, 'lat')  11.7 us
    psum x1, blocking collectives, shards(): square_sum = lax.psum(squares, 'width')  6.42 us
  transfers between devices with their start and end apart: 5, of which 5 were waited for; matrix products, arithmetic and copies ran while one was open for 0% of the time, Pallas kernels for 0%

commit v1 on v0

v1 whole, which is shorter than its diff:
```python
import jax
import jax.numpy as jnp
from jax import lax
from jax.sharding import PartitionSpec as P

sparsity_coef = 3.0
f32 = jnp.float32
bf16 = jnp.bfloat16


def swap(value, axis, distance):
    count = lax.axis_size(axis)
    return lax.ppermute(value, axis, [(i, i ^ distance) for i in range(count)])


def after(value, *earlier):
    return lax.optimization_barrier((value, *earlier))[0]


def lat_gather(block):
    count = lax.axis_size("lat")
    if count != 4:
        return [block] + [swap(block, "lat", k) for k in range(1, count)]
    z = lax.axis_index("lat")
    inner = (z == 1) | (z == 2)
    near = swap(block, "lat", 1)
    middle = lax.ppermute(block, "lat", [(1, 2), (2, 1)])
    out = lax.ppermute(middle, "lat", [(1, 0), (2, 3)])
    across = lax.ppermute(near, "lat", [(1, 2), (2, 1)])
    two = jnp.where(inner, across, out)
    ends = lax.ppermute(across, "lat", [(1, 0), (2, 3)])
    three = jnp.where(inner, middle, ends)
    return [block, near, two, three]


def width_sum(part):
    count = lax.axis_size("width")
    own = part.astype(bf16)
    if count == 4:
        others = [swap(own, "width", k) for k in (1, 2, 3)]
        return (own.astype(f32) + others[0].astype(f32)) + (
            others[1].astype(f32) + others[2].astype(f32)
        )
    total = own.astype(f32)
    step = 1
    while step < count:
        sent = total.astype(bf16)
        total = sent.astype(f32) + swap(sent, "width", step).astype(f32)
        step *= 2
    return total


def plain_sum(value, axis):
    step = 1
    while step < lax.axis_size(axis):
        value = value + swap(value, axis, step)
        step *= 2
    return value


def mm(a, b, contract):
    return lax.dot_general(a, b, ((contract[:1], contract[1:]), ((), ())), preferred_element_type=f32)


def shards(activations, rest_recon, w_enc, b_enc, w_dec, b_dec):
    lat_count = lax.axis_size("lat")
    groups = lax.axis_size("groups")
    local_rows = activations.shape[0]
    row_scale = 1.0 / jnp.sqrt(f32(local_rows * lat_count))
    first = lax.axis_index("groups") == 0
    others = range(1, lat_count)

    xs = lat_gather(activations)
    centered = [(x.astype(f32) - b_dec).astype(bf16) for x in xs]
    codes = [
        jnp.maximum(width_sum(mm(c, w_enc, (1, 0))) + b_enc, 0.0).astype(bf16) for c in centered
    ]
    held = [codes[k] if k == 0 else swap(codes[k], "lat", k) for k in range(lat_count)]

    half = w_dec.shape[1] // groups
    mine = lax.dynamic_slice_in_dim(w_dec, lax.axis_index("groups") * half, half, axis=1)
    mine = after(mine, xs[2])
    mine = lat_gather(mine)
    other = [None] + [swap(mine[k], "groups", 1) for k in others]

    recon_mine = sum(mm(held[k], mine[k], (1, 0)) for k in others)
    recon_other = sum(mm(held[k], other[k], (1, 0)) for k in others)
    recon = mm(held[0], w_dec, (1, 0)) + jnp.concatenate(
        [
            jnp.where(first, recon_mine, recon_other),
            jnp.where(first, recon_other, recon_mine),
        ],
        axis=1,
    )
    error_rows = rest_recon.astype(f32) + recon + b_dec - activations.astype(f32)
    res_grad = (2.0 * row_scale * error_rows).astype(bf16)
    res_mine = jnp.where(first, res_grad[:, :half], res_grad[:, half:])
    res_other = jnp.where(first, res_grad[:, half:], res_grad[:, :half])

    parts = [mm(res_grad, w_dec, (1, 1))] + [
        mm(res_mine, mine[k], (1, 1)) + mm(res_other, other[k], (1, 1)) for k in others
    ]
    code_sums = [width_sum(p) for p in parts]
    code_sums = [code_sums[0]] + [
        swap(code_sums[k].astype(bf16), "lat", k).astype(f32) for k in others
    ]
    dec_float = w_dec.astype(f32)
    norms = jnp.sqrt(plain_sum(jnp.sum(dec_float * dec_float, axis=1), "width") + 1e-06)
    pre_grad = [
        jnp.where(c > 0, s + sparsity_coef * row_scale * norms, 0.0).astype(bf16)
        for c, s in zip(codes, code_sums)
    ]
    res = lat_gather(res_grad)

    grad_enc = sum(mm(c, p, (0, 0)) for c, p in zip(centered, pre_grad))
    grad_benc = sum(jnp.sum(p.astype(f32), axis=0) for p in pre_grad)
    code_total = sum(jnp.sum(c.astype(f32), axis=0) for c in codes)
    grad_dec = sum(mm(c, r, (0, 0)) for c, r in zip(codes, res))
    grad_dec = grad_dec + (sparsity_coef * row_scale * code_total / norms)[:, None] * dec_float
    enc_term = jnp.dot(w_enc.astype(f32), grad_benc, precision=lax.Precision.HIGHEST)
    grad_bdec = plain_sum(jnp.sum(res_grad.astype(f32), axis=0) - enc_term, "lat")
    return (grad_enc, grad_benc, grad_dec, grad_bdec)


def solution(mesh):
    placed = (
        P(("groups", "lat"), "width"),
        P(("groups", "lat"), "width"),
        P("width", "lat"),
        P("lat"),
        P("lat", "width"),
        P("width"),
    )
    return jax.shard_map(
        shards,
        mesh=mesh,
        in_specs=placed,
        out_specs=(
            P(("groups", "width"), "lat"),
            P(("groups", "lat")),
            P(("groups", "lat"), "width"),
            P(("groups", "width")),
        ),
        check_vma=False,
    )
```

time: 192 us -> 115 us (0.60)
  waiting for transfers between devices: 142 us -> 46.2 us
  starting transfers between devices: 0.21 us -> 54.6 us
  blocking collectives: 18.1 us -> 0 us
  between operations: 13.8 us -> 1.25 us
  other arithmetic: 5.72 us -> 1.57 us
    psum x2 -> x0, waiting for transfers between devices: 62.8 us -> none  [the longest x1 31.6 us: shards(): lax.psum(pre_part.astype(jnp.bfloat16), 'width').astype(jnp.float32)]
    ppermute x0 -> x52, starting transfers between devices: none -> 54.6 us  [the longest x40 42.8 us: swap(): return lax.ppermute(value, axis, [(i, i ^ distance) for i in range(count)])]
    all_gather x2 -> x0, waiting for transfers between devices: 51.9 us -> none  [the longest x1 31.8 us: shards(): gathered = lax.all_gather(centered, 'lat', axis=0, tiled=True)]
    ppermute x0 -> x52, waiting for transfers between devices: none -> 46.2 us  [the longest x40 19 us: swap(): return lax.ppermute(value, axis, [(i, i ^ distance) for i in range(count)])]
    reduce_scatter x1 -> x0, waiting for transfers between devices: 27.2 us -> none  [shards(): lax.psum_scatter(jnp.dot(codes, w_dec, preferred_element_type=jnp.float32...]
    psum x2 -> x0, blocking collectives: 18.1 us -> none  [the longest x1 11.7 us: shards(): enc_total = lax.psum(enc_term, 'lat')]
    convert_element_type x2 -> x4, other arithmetic: 3.54 us -> 0.31 us  [the longest x1 0.22 us: shards(): jnp.maximum(width_sum(mm(c, w_enc, (1, 0))) + b_enc, 0.0).astype(bf16)]
    dot_general x6 -> x27, matrix products: 11.2 us -> 9.34 us  [the longest x26 9.08 us: mm(): lax.dot_general(a, b, ((contract[:1], contract[1:]), ((), ())), preferred...]
  transfers between devices with their start and end apart: 5 -> 52, of which waited for: 5 -> 16; matrix products, arithmetic and copies ran while one was open for 0% -> 8% of each run, Pallas kernels for 0% -> 0%
where the time goes in v1:
time: 115 us
  starting transfers between devices  54.6 us (47%)
  waiting for transfers between devices  46.2 us (40%)
  matrix products  9.34 us (8%)
  local copies, waits for them, and re-layouts  1.68 us (1%)
  other arithmetic  1.57 us (1%)
  between operations  1.25 us (1%)
    ppermute x40, starting transfers between devices, swap(): return lax.ppermute(value, axis, [(i, i ^ distance) for i in range(count)])  42.8 us
    ppermute x40, waiting for transfers between devices, swap(): return lax.ppermute(value, axis, [(i, i ^ distance) for i in range(count)])  19 us
    ppermute x3, waiting for transfers between devices, lat_gather(): out = lax.ppermute(middle, 'lat', [(1, 0), (2, 3)])  15.9 us
    ppermute x3, waiting for transfers between devices, lat_gather(): ends = lax.ppermute(across, 'lat', [(1, 0), (2, 3)])  11.4 us
    dot_general x26, matrix products, mm(): lax.dot_general(a, b, ((contract[:1], contract[1:]), ((), ())), preferred...  9.08 us
    ppermute x3, starting transfers between devices, lat_gather(): out = lax.ppermute(middle, 'lat', [(1, 0), (2, 3)])  3.87 us
    ppermute x3, starting transfers between devices, lat_gather(): ends = lax.ppermute(across, 'lat', [(1, 0), (2, 3)])  3.85 us
  transfers between devices with their start and end apart: 52, of which 16 were waited for; matrix products, arithmetic and copies ran while one was open for 8% of the time, Pallas kernels for 0%

profile of v1, /device:TPU:0, one launch (start us, length us, event | category | flops | bytes accessed | tf_op | source)
XLA Modules:
  0.0 114.7 jit_solution(8363214903457445032)
XLA Ops:
  0.7 3.1 %collective-permute-start.3 = (bf16[128,1024]{1,0:T(8,128)(2,1)}, bf16[128,1024]{1,0:T(8,128)(2,1)S(1)}, u32[]{:S(2)}, u32[]{:S(2)}) collective-permute-start(bf16[128,1024]{1,0:T(8,128)(2,1)} %param.6), channel_id=1, source_target_pairs={{0,4},{4,0},{8,12},{12,8},{1,5},{5,1},{9,13},{13,9},{2,6},{6,2},{1... | collective-permute-start | bytes 786440 | tf_op jit(solution)/shard_map/ppermute | solution.py:13
  7.8 2.5 %collective-permute-done.3 = bf16[128,1024]{1,0:T(8,128)(2,1)S(1)} collective-permute-done((bf16[128,1024]{1,0:T(8,128)(2,1)}, bf16[128,1024]{1,0:T(8,128)(2,1)S(1)}, u32[]{:S(2)}, u32[]{:S(2)}) %collective-permute-start.3) | collective-permute-done | bytes 262176 | tf_op jit(solution)/shard_map/ppermute | solution.py:13
  10.9 1.3 %collective-permute-start.10 = (bf16[128,1024]{1,0:T(8,128)(2,1)S(1)}, bf16[128,1024]{1,0:T(8,128)(2,1)S(1)}, u32[]{:S(2)}, u32[]{:S(2)}) collective-permute-start(bf16[128,1024]{1,0:T(8,128)(2,1)S(1)} %collective-permute-done.9), channel_id=1, source_target_pairs={{4,0},{8,12},{5,1},{9,13},{6,2},{10,14},{7,3},{11,15},{20,16},{24,... | collective-permute-start | bytes 786440 | tf_op jit(solution)/shard_map/ppermute | solution.py:28
  13.3 1.7 %collective-permute-start.32 = (f32[192]{0:T(256)S(1)}, f32[192]{0:T(256)S(1)}, u32[]{:S(2)}, u32[]{:S(2)}) collective-permute-start(f32[192]{0:T(256)S(1)} %add.245), channel_id=1, source_target_pairs={{0,2},{1,3},{2,0},{3,1},{4,6},{5,7},{6,4},{7,5},{8,10},{9,11},{10,... | collective-permute-start | bytes 2312 | tf_op jit(solution)/shard_map/ppermute | solution.py:13
  15.0 7.1 %collective-permute-done.10 = bf16[128,1024]{1,0:T(8,128)(2,1)S(1)} collective-permute-done((bf16[128,1024]{1,0:T(8,128)(2,1)S(1)}, bf16[128,1024]{1,0:T(8,128)(2,1)S(1)}, u32[]{:S(2)}, u32[]{:S(2)}) %collective-permute-start.10) | collective-permute-done | bytes 262176 | tf_op jit(solution)/shard_map/ppermute | solution.py:28
  23.8 1.4 %collective-permute-start.5 = (bf16[128,192]{0,1:T(8,128)(2,1)S(1)}, bf16[128,192]{0,1:T(8,128)(2,1)S(1)}, u32[]{:S(2)}, u32[]{:S(2)}) collective-permute-start(bf16[128,192]{0,1:T(8,128)(2,1)S(1)} %convolution_convert_fusion.3), channel_id=1, source_target_pairs={{0,2},{1,3},{2,0},{3,1},{4,6},{5,7},{6,4},{7,5},{8,10},{9,11},{10,... | collective-permute-start | bytes 147464 | tf_op jit(solution)/shard_map/ppermute | solution.py:13
  28.4 2.2 %collective-permute-done.19 = bf16[128,1024]{1,0:T(8,128)(2,1)S(1)} collective-permute-done((bf16[128,1024]{1,0:T(8,128)(2,1)S(1)}, bf16[128,1024]{1,0:T(8,128)(2,1)S(1)}, u32[]{:S(2)}, u32[]{:S(2)}) %collective-permute-start.19) | collective-permute-done | bytes 262176 | tf_op jit(solution)/shard_map/ppermute | solution.py:31
  31.5 3.5 %collective-permute-start.11 = (bf16[192,512]{1,0:T(8,128)(2,1)S(1)}, bf16[192,512]{1,0:T(8,128)(2,1)S(1)}, u32[]{:S(2)}, u32[]{:S(2)}) collective-permute-start(bf16[192,512]{1,0:T(8,128)(2,1)S(1)} %constant_dynamic-slice_fusion), channel_id=1, source_target_pairs={{0,4},{4,0},{8,12},{12,8},{1,5},{5,1},{9,13},{13,9},{2,6},{6,2},{1... | collective-permute-start | bytes 589832 | tf_op jit(solution)/shard_map/ppermute | solution.py:13
  36.9 3.4 %collective-permute-done.11 = bf16[192,512]{1,0:T(8,128)(2,1)S(1)} collective-permute-done((bf16[192,512]{1,0:T(8,128)(2,1)S(1)}, bf16[192,512]{1,0:T(8,128)(2,1)S(1)}, u32[]{:S(2)}, u32[]{:S(2)}) %collective-permute-start.11) | collective-permute-done | bytes 196640 | tf_op jit(solution)/shard_map/ppermute | solution.py:13
  41.0 1.6 %collective-permute-start.25 = (bf16[192,512]{1,0:T(8,128)(2,1)S(1)}, bf16[192,512]{1,0:T(8,128)(2,1)S(1)}, u32[]{:S(2)}, u32[]{:S(2)}) collective-permute-start(bf16[192,512]{1,0:T(8,128)(2,1)S(1)} %collective-permute-done.11), channel_id=1, source_target_pairs={{0,16},{16,0},{1,17},{17,1},{2,18},{18,2},{3,19},{19,3},{4,20},{20... | collective-permute-start | bytes 589832 | tf_op jit(solution)/shard_map/ppermute | solution.py:13
  44.2 1.7 %collective-permute-start.23 = (bf16[128,192]{0,1:T(8,128)(2,1)S(1)}, bf16[128,192]{0,1:T(8,128)(2,1)S(1)}, u32[]{:S(2)}, u32[]{:S(2)}) collective-permute-start(bf16[128,192]{0,1:T(8,128)(2,1)S(1)} %get-tuple-element.30), channel_id=1, source_target_pairs={{0,12},{4,8},{8,4},{12,0},{1,13},{5,9},{9,5},{13,1},{2,14},{6,10},... | collective-permute-start | bytes 147464 | tf_op jit(solution)/shard_map/ppermute | solution.py:13
  45.8 3.1 %collective-permute-start.15 = (bf16[128,192]{0,1:T(8,128)(2,1)S(1)}, bf16[128,192]{0,1:T(8,128)(2,1)S(1)}, u32[]{:S(2)}, u32[]{:S(2)}) collective-permute-start(bf16[128,192]{0,1:T(8,128)(2,1)S(1)} %get-tuple-element.29), channel_id=1, source_target_pairs={{0,8},{4,12},{8,0},{12,4},{1,9},{5,13},{9,1},{13,5},{2,10},{6,14},... | collective-permute-start | bytes 147464 | tf_op jit(solution)/shard_map/ppermute | solution.py:13
  49.0 3.9 %collective-permute-start.7 = (bf16[128,192]{0,1:T(8,128)(2,1)S(1)}, bf16[128,192]{0,1:T(8,128)(2,1)S(1)}, u32[]{:S(2)}, u32[]{:S(2)}) collective-permute-start(bf16[128,192]{0,1:T(8,128)(2,1)S(1)} %get-tuple-element.28), channel_id=1, source_target_pairs={{0,4},{4,0},{8,12},{12,8},{1,5},{5,1},{9,13},{13,9},{2,6},{6,2},{1... | collective-permute-start | bytes 147464 | tf_op jit(solution)/shard_map/ppermute | solution.py:13
  53.6 1.3 %collective-permute-start.26 = (bf16[192,512]{1,0:T(8,128)(2,1)S(1)}, bf16[192,512]{1,0:T(8,128)(2,1)S(1)}, u32[]{:S(2)}, u32[]{:S(2)}) collective-permute-start(bf16[192,512]{1,0:T(8,128)(2,1)S(1)} %broadcast_select_fusion.2), channel_id=1, source_target_pairs={{0,16},{16,0},{1,17},{17,1},{2,18},{18,2},{3,19},{19,3},{4,20},{20... | collective-permute-start | bytes 589832 | tf_op jit(solution)/shard_map/ppermute | solution.py:13
  56.5 6.1 %collective-permute-done.24 = bf16[192,512]{1,0:T(8,128)(2,1)S(1)} collective-permute-done((bf16[192,512]{1,0:T(8,128)(2,1)S(1)}, bf16[192,512]{1,0:T(8,128)(2,1)S(1)}, u32[]{:S(2)}, u32[]{:S(2)}) %collective-permute-start.24) | collective-permute-done | bytes 196640 | tf_op jit(solution)/shard_map/ppermute | solution.py:31
  64.1 4.2 %collective-permute-done.27 = bf16[192,512]{1,0:T(8,128)(2,1)S(1)} collective-permute-done((bf16[192,512]{1,0:T(8,128)(2,1)S(1)}, bf16[192,512]{1,0:T(8,128)(2,1)S(1)}, u32[]{:S(2)}, u32[]{:S(2)}) %collective-permute-start.27) | collective-permute-done | bytes 196640 | tf_op jit(solution)/shard_map/ppermute | solution.py:13
  80.5 2.0 %collective-permute-start.44 = (bf16[128,192]{0,1:T(8,128)(2,1)S(1)}, bf16[128,192]{0,1:T(8,128)(2,1)S(1)}, u32[]{:S(2)}, u32[]{:S(2)}) collective-permute-start(bf16[128,192]{0,1:T(8,128)(2,1)S(1)} %add_convert_fusion), channel_id=1, source_target_pairs={{0,12},{4,8},{8,4},{12,0},{1,13},{5,9},{9,5},{13,1},{2,14},{6,10},... | collective-permute-start | bytes 147464 | tf_op jit(solution)/shard_map/ppermute | solution.py:13
  82.5 1.6 %collective-permute-start.40 = (bf16[128,192]{0,1:T(8,128)(2,1)S(1)}, bf16[128,192]{0,1:T(8,128)(2,1)S(1)}, u32[]{:S(2)}, u32[]{:S(2)}) collective-permute-start(bf16[128,192]{0,1:T(8,128)(2,1)S(1)} %add_convert_fusion.1), channel_id=1, source_target_pairs={{0,8},{4,12},{8,0},{12,4},{1,9},{5,13},{9,1},{13,5},{2,10},{6,14},... | collective-permute-start | bytes 147464 | tf_op jit(solution)/shard_map/ppermute | solution.py:13
  87.0 1.7 %collective-permute-done.40 = bf16[128,192]{0,1:T(8,128)(2,1)S(1)} collective-permute-done((bf16[128,192]{0,1:T(8,128)(2,1)S(1)}, bf16[128,192]{0,1:T(8,128)(2,1)S(1)}, u32[]{:S(2)}, u32[]{:S(2)}) %collective-permute-start.40) | collective-permute-done | bytes 49184 | tf_op jit(solution)/shard_map/ppermute | solution.py:13
  94.7 3.3 %collective-permute-done.51 = f32[1024]{0:T(1024)S(1)} collective-permute-done((f32[1024]{0:T(1024)S(1)}, f32[1024]{0:T(1024)S(1)}, u32[]{:S(2)}, u32[]{:S(2)}) %collective-permute-start.51) | collective-permute-done | bytes 4128 | tf_op jit(solution)/shard_map/ppermute | solution.py:13
  99.3 1.3 %collective-permute-start.48 = (bf16[128,1024]{1,0:T(8,128)(2,1)S(1)}, bf16[128,1024]{1,0:T(8,128)(2,1)S(1)}, u32[]{:S(2)}, u32[]{:S(2)}) collective-permute-start(bf16[128,1024]{1,0:T(8,128)(2,1)S(1)} %collective-permute-done.47), channel_id=1, source_target_pairs={{4,0},{8,12},{5,1},{9,13},{6,2},{10,14},{7,3},{11,15},{20,16},{24,... | collective-permute-start | bytes 786440 | tf_op jit(solution)/shard_map/ppermute | solution.py:28
  100.9 1.3 %collective-permute-start.49 = (bf16[128,1024]{1,0:T(8,128)(2,1)S(1)}, bf16[128,1024]{1,0:T(8,128)(2,1)S(1)}, u32[]{:S(2)}, u32[]{:S(2)}) collective-permute-start(bf16[128,1024]{1,0:T(8,128)(2,1)S(1)} %collective-permute-done.46), channel_id=1, source_target_pairs={{4,0},{8,12},{5,1},{9,13},{6,2},{10,14},{7,3},{11,15},{20,16},{24,... | collective-permute-start | bytes 786440 | tf_op jit(solution)/shard_map/ppermute | solution.py:31
  102.2 7.9 %collective-permute-done.48 = bf16[128,1024]{1,0:T(8,128)(2,1)S(1)} collective-permute-done((bf16[128,1024]{1,0:T(8,128)(2,1)S(1)}, bf16[128,1024]{1,0:T(8,128)(2,1)S(1)}, u32[]{:S(2)}, u32[]{:S(2)}) %collective-permute-start.48) | collective-permute-done | bytes 262176 | tf_op jit(solution)/shard_map/ppermute | solution.py:28
  110.4 3.2 %collective-permute-done.49 = bf16[128,1024]{1,0:T(8,128)(2,1)S(1)} collective-permute-done((bf16[128,1024]{1,0:T(8,128)(2,1)S(1)}, bf16[128,1024]{1,0:T(8,128)(2,1)S(1)}, u32[]{:S(2)}, u32[]{:S(2)}) %collective-permute-start.49) | collective-permute-done | bytes 262176 | tf_op jit(solution)/shard_map/ppermute | solution.py:31
  (139 shorter events, 43.2 us)
Async XLA Ops:
  0.7 9.6 %collective-permute-start.3 = (bf16[128,1024]{1,0:T(8,128)(2,1)}, bf16[128,1024]{1,0:T(8,128)(2,1)S(1)}, u32[]{:S(2)}, u32[]{:S(2)}) collective-permute-start(bf16[128,1024]{1,0:T(8,128)(2,1)} %param.6), channel_id=1, source_target_pairs={{0,4},{4,0},{8,12},{12,8},{1,5},{5,1},{9,13},{13,9},{2,6},{6,2},{1... | collective-permute-start | bytes 786440 | tf_op jit(solution)/shard_map/ppermute | solution.py:13
  5.7 18.2 %collective-permute-start.2 = (bf16[128,192]{0,1:T(8,128)(2,1)S(1)}, bf16[128,192]{0,1:T(8,128)(2,1)S(1)}, u32[]{:S(2)}, u32[]{:S(2)}) collective-permute-start(bf16[128,192]{0,1:T(8,128)(2,1)S(1)} %convolution_convert_fusion.4), channel_id=1, source_target_pairs={{0,3},{1,2},{2,1},{3,0},{4,7},{5,6},{6,5},{7,4},{8,11},{9,10},{10,... | collective-permute-start | bytes 147464 | tf_op jit(solution)/shard_map/ppermute | solution.py:13
  6.4 18.8 %collective-permute-start.1 = (bf16[128,192]{0,1:T(8,128)(2,1)S(1)}, bf16[128,192]{0,1:T(8,128)(2,1)S(1)}, u32[]{:S(2)}, u32[]{:S(2)}) collective-permute-start(bf16[128,192]{0,1:T(8,128)(2,1)S(1)} %convolution_convert_fusion.4), channel_id=1, source_target_pairs={{0,2},{1,3},{2,0},{3,1},{4,6},{5,7},{6,4},{7,5},{8,10},{9,11},{10,... | collective-permute-start | bytes 147464 | tf_op jit(solution)/shard_map/ppermute | solution.py:13
  10.9 11.2 %collective-permute-start.10 = (bf16[128,1024]{1,0:T(8,128)(2,1)S(1)}, bf16[128,1024]{1,0:T(8,128)(2,1)S(1)}, u32[]{:S(2)}, u32[]{:S(2)}) collective-permute-start(bf16[128,1024]{1,0:T(8,128)(2,1)S(1)} %collective-permute-done.9), channel_id=1, source_target_pairs={{4,0},{8,12},{5,1},{9,13},{6,2},{10,14},{7,3},{11,15},{20,16},{24,... | collective-permute-start | bytes 786440 | tf_op jit(solution)/shard_map/ppermute | solution.py:28
  12.3 13.4 %collective-permute-start = (bf16[128,192]{0,1:T(8,128)(2,1)S(1)}, bf16[128,192]{0,1:T(8,128)(2,1)S(1)}, u32[]{:S(2)}, u32[]{:S(2)}) collective-permute-start(bf16[128,192]{0,1:T(8,128)(2,1)S(1)} %convolution_convert_fusion.4), channel_id=1, source_target_pairs={{0,1},{1,0},{2,3},{3,2},{4,5},{5,4},{6,7},{7,6},{8,9},{9,8},{10,11... | collective-permute-start | bytes 147464 | tf_op jit(solution)/shard_map/ppermute | solution.py:13
  13.3 10.2 %collective-permute-start.32 = (f32[192]{0:T(256)S(1)}, f32[192]{0:T(256)S(1)}, u32[]{:S(2)}, u32[]{:S(2)}) collective-permute-start(f32[192]{0:T(256)S(1)} %add.245), channel_id=1, source_target_pairs={{0,2},{1,3},{2,0},{3,1},{4,6},{5,7},{6,4},{7,5},{8,10},{9,11},{10,... | collective-permute-start | bytes 2312 | tf_op jit(solution)/shard_map/ppermute | solution.py:13
  22.1 8.4 %collective-permute-start.19 = (bf16[128,1024]{1,0:T(8,128)(2,1)S(1)}, bf16[128,1024]{1,0:T(8,128)(2,1)S(1)}, u32[]{:S(2)}, u32[]{:S(2)}) collective-permute-start(bf16[128,1024]{1,0:T(8,128)(2,1)S(1)} %collective-permute-done.8), channel_id=1, source_target_pairs={{4,0},{8,12},{5,1},{9,13},{6,2},{10,14},{7,3},{11,15},{20,16},{24,... | collective-permute-start | bytes 786440 | tf_op jit(solution)/shard_map/ppermute | solution.py:31
  25.7 9.3 %collective-permute-start.14 = (bf16[128,192]{0,1:T(8,128)(2,1)S(1)}, bf16[128,192]{0,1:T(8,128)(2,1)S(1)}, u32[]{:S(2)}, u32[]{:S(2)}) collective-permute-start(bf16[128,192]{0,1:T(8,128)(2,1)S(1)} %convolution_convert_fusion.2), channel_id=1, source_target_pairs={{0,3},{1,2},{2,1},{3,0},{4,7},{5,6},{6,5},{7,4},{8,11},{9,10},{10,... | collective-permute-start | bytes 147464 | tf_op jit(solution)/shard_map/ppermute | solution.py:13
  27.4 8.3 %collective-permute-start.13 = (bf16[128,192]{0,1:T(8,128)(2,1)S(1)}, bf16[128,192]{0,1:T(8,128)(2,1)S(1)}, u32[]{:S(2)}, u32[]{:S(2)}) collective-permute-start(bf16[128,192]{0,1:T(8,128)(2,1)S(1)} %convolution_convert_fusion.2), channel_id=1, source_target_pairs={{0,2},{1,3},{2,0},{3,1},{4,6},{5,7},{6,4},{7,5},{8,10},{9,11},{10,... | collective-permute-start | bytes 147464 | tf_op jit(solution)/shard_map/ppermute | solution.py:13
  30.8 10.2 %collective-permute-start.17 = (bf16[192,512]{1,0:T(8,128)(2,1)S(1)}, bf16[192,512]{1,0:T(8,128)(2,1)S(1)}, u32[]{:S(2)}, u32[]{:S(2)}) collective-permute-start(bf16[192,512]{1,0:T(8,128)(2,1)S(1)} %constant_dynamic-slice_fusion), channel_id=1, source_target_pairs={{4,8},{8,4},{5,9},{9,5},{6,10},{10,6},{7,11},{11,7},{20,24},{24,20... | collective-permute-start | bytes 589832 | tf_op jit(solution)/shard_map/ppermute | solution.py:27
  31.5 8.8 %collective-permute-start.11 = (bf16[192,512]{1,0:T(8,128)(2,1)S(1)}, bf16[192,512]{1,0:T(8,128)(2,1)S(1)}, u32[]{:S(2)}, u32[]{:S(2)}) collective-permute-start(bf16[192,512]{1,0:T(8,128)(2,1)S(1)} %constant_dynamic-slice_fusion), channel_id=1, source_target_pairs={{0,4},{4,0},{8,12},{12,8},{1,5},{5,1},{9,13},{13,9},{2,6},{6,2},{1... | collective-permute-start | bytes 589832 | tf_op jit(solution)/shard_map/ppermute | solution.py:13
  35.1 7.6 %collective-permute-start.22 = (bf16[128,192]{0,1:T(8,128)(2,1)S(1)}, bf16[128,192]{0,1:T(8,128)(2,1)S(1)}, u32[]{:S(2)}, u32[]{:S(2)}) collective-permute-start(bf16[128,192]{0,1:T(8,128)(2,1)S(1)} %convolution_convert_fusion.1), channel_id=1, source_target_pairs={{0,3},{1,2},{2,1},{3,0},{4,7},{5,6},{6,5},{7,4},{8,11},{9,10},{10,... | collective-permute-start | bytes 147464 | tf_op jit(solution)/shard_map/ppermute | solution.py:13
  35.7 8.2 %collective-permute-start.21 = (bf16[128,192]{0,1:T(8,128)(2,1)S(1)}, bf16[128,192]{0,1:T(8,128)(2,1)S(1)}, u32[]{:S(2)}, u32[]{:S(2)}) collective-permute-start(bf16[128,192]{0,1:T(8,128)(2,1)S(1)} %convolution_convert_fusion.1), channel_id=1, source_target_pairs={{0,2},{1,3},{2,0},{3,1},{4,6},{5,7},{6,4},{7,5},{8,10},{9,11},{10,... | collective-permute-start | bytes 147464 | tf_op jit(solution)/shard_map/ppermute | solution.py:13
  40.3 8.6 %collective-permute-start.16 = (bf16[192,512]{1,0:T(8,128)(2,1)S(1)}, bf16[192,512]{1,0:T(8,128)(2,1)S(1)}, u32[]{:S(2)}, u32[]{:S(2)}) collective-permute-start(bf16[192,512]{1,0:T(8,128)(2,1)S(1)} %collective-permute-done.11), channel_id=1, source_target_pairs={{4,8},{8,4},{5,9},{9,5},{6,10},{10,6},{7,11},{11,7},{20,24},{24,20... | collective-permute-start | bytes 589832 | tf_op jit(solution)/shard_map/ppermute | solution.py:29
  41.0 27.5 %collective-permute-start.25 = (bf16[192,512]{1,0:T(8,128)(2,1)S(1)}, bf16[192,512]{1,0:T(8,128)(2,1)S(1)}, u32[]{:S(2)}, u32[]{:S(2)}) collective-permute-start(bf16[192,512]{1,0:T(8,128)(2,1)S(1)} %collective-permute-done.11), channel_id=1, source_target_pairs={{0,16},{16,0},{1,17},{17,1},{2,18},{18,2},{3,19},{19,3},{4,20},{20... | collective-permute-start | bytes 589832 | tf_op jit(solution)/shard_map/ppermute | solution.py:13
  42.6 11.0 %collective-permute-start.18 = (bf16[192,512]{1,0:T(8,128)(2,1)S(1)}, bf16[192,512]{1,0:T(8,128)(2,1)S(1)}, u32[]{:S(2)}, u32[]{:S(2)}) collective-permute-start(bf16[192,512]{1,0:T(8,128)(2,1)S(1)} %collective-permute-done.17), channel_id=1, source_target_pairs={{4,0},{8,12},{5,1},{9,13},{6,2},{10,14},{7,3},{11,15},{20,16},{24,... | collective-permute-start | bytes 589832 | tf_op jit(solution)/shard_map/ppermute | solution.py:28
  44.2 19.2 %collective-permute-start.23 = (bf16[128,192]{0,1:T(8,128)(2,1)S(1)}, bf16[128,192]{0,1:T(8,128)(2,1)S(1)}, u32[]{:S(2)}, u32[]{:S(2)}) collective-permute-start(bf16[128,192]{0,1:T(8,128)(2,1)S(1)} %get-tuple-element.30), channel_id=1, source_target_pairs={{0,12},{4,8},{8,4},{12,0},{1,13},{5,9},{9,5},{13,1},{2,14},{6,10},... | collective-permute-start | bytes 147464 | tf_op jit(solution)/shard_map/ppermute | solution.py:13
  45.8 9.1 %collective-permute-start.15 = (bf16[128,192]{0,1:T(8,128)(2,1)S(1)}, bf16[128,192]{0,1:T(8,128)(2,1)S(1)}, u32[]{:S(2)}, u32[]{:S(2)}) collective-permute-start(bf16[128,192]{0,1:T(8,128)(2,1)S(1)} %get-tuple-element.29), channel_id=1, source_target_pairs={{0,8},{4,12},{8,0},{12,4},{1,9},{5,13},{9,1},{13,5},{2,10},{6,14},... | collective-permute-start | bytes 147464 | tf_op jit(solution)/shard_map/ppermute | solution.py:13
  49.0 14.6 %collective-permute-start.7 = (bf16[128,192]{0,1:T(8,128)(2,1)S(1)}, bf16[128,192]{0,1:T(8,128)(2,1)S(1)}, u32[]{:S(2)}, u32[]{:S(2)}) collective-permute-start(bf16[128,192]{0,1:T(8,128)(2,1)S(1)} %get-tuple-element.28), channel_id=1, source_target_pairs={{0,4},{4,0},{8,12},{12,8},{1,5},{5,1},{9,13},{13,9},{2,6},{6,2},{1... | collective-permute-start | bytes 147464 | tf_op jit(solution)/shard_map/ppermute | solution.py:13
  53.6 10.2 %collective-permute-start.26 = (bf16[192,512]{1,0:T(8,128)(2,1)S(1)}, bf16[192,512]{1,0:T(8,128)(2,1)S(1)}, u32[]{:S(2)}, u32[]{:S(2)}) collective-permute-start(bf16[192,512]{1,0:T(8,128)(2,1)S(1)} %broadcast_select_fusion.2), channel_id=1, source_target_pairs={{0,16},{16,0},{1,17},{17,1},{2,18},{18,2},{3,19},{19,3},{4,20},{20... | collective-permute-start | bytes 589832 | tf_op jit(solution)/shard_map/ppermute | solution.py:13
  84.4 14.3 %collective-permute-start.45 = (bf16[128,1024]{1,0:T(8,128)(2,1)S(1)}, bf16[128,1024]{1,0:T(8,128)(2,1)S(1)}, u32[]{:S(2)}, u32[]{:S(2)}) collective-permute-start(bf16[128,1024]{1,0:T(8,128)(2,1)S(1)} %get-tuple-element.13), channel_id=1, source_target_pairs={{0,4},{4,0},{8,12},{12,8},{1,5},{5,1},{9,13},{13,9},{2,6},{6,2},{1... | collective-permute-start | bytes 786440 | tf_op jit(solution)/shard_map/ppermute | solution.py:13
  85.3 14.0 %collective-permute-start.47 = (bf16[128,1024]{1,0:T(8,128)(2,1)S(1)}, bf16[128,1024]{1,0:T(8,128)(2,1)S(1)}, u32[]{:S(2)}, u32[]{:S(2)}) collective-permute-start(bf16[128,1024]{1,0:T(8,128)(2,1)S(1)} %get-tuple-element.13), channel_id=1, source_target_pairs={{4,8},{8,4},{5,9},{9,5},{6,10},{10,6},{7,11},{11,7},{20,24},{24,20... | collective-permute-start | bytes 786440 | tf_op jit(solution)/shard_map/ppermute | solution.py:27
  99.3 10.8 %collective-permute-start.48 = (bf16[128,1024]{1,0:T(8,128)(2,1)S(1)}, bf16[128,1024]{1,0:T(8,128)(2,1)S(1)}, u32[]{:S(2)}, u32[]{:S(2)}) collective-permute-start(bf16[128,1024]{1,0:T(8,128)(2,1)S(1)} %collective-permute-done.47), channel_id=1, source_target_pairs={{4,0},{8,12},{5,1},{9,13},{6,2},{10,14},{7,3},{11,15},{20,16},{24,... | collective-permute-start | bytes 786440 | tf_op jit(solution)/shard_map/ppermute | solution.py:28
  100.9 12.6 %collective-permute-start.49 = (bf16[128,1024]{1,0:T(8,128)(2,1)S(1)}, bf16[128,1024]{1,0:T(8,128)(2,1)S(1)}, u32[]{:S(2)}, u32[]{:S(2)}) collective-permute-start(bf16[128,1024]{1,0:T(8,128)(2,1)S(1)} %collective-permute-done.46), channel_id=1, source_target_pairs={{4,0},{8,12},{5,1},{9,13},{6,2},{10,14},{7,3},{11,15},{20,16},{24,... | collective-permute-start | bytes 786440 | tf_op jit(solution)/shard_map/ppermute | solution.py:31
  (35 other events, 169.1 us)

commit v2 on v0

v2 whole, which is shorter than its diff:
```python
import jax
import jax.numpy as jnp
from jax import lax
from jax.experimental import pallas as pl
from jax.experimental.pallas import tpu as pltpu
from jax.sharding import PartitionSpec as P

sparsity_coef = 3.0
f32 = jnp.float32
bf16 = jnp.bfloat16


def swap(value, axis, distance):
    count = lax.axis_size(axis)
    return lax.ppermute(value, axis, [(i, i ^ distance) for i in range(count)])


def ring_pairs(steps):
    count = lax.axis_size("lat")
    order = [0] + list(range(1, count, 2)) + list(range(count - 2 + count % 2, 0, -2))
    return [(order[i], order[(i + steps) % count]) for i in range(count)]


def shift(value, steps):
    return lax.ppermute(value, "lat", ring_pairs(steps))


def shift_crossed(value, steps):
    width = lax.axis_size("width")
    pairs = [
        (a * width + w, b * width + (w ^ 1)) for a, b in ring_pairs(steps) for w in range(width)
    ]
    return lax.ppermute(value, ("lat", "width"), pairs)


def after(value, *earlier):
    return lax.optimization_barrier((value, *earlier))[0]


def stage(*values):
    return lax.optimization_barrier(values)


def width_sum(part):
    total = part.astype(f32)
    step = 1
    while step < lax.axis_size("width"):
        sent = lax.reduce_precision(total, 8, 7)
        total = sent + swap(sent.astype(bf16), "width", 2 * step - 1).astype(f32)
        step *= 2
    return total


def plain_sum(value, axis):
    step = 1
    while step < lax.axis_size(axis):
        value = value + swap(value, axis, step)
        step *= 2
    return value


def mm(a, b, contract):
    return lax.dot_general(a, b, ((contract[:1], contract[1:]), ((), ())), preferred_element_type=f32)


VMEM = pl.BlockSpec(memory_space=pltpu.VMEM)


def call(kernel, name, outs, *operands):
    return pl.pallas_call(
        kernel,
        out_shape=[jax.ShapeDtypeStruct(shape, kind) for shape, kind in outs],
        in_specs=[VMEM] * len(operands),
        out_specs=[VMEM] * len(outs),
        cost_estimate=pl.CostEstimate(flops=2 * 10**10, bytes_accessed=10**6, transcendentals=0),
        compiler_params=pltpu.CompilerParams(vmem_limit_bytes=40 * 2**20),
        name=name,
    )(*operands)


def part_of(x, b_dec, w_enc_t):
    def kernel(x_ref, b_ref, w_ref, centered_ref, part_ref):
        centered_ref[...] = (x_ref[...].astype(f32) - b_ref[...]).astype(bf16)
        part_ref[...] = mm(centered_ref[...], w_ref[...], (1, 1)).astype(bf16)

    rows, lat = x.shape[0], w_enc_t.shape[0]
    return call(kernel, "part_of", [(x.shape, bf16), ((rows, lat), bf16)], x, b_dec[None], w_enc_t)


def recon_start(x, rest, b_dec, held, w_dec):
    def kernel(x_ref, r_ref, b_ref, h_ref, w_ref, base):
        base[...] = (
            mm(h_ref[...], w_ref[...], (1, 0))
            + r_ref[...].astype(f32)
            + b_ref[...]
            - x_ref[...].astype(f32)
        )

    return call(kernel, "recon_start", [(x.shape, f32)], x, rest, b_dec[None], held, w_dec)[0]


def res_and_parts(scale, base, w_dec, held, mine, other):
    rows, cols = base.shape
    half, lat, count = cols // 2, w_dec.shape[0], len(held)

    def kernel(base_ref, w_ref, *refs):
        h, m, o = (refs[i * count : (i + 1) * count] for i in range(3))
        res_ref, part_ref = refs[3 * count :]
        first = lax.axis_index("groups") == 0
        r_mine = sum(mm(h[k][...], m[k][...], (1, 0)) for k in range(count))
        r_other = sum(mm(h[k][...], o[k][...], (1, 0)) for k in range(count))
        low = scale * (base_ref[:, :half] + jnp.where(first, r_mine, r_other))
        high = scale * (base_ref[:, half:] + jnp.where(first, r_other, r_mine))
        res_ref[:, :half] = low.astype(bf16)
        res_ref[:, half:] = high.astype(bf16)
        g_mine = jnp.where(first, low, high).astype(bf16)
        g_other = jnp.where(first, high, low).astype(bf16)
        part_ref[0] = mm(res_ref[...], w_ref[...], (1, 1)).astype(bf16)
        for k in range(count):
            part_ref[k + 1] = (
                mm(g_mine, m[k][...], (1, 1)) + mm(g_other, o[k][...], (1, 1))
            ).astype(bf16)

    outs = [((rows, cols), bf16), ((count + 1, rows, lat), bf16)]
    return call(kernel, "res_and_parts", outs, base, w_dec, *held, *mine, *other)


def dec_add(total, codes, res):
    count = len(codes)

    def kernel(*refs):
        c, r = refs[:count], refs[count : 2 * count]
        value = sum(mm(c[k][...], r[k][...], (0, 0)) for k in range(count))
        if total is not None:
            value = refs[2 * count][...] + value
        refs[-1][...] = value

    outs = [((codes[0].shape[1], res[0].shape[1]), f32)]
    start = [] if total is None else [total]
    return call(kernel, "dec_add", outs, *codes, *res, *start)[0]


def pre_grads(codes, back, threshold, w_enc_t, res):
    count = len(codes)

    def kernel(n_ref, w_ref, res_ref, *refs):
        masks, sums, grads = (refs[i * count : (i + 1) * count] for i in range(3))
        bias, share = refs[3 * count :]
        total = 0.0
        for m, s, out in zip(masks, sums, grads):
            g = jnp.where(m[...].astype(f32) > 0, s[...].astype(f32) + n_ref[...], 0.0)
            out[...] = g.astype(bf16)
            total = total + jnp.sum(out[...].astype(f32), axis=0, keepdims=True)
        bias[...] = total
        share[...] = jnp.sum(res_ref[...].astype(f32), axis=0, keepdims=True) - lax.dot_general(
            total,
            w_ref[...].astype(f32),
            (((1,), (0,)), ((), ())),
            precision=lax.Precision.HIGHEST,
            preferred_element_type=f32,
        )

    lat, cols = w_enc_t.shape
    outs = [(codes[0].shape, bf16)] * count + [((1, lat), f32), ((1, cols), f32)]
    *grads, bias, share = call(
        kernel, "pre_grads", outs, threshold[None], w_enc_t, res, *codes, *back
    )
    return grads, bias[0], share[0]


def enc_end(centered, grads):
    count = len(grads)

    def kernel(*refs):
        g, c = refs[:count], refs[count : 2 * count]
        refs[-1][...] = sum(mm(g[k][...], c[k][...], (0, 0)) for k in range(count))

    outs = [((grads[0].shape[1], centered[0].shape[1]), f32)]
    return call(kernel, "enc_end", outs, *grads, *centered)[0]


def square_sums(w_dec):
    dec_float = w_dec.astype(f32)
    return plain_sum(jnp.sum(dec_float * dec_float, axis=1), "width")


def shards(activations, rest_recon, w_enc, b_enc, w_dec, b_dec):
    count = lax.axis_size("lat")
    row_scale = float((activations.shape[0] * count) ** -0.5)
    w_enc_t = w_enc.T
    half = w_dec.shape[1] // 2
    mine_own = lax.dynamic_slice_in_dim(w_dec, lax.axis_index("groups") * half, half, axis=1)

    def to_codes(total):
        return jnp.maximum(total + b_enc, 0.0).astype(bf16)

    xs, mine = [activations], [mine_own]
    for j in range(1, count):
        xs.append(shift(xs[-1], 1))
    squares = square_sums(after(w_dec, xs[1]))
    mine.append(shift(after(mine_own, xs[1]), -1))
    xs[-1], mine[1], squares = stage(xs[-1], mine[1], squares)
    for j in range(2, count):
        mine.append(shift(mine[-1], -1))
    other = [swap(m, "groups", 1) for m in mine[1:]]

    centered, codes = [], []
    for x in xs:
        c, part = part_of(x, b_dec, w_enc_t)
        centered.append(c)
        codes.append(to_codes(width_sum(part)))
    held = codes[:1] + [shift_crossed(codes[j], -j) for j in range(1, count)]

    base = recon_start(activations, rest_recon, b_dec, held[0], w_dec)
    res_grad, sums = res_and_parts(2.0 * row_scale, base, w_dec, held[1:], mine[1:], other)

    res = [res_grad]
    for j in range(1, count):
        res.append(shift(res[-1], 1))
    sums = width_sum(sums).astype(bf16)
    back = [sums[0]] + [shift_crossed(sums[j], j) for j in range(1, count)]
    norms = jnp.sqrt(squares + 1e-06)
    grads, grad_benc, share = pre_grads(
        codes, back, sparsity_coef * row_scale * norms, w_enc_t, res_grad
    )
    grad_bdec = plain_sum(share, "lat")
    grad_enc = enc_end(centered, grads).T
    code_total = sum(jnp.sum(c.astype(f32), axis=0) for c in codes)
    sparsity = (sparsity_coef * row_scale * code_total / norms)[:, None] * w_dec.astype(f32)
    grad_dec = dec_add(sparsity, codes[:2], res[:2])
    for j in range(2, count):
        grad_dec = dec_add(grad_dec, codes[j : j + 1], res[j : j + 1])
    return (grad_enc, grad_benc, grad_dec, grad_bdec)


def solution(mesh):
    placed = (
        P(("groups", "lat"), "width"),
        P(("groups", "lat"), "width"),
        P("width", "lat"),
        P("lat"),
        P("lat", "width"),
        P("width"),
    )
    return jax.shard_map(
        shards,
        mesh=mesh,
        in_specs=placed,
        out_specs=(
            P(("groups", "width"), "lat"),
            P(("groups", "lat")),
            P(("groups", "lat"), "width"),
            P(("groups", "width")),
        ),
        check_vma=False,
    )
```

time: 192 us -> 104 us (0.54)
  waiting for transfers between devices: 142 us -> 55.9 us
  starting transfers between devices: 0.21 us -> 35.9 us
  blocking collectives: 18.1 us -> 0 us
  between operations: 13.8 us -> 1 us
  matrix products: 11.2 us -> 0 us
  Pallas kernels: 0 us -> 6.71 us
  other arithmetic: 5.72 us -> 1.4 us
  local copies, waits for them, and re-layouts: 0.05 us -> 3.3 us
    psum x2 -> x0, waiting for transfers between devices: 62.8 us -> none  [the longest x1 31.6 us: shards(): lax.psum(pre_part.astype(jnp.bfloat16), 'width').astype(jnp.float32)]
    ppermute x0 -> x32, waiting for transfers between devices: none -> 55.9 us  [the longest x9 23.8 us: shift(): return lax.ppermute(value, 'lat', ring_pairs(steps))]
    all_gather x2 -> x0, waiting for transfers between devices: 51.9 us -> none  [the longest x1 31.8 us: shards(): gathered = lax.all_gather(centered, 'lat', axis=0, tiled=True)]
    ppermute x0 -> x32, starting transfers between devices: none -> 35.9 us  [the longest x9 20.3 us: shift(): return lax.ppermute(value, 'lat', ring_pairs(steps))]
    reduce_scatter x1 -> x0, waiting for transfers between devices: 27.2 us -> none  [shards(): lax.psum_scatter(jnp.dot(codes, w_dec, preferred_element_type=jnp.float32...]
    psum x2 -> x0, blocking collectives: 18.1 us -> none  [the longest x1 11.7 us: shards(): enc_total = lax.psum(enc_term, 'lat')]
    dot_general x6 -> x0, matrix products: 11.2 us -> none  [the longest x1 2.51 us: shards(): jnp.dot(codes, w_dec, preferred_element_type=jnp.float32)]
    pallas_call x0 -> x11, Pallas kernels: none -> 6.71 us  [call(): pl.pallas_call(kernel, out_shape=[jax.ShapeDtypeStruct(shape, kind) for s...]
  transfers between devices with their start and end apart: 5 -> 32, of which waited for: 5 -> 14; matrix products, arithmetic and copies ran while one was open for 0% -> 1% of each run, Pallas kernels for 0% -> 4%
where the time goes in v2:
time: 104 us
  waiting for transfers between devices  55.9 us (54%)
  starting transfers between devices  35.9 us (35%)
  Pallas kernels  6.71 us (6%)
  local copies, waits for them, and re-layouts  3.3 us (3%)
  other arithmetic  1.4 us (1%)
    ppermute x9, waiting for transfers between devices, shift(): return lax.ppermute(value, 'lat', ring_pairs(steps))  23.8 us
    ppermute x17, waiting for transfers between devices, swap(): return lax.ppermute(value, axis, [(i, i ^ distance) for i in range(count)])  22.7 us
    ppermute x9, starting transfers between devices, shift(): return lax.ppermute(value, 'lat', ring_pairs(steps))  20.3 us
    ppermute x17, starting transfers between devices, swap(): return lax.ppermute(value, axis, [(i, i ^ distance) for i in range(count)])  10 us
    ppermute x6, waiting for transfers between devices, shift_crossed(): return lax.ppermute(value, ('lat', 'width'), pairs)  9.36 us
    pallas_call x11, Pallas kernels, call(): pl.pallas_call(kernel, out_shape=[jax.ShapeDtypeStruct(shape, kind) for s...  6.71 us
    ppermute x6, starting transfers between devices, shift_crossed(): return lax.ppermute(value, ('lat', 'width'), pairs)  5.6 us
    unnamed x18, local copies, waits for them, and re-layouts  3.27 us
  transfers between devices with their start and end apart: 32, of which 14 were waited for; matrix products, arithmetic and copies ran while one was open for 1% of the time, Pallas kernels for 4%

profile of v2, /device:TPU:0, one launch (start us, length us, event | category | flops | bytes accessed | tf_op | source)
XLA Modules:
  0.0 104.2 jit_solution(12564364017268505204)
XLA Ops:
  0.6 3.1 %collective-permute-start = (bf16[128,1024]{1,0:T(8,128)(2,1)}, bf16[128,1024]{1,0:T(8,128)(2,1)S(1)}, u32[]{:S(2)}, u32[]{:S(2)}) collective-permute-start(bf16[128,1024]{1,0:T(8,128)(2,1)} %x_ref.3), channel_id=1, source_target_pairs={{0,4},{4,12},{12,8},{8,0},{1,5},{5,13},{13,9},{9,1},{2,6},{6,14},{... | collective-permute-start | bytes 786440 | tf_op jit(solution)/shard_map/ppermute | solution.py:25
  7.4 3.9 %collective-permute-done.x_ref = bf16[128,1024]{1,0:T(8,128)(2,1)S(1)} collective-permute-done((bf16[128,1024]{1,0:T(8,128)(2,1)}, bf16[128,1024]{1,0:T(8,128)(2,1)S(1)}, u32[]{:S(2)}, u32[]{:S(2)}) %collective-permute-start) | collective-permute-done | bytes 262176 | tf_op jit(solution)/shard_map/ppermute | solution.py:25
  13.3 1.5 %collective-permute-start.5 = (f32[192]{0:T(256)S(1)}, f32[192]{0:T(256)S(1)}, u32[]{:S(2)}, u32[]{:S(2)}) collective-permute-start(f32[192]{0:T(256)S(1)} %add.87), channel_id=1, source_target_pairs={{0,2},{1,3},{2,0},{3,1},{4,6},{5,7},{6,4},{7,5},{8,10},{9,11},{10,... | collective-permute-start | bytes 2312 | tf_op jit(solution)/shard_map/ppermute | solution.py:15
  14.9 2.1 %collective-permute-start.3 = (bf16[192,512]{1,0:T(8,128)(2,1)S(1)}, bf16[192,512]{1,0:T(8,128)(2,1)S(1)}, u32[]{:S(2)}, u32[]{:S(2)}) collective-permute-start(bf16[192,512]{1,0:T(8,128)(2,1)S(1)} %constant_dynamic-slice_fusion), channel_id=1, source_target_pairs={{0,8},{4,0},{12,4},{8,12},{1,9},{5,1},{13,5},{9,13},{2,10},{6,2},{... | collective-permute-start | bytes 589832 | tf_op jit(solution)/shard_map/ppermute | solution.py:25
  18.5 3.1 %collective-permute-done.1.x_ref = bf16[128,1024]{1,0:T(8,128)(2,1)S(1)} collective-permute-done((bf16[128,1024]{1,0:T(8,128)(2,1)S(1)}, bf16[128,1024]{1,0:T(8,128)(2,1)S(1)}, u32[]{:S(2)}, u32[]{:S(2)}) %collective-permute-start.1) | collective-permute-done | bytes 262176 | tf_op jit(solution)/shard_map/ppermute | solution.py:25
  21.6 4.9 %collective-permute-start.2 = (bf16[128,1024]{1,0:T(8,128)(2,1)S(1)}, bf16[128,1024]{1,0:T(8,128)(2,1)S(1)}, u32[]{:S(2)}, u32[]{:S(2)}) collective-permute-start(bf16[128,1024]{1,0:T(8,128)(2,1)S(1)} %collective-permute-done.1.x_ref), channel_id=1, source_target_pairs={{0,4},{4,12},{12,8},{8,0},{1,5},{5,13},{13,9},{9,1},{2,6},{6,14},{... | collective-permute-start | bytes 786440 | tf_op jit(solution)/shard_map/ppermute | solution.py:25
  27.0 5.4 %collective-permute-done.2.x_ref = bf16[128,1024]{1,0:T(8,128)(2,1)S(1)} collective-permute-done((bf16[128,1024]{1,0:T(8,128)(2,1)S(1)}, bf16[128,1024]{1,0:T(8,128)(2,1)S(1)}, u32[]{:S(2)}, u32[]{:S(2)}) %collective-permute-start.2) | collective-permute-done | bytes 262176 | tf_op jit(solution)/shard_map/ppermute | solution.py:25
  32.8 1.6 %collective-permute-start.12 = (bf16[128,192]{1,0:T(8,128)(2,1)S(1)}, bf16[128,192]{1,0:T(8,128)(2,1)S(1)}, u32[]{:S(2)}, u32[]{:S(2)}) collective-permute-start(bf16[128,192]{1,0:T(8,128)(2,1)S(1)} %fusion.8), channel_id=1, source_target_pairs={{0,3},{1,2},{2,1},{3,0},{4,7},{5,6},{6,5},{7,4},{8,11},{9,10},{10,... | collective-permute-start | bytes 147464 | tf_op jit(solution)/shard_map/ppermute | solution.py:15
  34.4 3.3 %collective-permute-start.17 = (bf16[192,512]{1,0:T(8,128)(2,1)S(1)}, bf16[192,512]{1,0:T(8,128)(2,1)S(1)}, u32[]{:S(2)}, u32[]{:S(2)}) collective-permute-start(bf16[192,512]{1,0:T(8,128)(2,1)S(1)} %collective-permute-done.3.refs_3_), channel_id=1, source_target_pairs={{0,8},{4,0},{12,4},{8,12},{1,9},{5,1},{13,5},{9,13},{2,10},{6,2},{... | collective-permute-start | bytes 589832 | tf_op jit(solution)/shard_map/ppermute | solution.py:25
  37.8 4.2 %collective-permute-done.17.refs_4_ = bf16[192,512]{1,0:T(8,128)(2,1)S(1)} collective-permute-done((bf16[192,512]{1,0:T(8,128)(2,1)S(1)}, bf16[192,512]{1,0:T(8,128)(2,1)S(1)}, u32[]{:S(2)}, u32[]{:S(2)}) %collective-permute-start.17) | collective-permute-done | bytes 196640 | tf_op jit(solution)/shard_map/ppermute | solution.py:25
  42.1 3.4 %collective-permute-start.18 = (bf16[192,512]{1,0:T(8,128)(2,1)S(1)}, bf16[192,512]{1,0:T(8,128)(2,1)S(1)}, u32[]{:S(2)}, u32[]{:S(2)}) collective-permute-start(bf16[192,512]{1,0:T(8,128)(2,1)S(1)} %collective-permute-done.17.refs_4_), channel_id=1, source_target_pairs={{0,8},{4,0},{12,4},{8,12},{1,9},{5,1},{13,5},{9,13},{2,10},{6,2},{... | collective-permute-start | bytes 589832 | tf_op jit(solution)/shard_map/ppermute | solution.py:25
  45.8 1.6 %collective-permute-start.19 = (bf16[192,512]{1,0:T(8,128)(2,1)S(1)}, bf16[192,512]{1,0:T(8,128)(2,1)S(1)}, u32[]{:S(2)}, u32[]{:S(2)}) collective-permute-start(bf16[192,512]{1,0:T(8,128)(2,1)S(1)} %collective-permute-done.3.refs_3_), channel_id=1, source_target_pairs={{0,16},{16,0},{1,17},{17,1},{2,18},{18,2},{3,19},{19,3},{4,20},{20... | collective-permute-start | bytes 589832 | tf_op jit(solution)/shard_map/ppermute | solution.py:15
  47.3 2.3 %collective-permute-start.10 = (bf16[128,192]{1,0:T(8,128)(2,1)S(1)}, bf16[128,192]{1,0:T(8,128)(2,1)S(1)}, u32[]{:S(2)}, u32[]{:S(2)}) collective-permute-start(bf16[128,192]{1,0:T(8,128)(2,1)S(1)} %get-tuple-element.61.refs_1_), channel_id=1, source_target_pairs={{0,9},{1,8},{2,11},{3,10},{4,1},{5,0},{6,3},{7,2},{12,5},{13,4},{1... | collective-permute-start | bytes 147464 | tf_op jit(solution)/shard_map/ppermute | solution.py:33
  51.1 5.3 %collective-permute-done.16.refs_2_ = bf16[128,192]{1,0:T(8,128)(2,1)S(1)} collective-permute-done((bf16[128,192]{1,0:T(8,128)(2,1)S(1)}, bf16[128,192]{1,0:T(8,128)(2,1)S(1)}, u32[]{:S(2)}, u32[]{:S(2)}) %collective-permute-start.16) | collective-permute-done | bytes 49184 | tf_op jit(solution)/shard_map/ppermute | solution.py:33
  56.4 1.5 %collective-permute-start.20 = (bf16[192,512]{1,0:T(8,128)(2,1)S(1)}, bf16[192,512]{1,0:T(8,128)(2,1)S(1)}, u32[]{:S(2)}, u32[]{:S(2)}) collective-permute-start(bf16[192,512]{1,0:T(8,128)(2,1)S(1)} %collective-permute-done.17.refs_4_), channel_id=1, source_target_pairs={{0,16},{16,0},{1,17},{17,1},{2,18},{18,2},{3,19},{19,3},{4,20},{20... | collective-permute-start | bytes 589832 | tf_op jit(solution)/shard_map/ppermute | solution.py:15
  58.7 5.0 %collective-permute-done.20.refs_7_ = bf16[192,512]{1,0:T(8,128)(2,1)S(1)} collective-permute-done((bf16[192,512]{1,0:T(8,128)(2,1)S(1)}, bf16[192,512]{1,0:T(8,128)(2,1)S(1)}, u32[]{:S(2)}, u32[]{:S(2)}) %collective-permute-start.20) | collective-permute-done | bytes 196640 | tf_op jit(solution)/shard_map/ppermute | solution.py:15
  63.6 2.1 %collective-permute-done.21.refs_8_ = bf16[192,512]{1,0:T(8,128)(2,1)S(1)} collective-permute-done((bf16[192,512]{1,0:T(8,128)(2,1)S(1)}, bf16[192,512]{1,0:T(8,128)(2,1)S(1)}, u32[]{:S(2)}, u32[]{:S(2)}) %collective-permute-start.21) | collective-permute-done | bytes 196640 | tf_op jit(solution)/shard_map/ppermute | solution.py:15
  66.8 1.5 %collective-permute-done.22 = bf16[4,128,192]{2,1,0:T(8,128)(2,1)S(1)} collective-permute-done((bf16[4,128,192]{2,1,0:T(8,128)(2,1)S(1)}, bf16[4,128,192]{2,1,0:T(8,128)(2,1)S(1)}, u32[]{:S(2)}, u32[]{:S(2)}) %collective-permute-start.22) | collective-permute-done | bytes 196640 | tf_op jit(solution)/shard_map/ppermute | solution.py:15
  68.8 7.9 %collective-permute-done.23 = bf16[4,128,192]{2,1,0:T(8,128)(2,1)S(1)} collective-permute-done((bf16[4,128,192]{2,1,0:T(8,128)(2,1)S(1)}, bf16[4,128,192]{2,1,0:T(8,128)(2,1)S(1)}, u32[]{:S(2)}, u32[]{:S(2)}) %collective-permute-start.23) | collective-permute-done | bytes 196640 | tf_op jit(solution)/shard_map/ppermute | solution.py:15
  78.8 2.5 %collective-permute-start.28 = (bf16[128,1024]{1,0:T(8,128)(2,1)S(1)}, bf16[128,1024]{1,0:T(8,128)(2,1)S(1)}, u32[]{:S(2)}, u32[]{:S(2)}) collective-permute-start(bf16[128,1024]{1,0:T(8,128)(2,1)S(1)} %collective-permute-done.27.refs_3_), channel_id=1, source_target_pairs={{0,4},{4,12},{12,8},{8,0},{1,5},{5,13},{13,9},{9,1},{2,6},{6,14},{... | collective-permute-start | bytes 786440 | tf_op jit(solution)/shard_map/ppermute | solution.py:25
  82.7 2.7 %collective-permute-done.24.refs_5_ = bf16[128,192]{1,0:T(8,128)(2,1)S(1)} collective-permute-done((bf16[128,192]{1,0:T(8,128)(2,1)S(1)}, bf16[128,192]{1,0:T(8,128)(2,1)S(1)}, u32[]{:S(2)}, u32[]{:S(2)}) %collective-permute-start.24) | collective-permute-done | bytes 49184 | tf_op jit(solution)/shard_map/ppermute | solution.py:33
  86.9 3.6 %collective-permute-done.30 = f32[1024]{0:T(1024)S(1)} collective-permute-done((f32[1024]{0:T(1024)S(1)}, f32[1024]{0:T(1024)S(1)}, u32[]{:S(2)}, u32[]{:S(2)}) %collective-permute-start.30) | collective-permute-done | bytes 4128 | tf_op jit(solution)/shard_map/ppermute | solution.py:15
  92.3 2.6 %collective-permute-done.31 = f32[1024]{0:T(1024)S(1)} collective-permute-done((f32[1024]{0:T(1024)S(1)}, f32[1024]{0:T(1024)S(1)}, u32[]{:S(2)}, u32[]{:S(2)}) %collective-permute-start.31) | collective-permute-done | bytes 4128 | tf_op jit(solution)/shard_map/ppermute | solution.py:15
  95.9 7.2 %collective-permute-done.29.refs_1_ = bf16[128,1024]{1,0:T(8,128)(2,1)S(1)} collective-permute-done((bf16[128,1024]{1,0:T(8,128)(2,1)S(1)}, bf16[128,1024]{1,0:T(8,128)(2,1)S(1)}, u32[]{:S(2)}, u32[]{:S(2)}) %collective-permute-start.29) | collective-permute-done | bytes 262176 | tf_op jit(solution)/shard_map/ppermute | solution.py:25
  (90 shorter events, 21.0 us)
Async XLA Ops:
  0.6 10.6 %collective-permute-start = (bf16[128,1024]{1,0:T(8,128)(2,1)}, bf16[128,1024]{1,0:T(8,128)(2,1)S(1)}, u32[]{:S(2)}, u32[]{:S(2)}) collective-permute-start(bf16[128,1024]{1,0:T(8,128)(2,1)} %x_ref.3), channel_id=1, source_target_pairs={{0,4},{4,12},{12,8},{8,0},{1,5},{5,13},{13,9},{9,1},{2,6},{6,14},{... | collective-permute-start | bytes 786440 | tf_op jit(solution)/shard_map/ppermute | solution.py:25
  6.6 8.1 %collective-permute-start.6 = (bf16[128,192]{1,0:T(8,128)(2,1)S(1)}, bf16[128,192]{1,0:T(8,128)(2,1)S(1)}, u32[]{:S(2)}, u32[]{:S(2)}) collective-permute-start(bf16[128,192]{1,0:T(8,128)(2,1)S(1)} %fusion.5), channel_id=1, source_target_pairs={{0,1},{1,0},{2,3},{3,2},{4,5},{5,4},{6,7},{7,6},{8,9},{9,8},{10,11... | collective-permute-start | bytes 147464 | tf_op jit(solution)/shard_map/ppermute | solution.py:15
  12.3 9.3 %collective-permute-start.1 = (bf16[128,1024]{1,0:T(8,128)(2,1)S(1)}, bf16[128,1024]{1,0:T(8,128)(2,1)S(1)}, u32[]{:S(2)}, u32[]{:S(2)}) collective-permute-start(bf16[128,1024]{1,0:T(8,128)(2,1)S(1)} %collective-permute-done.x_ref), channel_id=1, source_target_pairs={{0,4},{4,12},{12,8},{8,0},{1,5},{5,13},{13,9},{9,1},{2,6},{6,14},{... | collective-permute-start | bytes 786440 | tf_op jit(solution)/shard_map/ppermute | solution.py:25
  14.8 30.6 %collective-permute-start.7 = (bf16[128,192]{1,0:T(8,128)(2,1)S(1)}, bf16[128,192]{1,0:T(8,128)(2,1)S(1)}, u32[]{:S(2)}, u32[]{:S(2)}) collective-permute-start(bf16[128,192]{1,0:T(8,128)(2,1)S(1)} %fusion.6), channel_id=1, source_target_pairs={{0,3},{1,2},{2,1},{3,0},{4,7},{5,6},{6,5},{7,4},{8,11},{9,10},{10,... | collective-permute-start | bytes 147464 | tf_op jit(solution)/shard_map/ppermute | solution.py:15
  14.9 12.1 %collective-permute-start.3 = (bf16[192,512]{1,0:T(8,128)(2,1)S(1)}, bf16[192,512]{1,0:T(8,128)(2,1)S(1)}, u32[]{:S(2)}, u32[]{:S(2)}) collective-permute-start(bf16[192,512]{1,0:T(8,128)(2,1)S(1)} %constant_dynamic-slice_fusion), channel_id=1, source_target_pairs={{0,8},{4,0},{12,4},{8,12},{1,9},{5,1},{13,5},{9,13},{2,10},{6,2},{... | collective-permute-start | bytes 589832 | tf_op jit(solution)/shard_map/ppermute | solution.py:25
  17.0 28.4 %collective-permute-start.9 = (bf16[128,192]{1,0:T(8,128)(2,1)S(1)}, bf16[128,192]{1,0:T(8,128)(2,1)S(1)}, u32[]{:S(2)}, u32[]{:S(2)}) collective-permute-start(bf16[128,192]{1,0:T(8,128)(2,1)S(1)} %fusion.7), channel_id=1, source_target_pairs={{0,3},{1,2},{2,1},{3,0},{4,7},{5,6},{6,5},{7,4},{8,11},{9,10},{10,... | collective-permute-start | bytes 147464 | tf_op jit(solution)/shard_map/ppermute | solution.py:15
  21.6 10.7 %collective-permute-start.2 = (bf16[128,1024]{1,0:T(8,128)(2,1)S(1)}, bf16[128,1024]{1,0:T(8,128)(2,1)S(1)}, u32[]{:S(2)}, u32[]{:S(2)}) collective-permute-start(bf16[128,1024]{1,0:T(8,128)(2,1)S(1)} %collective-permute-done.1.x_ref), channel_id=1, source_target_pairs={{0,4},{4,12},{12,8},{8,0},{1,5},{5,13},{13,9},{9,1},{2,6},{6,14},{... | collective-permute-start | bytes 786440 | tf_op jit(solution)/shard_map/ppermute | solution.py:25
  26.9 5.9 %collective-permute-start.11 = (bf16[128,192]{1,0:T(8,128)(2,1)S(1)}, bf16[128,192]{1,0:T(8,128)(2,1)S(1)}, u32[]{:S(2)}, u32[]{:S(2)}) collective-permute-start(bf16[128,192]{1,0:T(8,128)(2,1)S(1)} %fusion.3), channel_id=1, source_target_pairs={{0,1},{1,0},{2,3},{3,2},{4,5},{5,4},{6,7},{7,6},{8,9},{9,8},{10,11... | collective-permute-start | bytes 147464 | tf_op jit(solution)/shard_map/ppermute | solution.py:15
  32.8 12.7 %collective-permute-start.12 = (bf16[128,192]{1,0:T(8,128)(2,1)S(1)}, bf16[128,192]{1,0:T(8,128)(2,1)S(1)}, u32[]{:S(2)}, u32[]{:S(2)}) collective-permute-start(bf16[128,192]{1,0:T(8,128)(2,1)S(1)} %fusion.8), channel_id=1, source_target_pairs={{0,3},{1,2},{2,1},{3,0},{4,7},{5,6},{6,5},{7,4},{8,11},{9,10},{10,... | collective-permute-start | bytes 147464 | tf_op jit(solution)/shard_map/ppermute | solution.py:15
  34.4 7.6 %collective-permute-start.17 = (bf16[192,512]{1,0:T(8,128)(2,1)S(1)}, bf16[192,512]{1,0:T(8,128)(2,1)S(1)}, u32[]{:S(2)}, u32[]{:S(2)}) collective-permute-start(bf16[192,512]{1,0:T(8,128)(2,1)S(1)} %collective-permute-done.3.refs_3_), channel_id=1, source_target_pairs={{0,8},{4,0},{12,4},{8,12},{1,9},{5,1},{13,5},{9,13},{2,10},{6,2},{... | collective-permute-start | bytes 589832 | tf_op jit(solution)/shard_map/ppermute | solution.py:25
  37.8 7.7 %collective-permute-start.15 = (bf16[128,192]{1,0:T(8,128)(2,1)S(1)}, bf16[128,192]{1,0:T(8,128)(2,1)S(1)}, u32[]{:S(2)}, u32[]{:S(2)}) collective-permute-start(bf16[128,192]{1,0:T(8,128)(2,1)S(1)} %fusion.9), channel_id=1, source_target_pairs={{0,3},{1,2},{2,1},{3,0},{4,7},{5,6},{6,5},{7,4},{8,11},{9,10},{10,... | collective-permute-start | bytes 147464 | tf_op jit(solution)/shard_map/ppermute | solution.py:15
  42.1 15.8 %collective-permute-start.18 = (bf16[192,512]{1,0:T(8,128)(2,1)S(1)}, bf16[192,512]{1,0:T(8,128)(2,1)S(1)}, u32[]{:S(2)}, u32[]{:S(2)}) collective-permute-start(bf16[192,512]{1,0:T(8,128)(2,1)S(1)} %collective-permute-done.17.refs_4_), channel_id=1, source_target_pairs={{0,8},{4,0},{12,4},{8,12},{1,9},{5,1},{13,5},{9,13},{2,10},{6,2},{... | collective-permute-start | bytes 589832 | tf_op jit(solution)/shard_map/ppermute | solution.py:25
  45.7 10.7 %collective-permute-start.16 = (bf16[128,192]{1,0:T(8,128)(2,1)S(1)}, bf16[128,192]{1,0:T(8,128)(2,1)S(1)}, u32[]{:S(2)}, u32[]{:S(2)}) collective-permute-start(bf16[128,192]{1,0:T(8,128)(2,1)S(1)} %get-tuple-element.53.refs_3_.refs_0_), channel_id=1, source_target_pairs={{0,5},{1,4},{2,7},{3,6},{4,13},{5,12},{6,15},{7,14},{12,9},{13,8},... | collective-permute-start | bytes 147464 | tf_op jit(solution)/shard_map/ppermute | solution.py:33
  45.8 12.9 %collective-permute-start.19 = (bf16[192,512]{1,0:T(8,128)(2,1)S(1)}, bf16[192,512]{1,0:T(8,128)(2,1)S(1)}, u32[]{:S(2)}, u32[]{:S(2)}) collective-permute-start(bf16[192,512]{1,0:T(8,128)(2,1)S(1)} %collective-permute-done.3.refs_3_), channel_id=1, source_target_pairs={{0,16},{16,0},{1,17},{17,1},{2,18},{18,2},{3,19},{19,3},{4,20},{20... | collective-permute-start | bytes 589832 | tf_op jit(solution)/shard_map/ppermute | solution.py:15
  47.3 11.3 %collective-permute-start.10 = (bf16[128,192]{1,0:T(8,128)(2,1)S(1)}, bf16[128,192]{1,0:T(8,128)(2,1)S(1)}, u32[]{:S(2)}, u32[]{:S(2)}) collective-permute-start(bf16[128,192]{1,0:T(8,128)(2,1)S(1)} %get-tuple-element.61.refs_1_), channel_id=1, source_target_pairs={{0,9},{1,8},{2,11},{3,10},{4,1},{5,0},{6,3},{7,2},{12,5},{13,4},{1... | collective-permute-start | bytes 147464 | tf_op jit(solution)/shard_map/ppermute | solution.py:33
  49.6 9.0 %collective-permute-start.13 = (bf16[128,192]{1,0:T(8,128)(2,1)S(1)}, bf16[128,192]{1,0:T(8,128)(2,1)S(1)}, u32[]{:S(2)}, u32[]{:S(2)}) collective-permute-start(bf16[128,192]{1,0:T(8,128)(2,1)S(1)} %get-tuple-element.63.refs_2_.refs_0_), channel_id=1, source_target_pairs={{0,13},{1,12},{2,15},{3,14},{4,9},{5,8},{6,11},{7,10},{12,1},{13,0... | collective-permute-start | bytes 147464 | tf_op jit(solution)/shard_map/ppermute | solution.py:33
  56.4 7.3 %collective-permute-start.20 = (bf16[192,512]{1,0:T(8,128)(2,1)S(1)}, bf16[192,512]{1,0:T(8,128)(2,1)S(1)}, u32[]{:S(2)}, u32[]{:S(2)}) collective-permute-start(bf16[192,512]{1,0:T(8,128)(2,1)S(1)} %collective-permute-done.17.refs_4_), channel_id=1, source_target_pairs={{0,16},{16,0},{1,17},{17,1},{2,18},{18,2},{3,19},{19,3},{4,20},{20... | collective-permute-start | bytes 589832 | tf_op jit(solution)/shard_map/ppermute | solution.py:15
  57.9 7.9 %collective-permute-start.21 = (bf16[192,512]{1,0:T(8,128)(2,1)S(1)}, bf16[192,512]{1,0:T(8,128)(2,1)S(1)}, u32[]{:S(2)}, u32[]{:S(2)}) collective-permute-start(bf16[192,512]{1,0:T(8,128)(2,1)S(1)} %collective-permute-done.18.refs_5_), channel_id=1, source_target_pairs={{0,16},{16,0},{1,17},{17,1},{2,18},{18,2},{3,19},{19,3},{4,20},{20... | collective-permute-start | bytes 589832 | tf_op jit(solution)/shard_map/ppermute | solution.py:15
  68.4 8.4 %collective-permute-start.23 = (bf16[4,128,192]{2,1,0:T(8,128)(2,1)S(1)}, bf16[4,128,192]{2,1,0:T(8,128)(2,1)S(1)}, u32[]{:S(2)}, u32[]{:S(2)}) collective-permute-start(bf16[4,128,192]{2,1,0:T(8,128)(2,1)S(1)} %fusion.1), channel_id=1, source_target_pairs={{0,3},{1,2},{2,1},{3,0},{4,7},{5,6},{6,5},{7,4},{8,11},{9,10},{10,... | collective-permute-start | bytes 589832 | tf_op jit(solution)/shard_map/ppermute | solution.py:15
  68.7 10.1 %collective-permute-start.27 = (bf16[128,1024]{1,0:T(8,128)(2,1)S(1)}, bf16[128,1024]{1,0:T(8,128)(2,1)S(1)}, u32[]{:S(2)}, u32[]{:S(2)}) collective-permute-start(bf16[128,1024]{1,0:T(8,128)(2,1)S(1)} %get-tuple-element.34.res_ref.refs_2_), channel_id=1, source_target_pairs={{0,4},{4,12},{12,8},{8,0},{1,5},{5,13},{13,9},{9,1},{2,6},{6,14},{... | collective-permute-start | bytes 786440 | tf_op jit(solution)/shard_map/ppermute | solution.py:25
  76.9 5.8 %collective-permute-start.25 = (bf16[128,192]{1,0:T(8,128)(2,1)S(1)}, bf16[128,192]{1,0:T(8,128)(2,1)S(1)}, u32[]{:S(2)}, u32[]{:S(2)}) collective-permute-start(bf16[128,192]{1,0:T(8,128)(2,1)S(1)} %get-tuple-element.55), channel_id=1, source_target_pairs={{0,13},{1,12},{2,15},{3,14},{4,9},{5,8},{6,11},{7,10},{12,1},{13,0... | collective-permute-start | bytes 147464 | tf_op jit(solution)/shard_map/ppermute | solution.py:33
  77.3 8.1 %collective-permute-start.24 = (bf16[128,192]{1,0:T(8,128)(2,1)S(1)}, bf16[128,192]{1,0:T(8,128)(2,1)S(1)}, u32[]{:S(2)}, u32[]{:S(2)}) collective-permute-start(bf16[128,192]{1,0:T(8,128)(2,1)S(1)} %get-tuple-element.56), channel_id=1, source_target_pairs={{0,5},{1,4},{2,7},{3,6},{4,13},{5,12},{6,15},{7,14},{12,9},{13,8},... | collective-permute-start | bytes 147464 | tf_op jit(solution)/shard_map/ppermute | solution.py:33
  78.8 16.8 %collective-permute-start.28 = (bf16[128,1024]{1,0:T(8,128)(2,1)S(1)}, bf16[128,1024]{1,0:T(8,128)(2,1)S(1)}, u32[]{:S(2)}, u32[]{:S(2)}) collective-permute-start(bf16[128,1024]{1,0:T(8,128)(2,1)S(1)} %collective-permute-done.27.refs_3_), channel_id=1, source_target_pairs={{0,4},{4,12},{12,8},{8,0},{1,5},{5,13},{13,9},{9,1},{2,6},{6,14},{... | collective-permute-start | bytes 786440 | tf_op jit(solution)/shard_map/ppermute | solution.py:25
  95.6 7.5 %collective-permute-start.29 = (bf16[128,1024]{1,0:T(8,128)(2,1)S(1)}, bf16[128,1024]{1,0:T(8,128)(2,1)S(1)}, u32[]{:S(2)}, u32[]{:S(2)}) collective-permute-start(bf16[128,1024]{1,0:T(8,128)(2,1)S(1)} %collective-permute-done.28.refs_1_), channel_id=1, source_target_pairs={{0,4},{4,12},{12,8},{8,0},{1,5},{5,13},{13,9},{9,1},{2,6},{6,14},{... | collective-permute-start | bytes 786440 | tf_op jit(solution)/shard_map/ppermute | solution.py:25
  (17 other events, 96.2 us)

commit v3 on v0

v3 whole, which is shorter than its diff:
```python
import jax
import jax.numpy as jnp
from jax import lax
from jax.experimental import pallas as pl
from jax.experimental.pallas import tpu as pltpu
from jax.sharding import PartitionSpec as P

sparsity_coef = 3.0
f32 = jnp.float32
bf16 = jnp.bfloat16


def swap(value, axis, distance):
    count = lax.axis_size(axis)
    return lax.ppermute(value, axis, [(i, i ^ distance) for i in range(count)])


def swap_crossed(value, distance):
    lat, width = lax.axis_size("lat"), lax.axis_size("width")
    pairs = [
        (z * width + w, (z ^ distance) * width + (w ^ 1)) for z in range(lat) for w in range(width)
    ]
    return lax.ppermute(value, ("lat", "width"), pairs)


def after(value, *earlier):
    return lax.optimization_barrier((value, *earlier))[0]


def stage(*values):
    return lax.optimization_barrier(values)


def keeps_low():
    index, odd = lax.axis_index("width"), 0
    for bit in range((lax.axis_size("width") - 1).bit_length()):
        odd = odd ^ ((index >> bit) & 1)
    return odd == 0


def pair_sum(keep, send):
    return keep.astype(f32) + swap(send, "width", 1).astype(f32)


def rest_sum(total):
    step = 3
    while step < lax.axis_size("width") * 3 // 2:
        sent = lax.reduce_precision(total, 8, 7)
        total = sent + swap(sent.astype(bf16), "width", step).astype(f32)
        step *= 2
    return total


def join(kept, other):
    low = keeps_low()
    first, second = jnp.where(low, kept, other), jnp.where(low, other, kept)
    return jnp.concatenate([first, second], axis=0)


def plain_sum(value, axis):
    step = 1
    while step < lax.axis_size(axis):
        value = value + swap(value, axis, step)
        step *= 2
    return value


def mm(a, b, contract):
    return lax.dot_general(a, b, ((contract[:1], contract[1:]), ((), ())), preferred_element_type=f32)


VMEM = pl.BlockSpec(memory_space=pltpu.VMEM)


def call(kernel, name, outs, *operands):
    return pl.pallas_call(
        kernel,
        out_shape=[jax.ShapeDtypeStruct(shape, kind) for shape, kind in outs],
        in_specs=[VMEM] * len(operands),
        out_specs=[VMEM] * len(outs),
        cost_estimate=pl.CostEstimate(flops=10**6, bytes_accessed=10**6, transcendentals=0),
        compiler_params=pltpu.CompilerParams(vmem_limit_bytes=24 * 2**20),
        name=name,
    )(*operands)


def split(part, keep_ref, send_ref):
    rows = part.shape[0] // 2
    low = keeps_low()
    keep_ref[...] = jnp.where(low, part[:rows], part[rows:]).astype(bf16)
    send_ref[...] = jnp.where(low, part[rows:], part[:rows]).astype(bf16)


def part_of(x, b_dec, w_enc_t):
    rows, lat = x.shape[0] // 2, w_enc_t.shape[0]

    def kernel(x_ref, b_ref, w_ref, centered_ref, keep_ref, send_ref):
        centered_ref[...] = (x_ref[...].astype(f32) - b_ref[...]).astype(bf16)
        split(mm(centered_ref[...], w_ref[...], (1, 1)), keep_ref, send_ref)

    outs = [(x.shape, bf16), ((rows, lat), bf16), ((rows, lat), bf16)]
    return call(kernel, "part_of", outs, x, b_dec[None], w_enc_t)


def error_start(x, rest, b_dec):
    def kernel(x_ref, r_ref, b_ref, base):
        base[...] = r_ref[...].astype(f32) + b_ref[...] - x_ref[...].astype(f32)

    return call(kernel, "error_start", [(x.shape, f32)], x, rest, b_dec[None])[0]


def res_and_parts(scale, base, w_dec, codes, codes_other, crossed, crossed_other, mine, other):
    rows, cols = base.shape
    half, lat, count = cols // 2, w_dec.shape[0], len(mine)

    def kernel(base_ref, w_ref, c_ref, c_other_ref, x_ref, x_other_ref, *refs):
        m, o = refs[:count], refs[count : 2 * count]
        codes_ref, res_ref, keep_ref, send_ref = refs[2 * count :]
        first = lax.axis_index("groups") == 0
        for k in range(count + 1):
            codes_ref[k] = join(c_ref[k].astype(f32), c_other_ref[k].astype(f32)).astype(bf16)
        start = base_ref[...] + mm(codes_ref[0], w_ref[...], (1, 0))
        held = [
            join(x_other_ref[k].astype(f32), x_ref[k].astype(f32)).astype(bf16)
            for k in range(count)
        ]
        r_mine = sum(mm(held[k], m[k][...], (1, 0)) for k in range(count))
        r_other = sum(mm(held[k], o[k][...], (1, 0)) for k in range(count))
        low = scale * (start[:, :half] + jnp.where(first, r_mine, r_other))
        high = scale * (start[:, half:] + jnp.where(first, r_other, r_mine))
        res_ref[:, :half] = low.astype(bf16)
        res_ref[:, half:] = high.astype(bf16)
        g_mine = jnp.where(first, low, high).astype(bf16)
        g_other = jnp.where(first, high, low).astype(bf16)
        split(mm(res_ref[...], w_ref[...], (1, 1)), keep_ref.at[0], send_ref.at[0])
        for k in range(count):
            part = mm(g_mine, m[k][...], (1, 1)) + mm(g_other, o[k][...], (1, 1))
            split(part, keep_ref.at[k + 1], send_ref.at[k + 1])

    parts = ((count + 1, rows // 2, lat), bf16)
    outs = [((count + 1, rows, lat), bf16), ((rows, cols), bf16), parts, parts]
    return call(
        kernel, "res_and_parts", outs,
        base, w_dec, codes, codes_other, crossed, crossed_other, *mine, *other,
    )


def dec_add(total, codes, res, *shares):
    count = len(res)

    def kernel(total_ref, c_ref, *refs):
        value = sum(mm(c_ref[k], refs[k][...], (0, 0)) for k in range(count))
        refs[count + len(shares)][...] = total_ref[...] + value
        if shares:
            refs[-1][...] = refs[count][...] + refs[count + 1][...]

    outs = [(total.shape, f32)] + [(s.shape, f32) for s in shares[:1]]
    return call(kernel, "dec_add", outs, total, codes, *res, *shares)


def pre_grads(codes, sums, sums_other, crossed, crossed_other, threshold, w_enc_t, res):
    count = codes.shape[0]

    def kernel(n_ref, w_ref, res_ref, c_ref, s_ref, so_ref, x_ref, xo_ref, out, bias, share):
        total = 0.0
        for k in range(count):
            if k:
                back = join(xo_ref[k - 1].astype(f32), x_ref[k - 1].astype(f32))
            else:
                back = join(s_ref[0].astype(f32), so_ref[0].astype(f32))
            g = jnp.where(c_ref[k].astype(f32) > 0, back + n_ref[...], 0.0)
            out[k] = g.astype(bf16)
            total = total + jnp.sum(out[k].astype(f32), axis=0, keepdims=True)
        bias[...] = total
        high = total.astype(bf16)
        rest = total - high.astype(f32)
        mid = rest.astype(bf16)
        low = (rest - mid.astype(f32)).astype(bf16)
        row = lax.broadcasted_iota(jnp.int32, (8, total.shape[1]), 0)
        pieces = jnp.where(row == 0, high.astype(f32), jnp.where(row == 1, mid.astype(f32), 0.0))
        pieces = jnp.where(row == 2, low.astype(f32), pieces).astype(bf16)
        product = jnp.sum(mm(pieces, w_ref[...], (1, 0)), axis=0, keepdims=True)
        share[...] = jnp.sum(res_ref[...].astype(f32), axis=0, keepdims=True) - product

    lat, cols = w_enc_t.shape
    outs = [(codes.shape, bf16), ((1, lat), f32), ((1, cols), f32)]
    grads, bias, share = call(
        kernel, "pre_grads", outs,
        threshold[None], w_enc_t, res, codes, sums, sums_other, crossed, crossed_other,
    )
    return grads, bias[0], share


def enc_end(centered, grads):
    count = len(centered)

    def kernel(g_ref, *refs):
        refs[-1][...] = sum(mm(g_ref[k], refs[k][...], (0, 0)) for k in range(count))

    outs = [((grads.shape[2], centered[0].shape[1]), f32)]
    return call(kernel, "enc_end", outs, grads, *centered)[0]


def halves(stacked, first):
    return stacked[:first], stacked[first:]


def shards(activations, rest_recon, w_enc, b_enc, w_dec, b_dec):
    count = lax.axis_size("lat")
    rows = activations.shape[0]
    row_scale = float((rows * count) ** -0.5)
    w_enc_t = w_enc.T
    half = w_dec.shape[1] // 2
    late = 2
    order = [k for k in range(count) if k != late] + [late]
    early = order[1:-1]

    def early_swaps(block):
        return [swap(block, "lat", k) for k in early]

    def late_swap(block, swapped):
        return swap(swapped[-1], "lat", 1) if count == 4 else swap(block, "lat", late)

    mine_own = lax.dynamic_slice_in_dim(w_dec, lax.axis_index("groups") * half, half, axis=1)
    xs, mine = early_swaps(activations), early_swaps(mine_own)
    arrived = stage(*xs, *mine)
    xs, mine = list(arrived[: len(xs)]), list(arrived[len(xs) :])

    final, mine_late = late_swap(activations, xs), late_swap(mine_own, mine)
    other = [swap(m, "groups", 1) for m in mine]
    dec_float = after(w_dec, mine[0]).astype(f32)
    squares = jnp.sum(dec_float * dec_float, axis=1)
    squares = squares + swap(squares, "width", 1)
    base = error_start(activations, rest_recon, b_dec)
    centered, keep, send = zip(*(part_of(x, b_dec, w_enc_t) for x in [activations, *xs]))
    total = pair_sum(jnp.stack(keep), jnp.stack(send))
    final, mine_late, squares, base, total, *other = stage(
        final, mine_late, squares, base, total, *other
    )
    mine.append(mine_late)

    last_centered, last_keep, last_send = part_of(final, b_dec, w_enc_t)
    centered += (last_centered,)
    total = jnp.concatenate([total, pair_sum(last_keep, last_send)[None]])
    codes = jnp.maximum(rest_sum(total) + b_enc, 0.0).astype(bf16)
    other.append(swap(mine_late, "groups", 1))
    codes, other[-1] = stage(codes, other[-1])
    crossed = jnp.stack([swap_crossed(codes[i], k) for i, k in enumerate(order) if k])
    codes_other = swap(codes, "width", 1)
    step = 3
    while step < lax.axis_size("width") * 3 // 2:
        squares = squares + swap(after(squares, codes), "width", step)
        step *= 2
    crossed, codes_other, squares = stage(crossed, codes_other, squares)
    crossed_other = swap(crossed, "width", 1)
    codes, res_grad, keep, send = res_and_parts(
        2.0 * row_scale, base, w_dec, codes, codes_other, crossed, crossed_other, mine, other
    )

    res = early_swaps(res_grad)
    sums = rest_sum(pair_sum(keep, send)).astype(bf16)
    crossed = jnp.stack([swap_crossed(sums[i], k) for i, k in enumerate(order) if k])
    sums_other = swap(sums[:1], "width", 1)
    res[-1], crossed, sums_other = stage(res[-1], crossed, sums_other)
    norms = jnp.sqrt(squares + 1e-06)
    grads, grad_benc, share = pre_grads(
        codes,
        sums[:1],
        sums_other,
        crossed,
        swap(crossed, "width", 1),
        sparsity_coef * row_scale * norms,
        w_enc_t,
        res_grad,
    )
    step = 1
    while 2 * step < count:
        share = share + swap(share, "lat", step)
        step *= 2
    share, *res = stage(share, *res)
    res_late = late_swap(res_grad, res)
    grad_enc = enc_end(centered, grads).T
    code_total = jnp.sum(codes.astype(f32), axis=(0, 1))
    sparsity = (sparsity_coef * row_scale * code_total / norms)[:, None] * w_dec.astype(f32)
    (grad_dec,) = dec_add(sparsity, codes[:-1], [res_grad, *res])
    grad_dec, grad_bdec = dec_add(
        grad_dec, codes[-1:], [res_late], share, swap(share, "lat", step)
    )
    return (grad_enc, grad_benc, grad_dec, grad_bdec[0])


def solution(mesh):
    placed = (
        P(("groups", "lat"), "width"),
        P(("groups", "lat"), "width"),
        P("width", "lat"),
        P("lat"),
        P("lat", "width"),
        P("width"),
    )
    return jax.shard_map(
        shards,
        mesh=mesh,
        in_specs=placed,
        out_specs=(
            P(("groups", "width"), "lat"),
            P(("groups", "lat")),
            P(("groups", "lat"), "width"),
            P(("groups", "width")),
        ),
        check_vma=False,
    )
```

time: 192 us -> 94.8 us (0.49)
  waiting for transfers between devices: 142 us -> 51.9 us
  starting transfers between devices: 0.21 us -> 32.3 us
  blocking collectives: 18.1 us -> 0 us
  between operations: 13.8 us -> 0.9 us
  matrix products: 11.2 us -> 0 us
  Pallas kernels: 0 us -> 6.2 us
  other arithmetic: 5.72 us -> 0.66 us
  local copies, waits for them, and re-layouts: 0.05 us -> 2.67 us
    psum x2 -> x0, waiting for transfers between devices: 62.8 us -> none  [the longest x1 31.6 us: shards(): lax.psum(pre_part.astype(jnp.bfloat16), 'width').astype(jnp.float32)]
    all_gather x2 -> x0, waiting for transfers between devices: 51.9 us -> none  [the longest x1 31.8 us: shards(): gathered = lax.all_gather(centered, 'lat', axis=0, tiled=True)]
    ppermute x0 -> x31, waiting for transfers between devices: none -> 51.9 us  [the longest x25 44.4 us: swap(): return lax.ppermute(value, axis, [(i, i ^ distance) for i in range(count)])]
    ppermute x0 -> x31, starting transfers between devices: none -> 32.3 us  [the longest x25 24.6 us: swap(): return lax.ppermute(value, axis, [(i, i ^ distance) for i in range(count)])]
    reduce_scatter x1 -> x0, waiting for transfers between devices: 27.2 us -> none  [shards(): lax.psum_scatter(jnp.dot(codes, w_dec, preferred_element_type=jnp.float32...]
    psum x2 -> x0, blocking collectives: 18.1 us -> none  [the longest x1 11.7 us: shards(): enc_total = lax.psum(enc_term, 'lat')]
    dot_general x6 -> x0, matrix products: 11.2 us -> none  [the longest x1 2.51 us: shards(): jnp.dot(codes, w_dec, preferred_element_type=jnp.float32)]
    pallas_call x0 -> x10, Pallas kernels: none -> 6.2 us  [call(): pl.pallas_call(kernel, out_shape=[jax.ShapeDtypeStruct(shape, kind) for s...]
  transfers between devices with their start and end apart: 5 -> 31, of which waited for: 5 -> 18; matrix products, arithmetic and copies ran while one was open for 0% -> 2% of each run, Pallas kernels for 0% -> 4%
where the time goes in v3:
time: 94.8 us; the launch traced here: 94.6 us
  waiting for transfers between devices  51.9 us (55%)
  starting transfers between devices  32.3 us (34%)
  Pallas kernels  6.2 us (7%)
  local copies, waits for them, and re-layouts  2.67 us (3%)
    ppermute x25, waiting for transfers between devices, swap(): return lax.ppermute(value, axis, [(i, i ^ distance) for i in range(count)])  44.4 us
    ppermute x25, starting transfers between devices, swap(): return lax.ppermute(value, axis, [(i, i ^ distance) for i in range(count)])  24.6 us
    ppermute x6, starting transfers between devices, swap_crossed(): return lax.ppermute(value, ('lat', 'width'), pairs)  7.66 us
    ppermute x6, waiting for transfers between devices, swap_crossed(): return lax.ppermute(value, ('lat', 'width'), pairs)  7.51 us
    pallas_call x10, Pallas kernels, call(): pl.pallas_call(kernel, out_shape=[jax.ShapeDtypeStruct(shape, kind) for s...  6.2 us
  transfers between devices with their start and end apart: 31, of which 18 were waited for; matrix products, arithmetic and copies ran while one was open for 2% of the time, Pallas kernels for 4%

profile of v3, /device:TPU:0, one launch (start us, length us, event | category | flops | bytes accessed | tf_op | source)
XLA Modules:
  0.0 94.6 jit_solution(3264777800931051673)
XLA Ops:
  0.6 5.1 %collective-permute-start.1 = (bf16[128,1024]{1,0:T(8,128)(2,1)}, bf16[128,1024]{1,0:T(8,128)(2,1)S(1)}, u32[]{:S(2)}, u32[]{:S(2)}) collective-permute-start(bf16[128,1024]{1,0:T(8,128)(2,1)} %x_ref.3), channel_id=1, source_target_pairs={{0,12},{4,8},{8,4},{12,0},{1,13},{5,9},{9,5},{13,1},{2,14},{6,10},... | collective-permute-start | bytes 786440 | tf_op jit(solution)/shard_map/ppermute | solution.py:15
  7.7 1.2 %collective-permute-start.2 = (bf16[192,512]{1,0:T(8,128)(2,1)S(1)}, bf16[192,512]{1,0:T(8,128)(2,1)S(1)}, u32[]{:S(2)}, u32[]{:S(2)}) collective-permute-start(bf16[192,512]{1,0:T(8,128)(2,1)S(1)} %constant_dynamic-slice_fusion), channel_id=1, source_target_pairs={{0,4},{4,0},{8,12},{12,8},{1,5},{5,1},{9,13},{13,9},{2,6},{6,2},{1... | collective-permute-start | bytes 589832 | tf_op jit(solution)/shard_map/ppermute | solution.py:15
  10.1 12.9 %collective-permute-done.3.refs_1_ = bf16[192,512]{1,0:T(8,128)(2,1)S(1)} collective-permute-done((bf16[192,512]{1,0:T(8,128)(2,1)S(1)}, bf16[192,512]{1,0:T(8,128)(2,1)S(1)}, u32[]{:S(2)}, u32[]{:S(2)}) %collective-permute-start.3) | collective-permute-done | bytes 196640 | tf_op jit(solution)/shard_map/ppermute | solution.py:15
  23.1 3.4 %collective-permute-done.2.refs_0_ = bf16[192,512]{1,0:T(8,128)(2,1)S(1)} collective-permute-done((bf16[192,512]{1,0:T(8,128)(2,1)S(1)}, bf16[192,512]{1,0:T(8,128)(2,1)S(1)}, u32[]{:S(2)}, u32[]{:S(2)}) %collective-permute-start.2) | collective-permute-done | bytes 196640 | tf_op jit(solution)/shard_map/ppermute | solution.py:15
  26.4 1.7 %collective-permute-start.4 = (bf16[128,1024]{1,0:T(8,128)(2,1)S(1)}, bf16[128,1024]{1,0:T(8,128)(2,1)S(1)}, u32[]{:S(2)}, u32[]{:S(2)}) collective-permute-start(bf16[128,1024]{1,0:T(8,128)(2,1)S(1)} %collective-permute-done.1.x_ref), channel_id=1, source_target_pairs={{0,4},{4,0},{8,12},{12,8},{1,5},{5,1},{9,13},{13,9},{2,6},{6,2},{1... | collective-permute-start | bytes 786440 | tf_op jit(solution)/shard_map/ppermute | solution.py:15
  29.9 1.6 %collective-permute-start.9 = (bf16[192,512]{1,0:T(8,128)(2,1)S(1)}, bf16[192,512]{1,0:T(8,128)(2,1)S(1)}, u32[]{:S(2)}, u32[]{:S(2)}) collective-permute-start(bf16[192,512]{1,0:T(8,128)(2,1)S(1)} %collective-permute-done.3.refs_1_), channel_id=1, source_target_pairs={{0,16},{16,0},{1,17},{17,1},{2,18},{18,2},{3,19},{19,3},{4,20},{20... | collective-permute-start | bytes 589832 | tf_op jit(solution)/shard_map/ppermute | solution.py:15
  32.4 5.3 %collective-permute-done.9.refs_4_ = bf16[192,512]{1,0:T(8,128)(2,1)S(1)} collective-permute-done((bf16[192,512]{1,0:T(8,128)(2,1)S(1)}, bf16[192,512]{1,0:T(8,128)(2,1)S(1)}, u32[]{:S(2)}, u32[]{:S(2)}) %collective-permute-start.9) | collective-permute-done | bytes 196640 | tf_op jit(solution)/shard_map/ppermute | solution.py:15
  38.9 2.5 %collective-permute-done.8.refs_3_ = bf16[192,512]{1,0:T(8,128)(2,1)S(1)} collective-permute-done((bf16[192,512]{1,0:T(8,128)(2,1)S(1)}, bf16[192,512]{1,0:T(8,128)(2,1)S(1)}, u32[]{:S(2)}, u32[]{:S(2)}) %collective-permute-start.8) | collective-permute-done | bytes 196640 | tf_op jit(solution)/shard_map/ppermute | solution.py:15
  43.0 1.3 %collective-permute-start.11 = (bf16[4,64,192]{2,1,0:T(8,128)(2,1)S(1)}, bf16[4,64,192]{2,1,0:T(8,128)(2,1)S(1)}, u32[]{:S(2)}, u32[]{:S(2)}) collective-permute-start(bf16[4,64,192]{2,1,0:T(8,128)(2,1)S(1)} %fusion.1), channel_id=1, source_target_pairs={{0,3},{1,2},{2,1},{3,0},{4,7},{5,6},{6,5},{7,4},{8,11},{9,10},{10,... | collective-permute-start | bytes 294920 | tf_op jit(solution)/shard_map/ppermute | solution.py:15
  44.3 1.5 %collective-permute-start.12 = (bf16[192,512]{1,0:T(8,128)(2,1)S(1)}, bf16[192,512]{1,0:T(8,128)(2,1)S(1)}, u32[]{:S(2)}, u32[]{:S(2)}) collective-permute-start(bf16[192,512]{1,0:T(8,128)(2,1)S(1)} %collective-permute-done.5.refs_2_), channel_id=1, source_target_pairs={{0,16},{16,0},{1,17},{17,1},{2,18},{18,2},{3,19},{19,3},{4,20},{20... | collective-permute-start | bytes 589832 | tf_op jit(solution)/shard_map/ppermute | solution.py:15
  45.8 2.7 %collective-permute-done.11 = bf16[4,64,192]{2,1,0:T(8,128)(2,1)S(1)} collective-permute-done((bf16[4,64,192]{2,1,0:T(8,128)(2,1)S(1)}, bf16[4,64,192]{2,1,0:T(8,128)(2,1)S(1)}, u32[]{:S(2)}, u32[]{:S(2)}) %collective-permute-start.11) | collective-permute-done | bytes 98336 | tf_op jit(solution)/shard_map/ppermute | solution.py:15
  48.5 2.9 %collective-permute-done.12.refs_5_ = bf16[192,512]{1,0:T(8,128)(2,1)S(1)} collective-permute-done((bf16[192,512]{1,0:T(8,128)(2,1)S(1)}, bf16[192,512]{1,0:T(8,128)(2,1)S(1)}, u32[]{:S(2)}, u32[]{:S(2)}) %collective-permute-start.12) | collective-permute-done | bytes 196640 | tf_op jit(solution)/shard_map/ppermute | solution.py:15
  52.2 2.5 %collective-permute-start.14 = (bf16[64,192]{1,0:T(8,128)(2,1)S(1)}, bf16[64,192]{1,0:T(8,128)(2,1)S(1)}, u32[]{:S(2)}, u32[]{:S(2)}) collective-permute-start(bf16[64,192]{1,0:T(8,128)(2,1)S(1)} %get-tuple-element.100), channel_id=1, source_target_pairs={{0,13},{1,12},{2,15},{3,14},{4,9},{5,8},{6,11},{7,10},{8,5},{9,4},... | collective-permute-start | bytes 73736 | tf_op jit(solution)/shard_map/ppermute | solution.py:23
  55.9 1.9 %collective-permute-done.17 = f32[192]{0:T(256)S(1)} collective-permute-done((f32[192]{0:T(256)S(1)}, f32[192]{0:T(256)S(1)}, u32[]{:S(2)}, u32[]{:S(2)}) %collective-permute-start.17) | collective-permute-done | bytes 800 | tf_op jit(solution)/shard_map/ppermute | solution.py:15
  63.0 2.1 %collective-permute-start.21 = (bf16[128,1024]{1,0:T(8,128)(2,1)S(1)}, bf16[128,1024]{1,0:T(8,128)(2,1)S(1)}, u32[]{:S(2)}, u32[]{:S(2)}) collective-permute-start(bf16[128,1024]{1,0:T(8,128)(2,1)S(1)} %get-tuple-element.75.res_ref.refs_0_), channel_id=1, source_target_pairs={{0,12},{4,8},{8,4},{12,0},{1,13},{5,9},{9,5},{13,1},{2,14},{6,10},... | collective-permute-start | bytes 786440 | tf_op jit(solution)/shard_map/ppermute | solution.py:15
  65.1 2.6 %collective-permute-done.20 = bf16[4,64,192]{2,1,0:T(8,128)(2,1)S(1)} collective-permute-done((bf16[4,64,192]{2,1,0:T(8,128)(2,1)S(1)}, bf16[4,64,192]{2,1,0:T(8,128)(2,1)S(1)}, u32[]{:S(2)}, u32[]{:S(2)}) %collective-permute-start.20) | collective-permute-done | bytes 98336 | tf_op jit(solution)/shard_map/ppermute | solution.py:15
  68.4 2.3 %collective-permute-start.24 = (bf16[64,192]{1,0:T(8,128)(2,1)S(1)}, bf16[64,192]{1,0:T(8,128)(2,1)S(1)}, u32[]{:S(2)}, u32[]{:S(2)}) collective-permute-start(bf16[64,192]{1,0:T(8,128)(2,1)S(1)} %get-tuple-element.95), channel_id=1, source_target_pairs={{0,9},{1,8},{2,11},{3,10},{4,13},{5,12},{6,15},{7,14},{8,1},{9,0},... | collective-permute-start | bytes 73736 | tf_op jit(solution)/shard_map/ppermute | solution.py:23
  70.7 1.5 %collective-permute-start.23 = (bf16[64,192]{1,0:T(8,128)(2,1)S(1)}, bf16[64,192]{1,0:T(8,128)(2,1)S(1)}, u32[]{:S(2)}, u32[]{:S(2)}) collective-permute-start(bf16[64,192]{1,0:T(8,128)(2,1)S(1)} %get-tuple-element.96), channel_id=1, source_target_pairs={{0,13},{1,12},{2,15},{3,14},{4,9},{5,8},{6,11},{7,10},{8,5},{9,4},... | collective-permute-start | bytes 73736 | tf_op jit(solution)/shard_map/ppermute | solution.py:23
  72.2 3.8 %collective-permute-done.22 = bf16[64,192]{1,0:T(8,128)(2,1)S(1)} collective-permute-done((bf16[64,192]{1,0:T(8,128)(2,1)S(1)}, bf16[64,192]{1,0:T(8,128)(2,1)S(1)}, u32[]{:S(2)}, u32[]{:S(2)}) %collective-permute-start.22) | collective-permute-done | bytes 24608 | tf_op jit(solution)/shard_map/ppermute | solution.py:23
  76.0 3.7 %collective-permute-done.24 = bf16[64,192]{1,0:T(8,128)(2,1)S(1)} collective-permute-done((bf16[64,192]{1,0:T(8,128)(2,1)S(1)}, bf16[64,192]{1,0:T(8,128)(2,1)S(1)}, u32[]{:S(2)}, u32[]{:S(2)}) %collective-permute-start.24) | collective-permute-done | bytes 24608 | tf_op jit(solution)/shard_map/ppermute | solution.py:23
  83.3 2.6 %collective-permute-done.27 = f32[1,1024]{1,0:T(1,128)S(1)} collective-permute-done((f32[1,1024]{1,0:T(1,128)S(1)}, f32[1,1024]{1,0:T(1,128)S(1)}, u32[]{:S(2)}, u32[]{:S(2)}) %collective-permute-start.27) | collective-permute-done | bytes 4128 | tf_op jit(solution)/shard_map/ppermute | solution.py:15
  87.0 1.9 %collective-permute-start.30 = (f32[1,1024]{1,0:T(1,128)S(1)}, f32[1,1024]{1,0:T(1,128)S(1)}, u32[]{:S(2)}, u32[]{:S(2)}) collective-permute-start(f32[1,1024]{1,0:T(1,128)S(1)} %add.53.refs_1_), channel_id=1, source_target_pairs={{0,8},{4,12},{8,0},{12,4},{1,9},{5,13},{9,1},{13,5},{2,10},{6,14},... | collective-permute-start | bytes 12296 | tf_op jit(solution)/shard_map/ppermute | solution.py:15
  89.1 1.5 %enc_end.1 = f32[192,1024]{1,0:T(8,128)} custom-call(bf16[4,128,192]{2,1,0:T(8,128)(2,1)S(1)} %get-tuple-element.81.g_ref, bf16[128,1024]{1,0:T(8,128)(2,1)S(1)} %get-tuple-element.82.refs_0_, bf16[128,1024]{1,0:T(8,128)(2,1)S(1)} %get-tuple-element.83.refs_1_, bf16[128,1024]{1,0:T(8,128)(2,1)S(1)} %get-tuple-element.84.refs_2_, ...), custom_call_target="tpu_custom_call" | custom-call | flops 1000000 | bytes 1000000 | tf_op jit(solution)/shard_map/enc_end/pallas_call | solution.py:76
  91.9 1.6 %collective-permute-done.29.refs_0_ = bf16[128,1024]{1,0:T(8,128)(2,1)S(1)} collective-permute-done((bf16[128,1024]{1,0:T(8,128)(2,1)S(1)}, bf16[128,1024]{1,0:T(8,128)(2,1)S(1)}, u32[]{:S(2)}, u32[]{:S(2)}) %collective-permute-start.29) | collective-permute-done | bytes 262176 | tf_op jit(solution)/shard_map/ppermute | solution.py:15
  (83 shorter events, 23.6 us)
Async XLA Ops:
  0.6 25.8 %collective-permute-start.1 = (bf16[128,1024]{1,0:T(8,128)(2,1)}, bf16[128,1024]{1,0:T(8,128)(2,1)S(1)}, u32[]{:S(2)}, u32[]{:S(2)}) collective-permute-start(bf16[128,1024]{1,0:T(8,128)(2,1)} %x_ref.3), channel_id=1, source_target_pairs={{0,12},{4,8},{8,4},{12,0},{1,13},{5,9},{9,5},{13,1},{2,14},{6,10},... | collective-permute-start | bytes 786440 | tf_op jit(solution)/shard_map/ppermute | solution.py:15
  5.8 20.7 %collective-permute-start = (bf16[128,1024]{1,0:T(8,128)(2,1)}, bf16[128,1024]{1,0:T(8,128)(2,1)S(1)}, u32[]{:S(2)}, u32[]{:S(2)}) collective-permute-start(bf16[128,1024]{1,0:T(8,128)(2,1)} %x_ref.3), channel_id=1, source_target_pairs={{0,4},{4,0},{8,12},{12,8},{1,5},{5,1},{9,13},{13,9},{2,6},{6,2},{1... | collective-permute-start | bytes 786440 | tf_op jit(solution)/shard_map/ppermute | solution.py:15
  6.7 16.4 %collective-permute-start.3 = (bf16[192,512]{1,0:T(8,128)(2,1)S(1)}, bf16[192,512]{1,0:T(8,128)(2,1)S(1)}, u32[]{:S(2)}, u32[]{:S(2)}) collective-permute-start(bf16[192,512]{1,0:T(8,128)(2,1)S(1)} %constant_dynamic-slice_fusion), channel_id=1, source_target_pairs={{0,12},{4,8},{8,4},{12,0},{1,13},{5,9},{9,5},{13,1},{2,14},{6,10},... | collective-permute-start | bytes 589832 | tf_op jit(solution)/shard_map/ppermute | solution.py:15
  7.7 18.7 %collective-permute-start.2 = (bf16[192,512]{1,0:T(8,128)(2,1)S(1)}, bf16[192,512]{1,0:T(8,128)(2,1)S(1)}, u32[]{:S(2)}, u32[]{:S(2)}) collective-permute-start(bf16[192,512]{1,0:T(8,128)(2,1)S(1)} %constant_dynamic-slice_fusion), channel_id=1, source_target_pairs={{0,4},{4,0},{8,12},{12,8},{1,5},{5,1},{9,13},{13,9},{2,6},{6,2},{1... | collective-permute-start | bytes 589832 | tf_op jit(solution)/shard_map/ppermute | solution.py:15
  26.4 14.9 %collective-permute-start.4 = (bf16[128,1024]{1,0:T(8,128)(2,1)S(1)}, bf16[128,1024]{1,0:T(8,128)(2,1)S(1)}, u32[]{:S(2)}, u32[]{:S(2)}) collective-permute-start(bf16[128,1024]{1,0:T(8,128)(2,1)S(1)} %collective-permute-done.1.x_ref), channel_id=1, source_target_pairs={{0,4},{4,0},{8,12},{12,8},{1,5},{5,1},{9,13},{13,9},{2,6},{6,2},{1... | collective-permute-start | bytes 786440 | tf_op jit(solution)/shard_map/ppermute | solution.py:15
  28.8 3.5 %collective-permute-start.7 = (bf16[3,64,192]{2,1,0:T(8,128)(2,1)S(1)}, bf16[3,64,192]{2,1,0:T(8,128)(2,1)S(1)}, u32[]{:S(2)}, u32[]{:S(2)}) collective-permute-start(bf16[3,64,192]{2,1,0:T(8,128)(2,1)S(1)} %pad_maximum_fusion), channel_id=1, source_target_pairs={{0,1},{1,0},{2,3},{3,2},{4,5},{5,4},{6,7},{7,6},{8,9},{9,8},{10,11... | collective-permute-start | bytes 221192 | tf_op jit(solution)/shard_map/ppermute | solution.py:15
  29.9 7.8 %collective-permute-start.9 = (bf16[192,512]{1,0:T(8,128)(2,1)S(1)}, bf16[192,512]{1,0:T(8,128)(2,1)S(1)}, u32[]{:S(2)}, u32[]{:S(2)}) collective-permute-start(bf16[192,512]{1,0:T(8,128)(2,1)S(1)} %collective-permute-done.3.refs_1_), channel_id=1, source_target_pairs={{0,16},{16,0},{1,17},{17,1},{2,18},{18,2},{3,19},{19,3},{4,20},{20... | collective-permute-start | bytes 589832 | tf_op jit(solution)/shard_map/ppermute | solution.py:15
  31.5 7.4 %collective-permute-start.5 = (bf16[192,512]{1,0:T(8,128)(2,1)S(1)}, bf16[192,512]{1,0:T(8,128)(2,1)S(1)}, u32[]{:S(2)}, u32[]{:S(2)}) collective-permute-start(bf16[192,512]{1,0:T(8,128)(2,1)S(1)} %collective-permute-done.3.refs_1_), channel_id=1, source_target_pairs={{0,4},{4,0},{8,12},{12,8},{1,5},{5,1},{9,13},{13,9},{2,6},{6,2},{1... | collective-permute-start | bytes 589832 | tf_op jit(solution)/shard_map/ppermute | solution.py:15
  31.8 9.5 %collective-permute-start.8 = (bf16[192,512]{1,0:T(8,128)(2,1)S(1)}, bf16[192,512]{1,0:T(8,128)(2,1)S(1)}, u32[]{:S(2)}, u32[]{:S(2)}) collective-permute-start(bf16[192,512]{1,0:T(8,128)(2,1)S(1)} %collective-permute-done.2.refs_0_), channel_id=1, source_target_pairs={{0,16},{16,0},{1,17},{17,1},{2,18},{18,2},{3,19},{19,3},{4,20},{20... | collective-permute-start | bytes 589832 | tf_op jit(solution)/shard_map/ppermute | solution.py:15
  43.0 5.5 %collective-permute-start.11 = (bf16[4,64,192]{2,1,0:T(8,128)(2,1)S(1)}, bf16[4,64,192]{2,1,0:T(8,128)(2,1)S(1)}, u32[]{:S(2)}, u32[]{:S(2)}) collective-permute-start(bf16[4,64,192]{2,1,0:T(8,128)(2,1)S(1)} %fusion.1), channel_id=1, source_target_pairs={{0,3},{1,2},{2,1},{3,0},{4,7},{5,6},{6,5},{7,4},{8,11},{9,10},{10,... | collective-permute-start | bytes 294920 | tf_op jit(solution)/shard_map/ppermute | solution.py:15
  44.3 7.2 %collective-permute-start.12 = (bf16[192,512]{1,0:T(8,128)(2,1)S(1)}, bf16[192,512]{1,0:T(8,128)(2,1)S(1)}, u32[]{:S(2)}, u32[]{:S(2)}) collective-permute-start(bf16[192,512]{1,0:T(8,128)(2,1)S(1)} %collective-permute-done.5.refs_2_), channel_id=1, source_target_pairs={{0,16},{16,0},{1,17},{17,1},{2,18},{18,2},{3,19},{19,3},{4,20},{20... | collective-permute-start | bytes 589832 | tf_op jit(solution)/shard_map/ppermute | solution.py:15
  51.4 6.3 %collective-permute-start.13 = (bf16[64,192]{1,0:T(8,128)(2,1)S(1)}, bf16[64,192]{1,0:T(8,128)(2,1)S(1)}, u32[]{:S(2)}, u32[]{:S(2)}) collective-permute-start(bf16[64,192]{1,0:T(8,128)(2,1)S(1)} %get-tuple-element.98), channel_id=1, source_target_pairs={{0,5},{1,4},{2,7},{3,6},{4,1},{5,0},{6,3},{7,2},{8,13},{9,12},{10,... | collective-permute-start | bytes 73736 | tf_op jit(solution)/shard_map/ppermute | solution.py:23
  51.5 6.2 %collective-permute-start.15 = (bf16[64,192]{1,0:T(8,128)(2,1)S(1)}, bf16[64,192]{1,0:T(8,128)(2,1)S(1)}, u32[]{:S(2)}, u32[]{:S(2)}) collective-permute-start(bf16[64,192]{1,0:T(8,128)(2,1)S(1)} %get-tuple-element.99), channel_id=1, source_target_pairs={{0,9},{1,8},{2,11},{3,10},{4,13},{5,12},{6,15},{7,14},{8,1},{9,0},... | collective-permute-start | bytes 73736 | tf_op jit(solution)/shard_map/ppermute | solution.py:23
  52.2 5.6 %collective-permute-start.14 = (bf16[64,192]{1,0:T(8,128)(2,1)S(1)}, bf16[64,192]{1,0:T(8,128)(2,1)S(1)}, u32[]{:S(2)}, u32[]{:S(2)}) collective-permute-start(bf16[64,192]{1,0:T(8,128)(2,1)S(1)} %get-tuple-element.100), channel_id=1, source_target_pairs={{0,13},{1,12},{2,15},{3,14},{4,9},{5,8},{6,11},{7,10},{8,5},{9,4},... | collective-permute-start | bytes 73736 | tf_op jit(solution)/shard_map/ppermute | solution.py:23
  62.3 5.4 %collective-permute-start.20 = (bf16[4,64,192]{2,1,0:T(8,128)(2,1)S(1)}, bf16[4,64,192]{2,1,0:T(8,128)(2,1)S(1)}, u32[]{:S(2)}, u32[]{:S(2)}) collective-permute-start(bf16[4,64,192]{2,1,0:T(8,128)(2,1)S(1)} %fusion), channel_id=1, source_target_pairs={{0,3},{1,2},{2,1},{3,0},{4,7},{5,6},{6,5},{7,4},{8,11},{9,10},{10,... | collective-permute-start | bytes 294920 | tf_op jit(solution)/shard_map/ppermute | solution.py:15
  62.9 23.0 %collective-permute-start.28 = (bf16[128,1024]{1,0:T(8,128)(2,1)S(1)}, bf16[128,1024]{1,0:T(8,128)(2,1)S(1)}, u32[]{:S(2)}, u32[]{:S(2)}) collective-permute-start(bf16[128,1024]{1,0:T(8,128)(2,1)S(1)} %get-tuple-element.75.res_ref.refs_0_), channel_id=1, source_target_pairs={{0,4},{4,0},{8,12},{12,8},{1,5},{5,1},{9,13},{13,9},{2,6},{6,2},{1... | collective-permute-start | bytes 786440 | tf_op jit(solution)/shard_map/ppermute | solution.py:15
  63.0 16.8 %collective-permute-start.21 = (bf16[128,1024]{1,0:T(8,128)(2,1)S(1)}, bf16[128,1024]{1,0:T(8,128)(2,1)S(1)}, u32[]{:S(2)}, u32[]{:S(2)}) collective-permute-start(bf16[128,1024]{1,0:T(8,128)(2,1)S(1)} %get-tuple-element.75.res_ref.refs_0_), channel_id=1, source_target_pairs={{0,12},{4,8},{8,4},{12,0},{1,13},{5,9},{9,5},{13,1},{2,14},{6,10},... | collective-permute-start | bytes 786440 | tf_op jit(solution)/shard_map/ppermute | solution.py:15
  67.8 8.2 %collective-permute-start.22 = (bf16[64,192]{1,0:T(8,128)(2,1)S(1)}, bf16[64,192]{1,0:T(8,128)(2,1)S(1)}, u32[]{:S(2)}, u32[]{:S(2)}) collective-permute-start(bf16[64,192]{1,0:T(8,128)(2,1)S(1)} %get-tuple-element.94), channel_id=1, source_target_pairs={{0,5},{1,4},{2,7},{3,6},{4,1},{5,0},{6,3},{7,2},{8,13},{9,12},{10,... | collective-permute-start | bytes 73736 | tf_op jit(solution)/shard_map/ppermute | solution.py:23
  68.4 11.3 %collective-permute-start.24 = (bf16[64,192]{1,0:T(8,128)(2,1)S(1)}, bf16[64,192]{1,0:T(8,128)(2,1)S(1)}, u32[]{:S(2)}, u32[]{:S(2)}) collective-permute-start(bf16[64,192]{1,0:T(8,128)(2,1)S(1)} %get-tuple-element.95), channel_id=1, source_target_pairs={{0,9},{1,8},{2,11},{3,10},{4,13},{5,12},{6,15},{7,14},{8,1},{9,0},... | collective-permute-start | bytes 73736 | tf_op jit(solution)/shard_map/ppermute | solution.py:23
  70.7 9.1 %collective-permute-start.23 = (bf16[64,192]{1,0:T(8,128)(2,1)S(1)}, bf16[64,192]{1,0:T(8,128)(2,1)S(1)}, u32[]{:S(2)}, u32[]{:S(2)}) collective-permute-start(bf16[64,192]{1,0:T(8,128)(2,1)S(1)} %get-tuple-element.96), channel_id=1, source_target_pairs={{0,13},{1,12},{2,15},{3,14},{4,9},{5,8},{6,11},{7,10},{8,5},{9,4},... | collective-permute-start | bytes 73736 | tf_op jit(solution)/shard_map/ppermute | solution.py:23
  76.0 3.7 %collective-permute-start.25 = (bf16[1,64,192]{2,1,0:T(8,128)(2,1)S(1)}, bf16[1,64,192]{2,1,0:T(8,128)(2,1)S(1)}, u32[]{:S(2)}, u32[]{:S(2)}) collective-permute-start(bf16[1,64,192]{2,1,0:T(8,128)(2,1)S(1)} %get-tuple-element.97.s_ref), channel_id=1, source_target_pairs={{0,1},{1,0},{2,3},{3,2},{4,5},{5,4},{6,7},{7,6},{8,9},{9,8},{10,11... | collective-permute-start | bytes 73736 | tf_op jit(solution)/shard_map/ppermute | solution.py:15
  82.2 3.6 %collective-permute-start.27 = (f32[1,1024]{1,0:T(1,128)S(1)}, f32[1,1024]{1,0:T(1,128)S(1)}, u32[]{:S(2)}, u32[]{:S(2)}) collective-permute-start(f32[1,1024]{1,0:T(1,128)S(1)} %get-tuple-element.87), channel_id=1, source_target_pairs={{0,4},{4,0},{8,12},{12,8},{1,5},{5,1},{9,13},{13,9},{2,6},{6,2},{1... | collective-permute-start | bytes 12296 | tf_op jit(solution)/shard_map/ppermute | solution.py:15
  85.9 7.6 %collective-permute-start.29 = (bf16[128,1024]{1,0:T(8,128)(2,1)S(1)}, bf16[128,1024]{1,0:T(8,128)(2,1)S(1)}, u32[]{:S(2)}, u32[]{:S(2)}) collective-permute-start(bf16[128,1024]{1,0:T(8,128)(2,1)S(1)} %collective-permute-done.21.refs_2_), channel_id=1, source_target_pairs={{0,4},{4,0},{8,12},{12,8},{1,5},{5,1},{9,13},{13,9},{2,6},{6,2},{1... | collective-permute-start | bytes 786440 | tf_op jit(solution)/shard_map/ppermute | solution.py:15
  87.0 4.9 %collective-permute-start.30 = (f32[1,1024]{1,0:T(1,128)S(1)}, f32[1,1024]{1,0:T(1,128)S(1)}, u32[]{:S(2)}, u32[]{:S(2)}) collective-permute-start(f32[1,1024]{1,0:T(1,128)S(1)} %add.53.refs_1_), channel_id=1, source_target_pairs={{0,8},{4,12},{8,0},{12,4},{1,9},{5,13},{9,1},{13,5},{2,10},{6,14},... | collective-permute-start | bytes 12296 | tf_op jit(solution)/shard_map/ppermute | solution.py:15
  (14 other events, 34.3 us)

commit v4 on v0

v4 whole, which is shorter than its diff:
```python
import jax
import jax.numpy as jnp
from jax import lax
from jax.experimental import pallas as pl
from jax.experimental.pallas import tpu as pltpu
from jax.sharding import PartitionSpec as P

sparsity_coef = 3.0
f32 = jnp.float32
bf16 = jnp.bfloat16


def swap(value, axis, distance):
    count = lax.axis_size(axis)
    return lax.ppermute(value, axis, [(i, i ^ distance) for i in range(count)])


def after(value, *earlier):
    return lax.optimization_barrier((value, *earlier))[0]


def stage(*values):
    return lax.optimization_barrier(values)


def width_sum(part):
    total, step = part.astype(f32), 1
    while step < lax.axis_size("width"):
        sent = lax.reduce_precision(total, 8, 7)
        total = sent + swap(sent.astype(bf16), "width", 2 * step - 1).astype(f32)
        step *= 2
    return total


def plain_sum(value, axis):
    step = 1
    while step < lax.axis_size(axis):
        value = value + swap(value, axis, step)
        step *= 2
    return value


def mm(a, b, contract):
    return lax.dot_general(a, b, ((contract[:1], contract[1:]), ((), ())), preferred_element_type=f32)


VMEM = pl.BlockSpec(memory_space=pltpu.VMEM)


def call(kernel, name, outs, *operands):
    return pl.pallas_call(
        kernel,
        out_shape=[jax.ShapeDtypeStruct(shape, kind) for shape, kind in outs],
        in_specs=[VMEM] * len(operands),
        out_specs=[VMEM] * len(outs),
        cost_estimate=pl.CostEstimate(flops=10**6, bytes_accessed=10**6, transcendentals=0),
        compiler_params=pltpu.CompilerParams(vmem_limit_bytes=24 * 2**20),
        name=name,
    )(*operands)


def part_of(x, b_dec, w_enc_t):
    def kernel(x_ref, b_ref, w_ref, centered_ref, part_ref):
        centered_ref[...] = (x_ref[...].astype(f32) - b_ref[...]).astype(bf16)
        part_ref[...] = mm(centered_ref[...], w_ref[...], (1, 1)).astype(bf16)

    outs = [(x.shape, bf16), ((x.shape[0], w_enc_t.shape[0]), bf16)]
    return call(kernel, "part_of", outs, x, b_dec[None], w_enc_t)


def recon_of(codes, w_dec, *sums):
    def kernel(c_ref, w_ref, *refs):
        value = mm(c_ref[...], w_ref[...], (1, 0))
        for ref in refs[:-1]:
            value = value + ref[...].astype(f32)
        refs[-1][...] = value.astype(bf16)

    outs = [((codes.shape[0], w_dec.shape[1]), bf16)]
    return call(kernel, "recon_of", outs, codes, w_dec, *sums)[0]


def res_of(scale, x, rest, b_dec, codes, w_dec, sums):
    def kernel(x_ref, r_ref, b_ref, c_ref, w_ref, *refs):
        value = r_ref[...].astype(f32) + b_ref[...] - x_ref[...].astype(f32)
        value = value + mm(c_ref[...], w_ref[...], (1, 0))
        for ref in refs[:-2]:
            value = value + ref[...].astype(f32)
        res_ref, part_ref = refs[-2:]
        res_ref[...] = (scale * value).astype(bf16)
        part_ref[...] = mm(res_ref[...], w_ref[...], (1, 1)).astype(bf16)

    outs = [(x.shape, bf16), (codes.shape, bf16)]
    return call(kernel, "res_of", outs, x, rest, b_dec[None], codes, w_dec, *sums)


def code_part(res, w_dec):
    def kernel(r_ref, w_ref, out):
        out[...] = mm(r_ref[...], w_ref[...], (1, 1)).astype(bf16)

    return call(kernel, "code_part", [((res.shape[0], w_dec.shape[0]), bf16)], res, w_dec)[0]


def dec_add(total, codes, res, *shares):
    count = len(res)

    def kernel(total_ref, *refs):
        value = sum(mm(refs[k][...], refs[count + k][...], (0, 0)) for k in range(count))
        refs[2 * count + len(shares)][...] = total_ref[...] + value
        if shares:
            refs[-1][...] = refs[2 * count][...] + refs[2 * count + 1][...]

    outs = [(total.shape, f32)] + [(s.shape, f32) for s in shares[:1]]
    return call(kernel, "dec_add", outs, total, *codes, *res, *shares)


def pre_grads(codes, sums, threshold, w_enc_t, res):
    count = len(codes)

    def kernel(n_ref, w_ref, res_ref, *refs):
        c, s = refs[:count], refs[count : 2 * count]
        out, bias, share = refs[2 * count :]
        total = 0.0
        for k in range(count):
            g = jnp.where(c[k][...].astype(f32) > 0, s[k][...] + n_ref[...], 0.0)
            out[k] = g.astype(bf16)
            total = total + jnp.sum(out[k].astype(f32), axis=0, keepdims=True)
        bias[...] = total
        high = total.astype(bf16)
        rest = total - high.astype(f32)
        mid = rest.astype(bf16)
        low = (rest - mid.astype(f32)).astype(bf16)
        row = lax.broadcasted_iota(jnp.int32, (8, total.shape[1]), 0)
        pieces = jnp.where(row == 0, high.astype(f32), jnp.where(row == 1, mid.astype(f32), 0.0))
        pieces = jnp.where(row == 2, low.astype(f32), pieces).astype(bf16)
        product = jnp.sum(mm(pieces, w_ref[...], (1, 0)), axis=0, keepdims=True)
        share[...] = jnp.sum(res_ref[...].astype(f32), axis=0, keepdims=True) - product

    lat, cols = w_enc_t.shape
    outs = [((count, *codes[0].shape), bf16), ((1, lat), f32), ((1, cols), f32)]
    grads, bias, share = call(
        kernel, "pre_grads", outs, threshold[None], w_enc_t, res, *codes, *sums
    )
    return grads, bias[0], share


def enc_end(centered, grads):
    count = len(centered)

    def kernel(g_ref, *refs):
        refs[-1][...] = sum(mm(g_ref[k], refs[k][...], (0, 0)) for k in range(count))

    outs = [((grads.shape[2], centered[0].shape[1]), f32)]
    return call(kernel, "enc_end", outs, grads, *centered)[0]


def square_sums(w_dec):
    dec_float = w_dec.astype(f32)
    value, step = jnp.sum(dec_float * dec_float, axis=1), 1
    while step < lax.axis_size("width"):
        value = value + swap(value, "width", 2 * step - 1)
        step *= 2
    return value


def shards(activations, rest_recon, w_enc, b_enc, w_dec, b_dec):
    count = lax.axis_size("lat")
    line = count == 4
    others = range(1, count)
    row_scale = float((activations.shape[0] * count) ** -0.5)
    w_enc_t = w_enc.T

    def lat_swap(block, distance):
        return swap(block, "lat", distance)

    xs = [activations] + [lat_swap(activations, k) if k != 2 or not line else None for k in others]
    centered, parts, codes = [None] * count, [None] * count, [None] * count

    def add_parts(blocks):
        for k in blocks:
            centered[k], parts[k] = part_of(xs[k], b_dec, w_enc_t)

    def add_codes(blocks, total):
        for i, k in enumerate(blocks):
            codes[k] = jnp.maximum(total[i] + b_enc, 0.0).astype(bf16)

    def sum_parts(blocks):
        return width_sum(jnp.stack([parts[k] for k in blocks]))

    add_parts([0])
    if line:
        xs[1], xs[3], centered[0], parts[0] = stage(xs[1], xs[3], centered[0], parts[0])
        xs[2] = lat_swap(xs[3], 1)
        add_parts([1, 3])
        xs[2], total = stage(xs[2], sum_parts([3]))
        add_codes([3], total)
        passed = lat_swap(recon_of(codes[3], w_dec), 1)
        add_parts([2])
        passed, total = stage(passed, sum_parts([0, 1, 2]))
        add_codes([0, 1, 2], total)
        sums = [
            lat_swap(recon_of(codes[1], w_dec), 1),
            lat_swap(recon_of(codes[2], w_dec, passed), 2),
        ]
    else:
        add_parts(others)
        add_codes(range(count), sum_parts(range(count)))
        sums = [lat_swap(recon_of(codes[k], w_dec), k) for k in others]
    res_grad, part = res_of(
        2.0 * row_scale, activations, rest_recon, b_dec, codes[0], w_dec, sums
    )

    res = [res_grad] + [lat_swap(res_grad, k) if k != 3 or not line else None for k in others]
    if line:
        res[1], res[2] = stage(res[1], res[2])
        res[3] = lat_swap(res[2], 1)
    parts = [part] + [code_part(res[k], w_dec) for k in others]
    early = width_sum(jnp.stack(parts[:-1]))
    code_sums = [early[k] for k in range(count - 1)] + [width_sum(parts[-1])]
    squares = square_sums(after(w_dec, xs[1]))
    norms = jnp.sqrt(squares + 1e-06)
    grads, grad_benc, share = pre_grads(
        codes, code_sums, sparsity_coef * row_scale * norms, w_enc_t, res_grad
    )
    step = 1
    while 2 * step < count:
        share = share + lat_swap(share, step)
        step *= 2
    grad_enc = enc_end(centered, grads).T
    code_total = sum(jnp.sum(c.astype(f32), axis=0) for c in codes)
    sparsity = (sparsity_coef * row_scale * code_total / norms)[:, None] * w_dec.astype(f32)
    (grad_dec,) = dec_add(sparsity, codes, res)
    grad_bdec = share + lat_swap(share, step)
    return (grad_enc, grad_benc, grad_dec, grad_bdec[0])


def solution(mesh):
    placed = (
        P(("groups", "lat"), "width"),
        P(("groups", "lat"), "width"),
        P("width", "lat"),
        P("lat"),
        P("lat", "width"),
        P("width"),
    )
    return jax.shard_map(
        shards,
        mesh=mesh,
        in_specs=placed,
        out_specs=(
            P(("groups", "width"), "lat"),
            P(("groups", "lat")),
            P(("groups", "lat"), "width"),
            P(("groups", "width")),
        ),
        check_vma=False,
    )
```

time: 192 us -> 93.4 us (0.49)
  waiting for transfers between devices: 142 us -> 61.5 us
  starting transfers between devices: 0.21 us -> 19.8 us
  blocking collectives: 18.1 us -> 0 us
  between operations: 13.8 us -> 0.89 us
  matrix products: 11.2 us -> 0 us
  Pallas kernels: 0 us -> 6.78 us
  other arithmetic: 5.72 us -> 1.47 us
  local copies, waits for them, and re-layouts: 0.05 us -> 2.68 us
    psum x2 -> x0, waiting for transfers between devices: 62.8 us -> none  [the longest x1 31.6 us: shards(): lax.psum(pre_part.astype(jnp.bfloat16), 'width').astype(jnp.float32)]
    ppermute x0 -> x21, waiting for transfers between devices: none -> 61.5 us  [swap(): return lax.ppermute(value, axis, [(i, i ^ distance) for i in range(count)])]
    all_gather x2 -> x0, waiting for transfers between devices: 51.9 us -> none  [the longest x1 31.8 us: shards(): gathered = lax.all_gather(centered, 'lat', axis=0, tiled=True)]
    reduce_scatter x1 -> x0, waiting for transfers between devices: 27.2 us -> none  [shards(): lax.psum_scatter(jnp.dot(codes, w_dec, preferred_element_type=jnp.float32...]
    ppermute x0 -> x21, starting transfers between devices: none -> 19.8 us  [swap(): return lax.ppermute(value, axis, [(i, i ^ distance) for i in range(count)])]
    psum x2 -> x0, blocking collectives: 18.1 us -> none  [the longest x1 11.7 us: shards(): enc_total = lax.psum(enc_term, 'lat')]
    dot_general x6 -> x0, matrix products: 11.2 us -> none  [the longest x1 2.51 us: shards(): jnp.dot(codes, w_dec, preferred_element_type=jnp.float32)]
    pallas_call x0 -> x14, Pallas kernels: none -> 6.78 us  [call(): pl.pallas_call(kernel, out_shape=[jax.ShapeDtypeStruct(shape, kind) for s...]
  transfers between devices with their start and end apart: 5 -> 21, of which waited for: 5 -> 19; matrix products, arithmetic and copies ran while one was open for 0% -> 1% of each run, Pallas kernels for 0% -> 5%
where the time goes in v4:
time: 93.4 us; the launch traced here: 93.2 us
  waiting for transfers between devices  61.5 us (66%)
  starting transfers between devices  19.8 us (21%)
  Pallas kernels  6.78 us (7%)
  local copies, waits for them, and re-layouts  2.68 us (3%)
  other arithmetic  1.47 us (2%)
    ppermute x21, waiting for transfers between devices, swap(): return lax.ppermute(value, axis, [(i, i ^ distance) for i in range(count)])  61.5 us
    ppermute x21, starting transfers between devices, swap(): return lax.ppermute(value, axis, [(i, i ^ distance) for i in range(count)])  19.8 us
    pallas_call x14, Pallas kernels, call(): pl.pallas_call(kernel, out_shape=[jax.ShapeDtypeStruct(shape, kind) for s...  6.78 us
    unnamed x16, local copies, waits for them, and re-layouts  2.66 us
  transfers between devices with their start and end apart: 21, of which 19 were waited for; matrix products, arithmetic and copies ran while one was open for 1% of the time, Pallas kernels for 5%

profile of v4, /device:TPU:0, one launch (start us, length us, event | category | flops | bytes accessed | tf_op | source)
XLA Modules:
  0.0 93.2 jit_solution(17250451206473912429)
XLA Ops:
  0.6 5.1 %collective-permute-start.1 = (bf16[128,1024]{1,0:T(8,128)(2,1)}, bf16[128,1024]{1,0:T(8,128)(2,1)S(1)}, u32[]{:S(2)}, u32[]{:S(2)}) collective-permute-start(bf16[128,1024]{1,0:T(8,128)(2,1)} %x_ref.3), channel_id=1, source_target_pairs={{0,12},{4,8},{8,4},{12,0},{1,13},{5,9},{9,5},{13,1},{2,14},{6,10},... | collective-permute-start | bytes 786440 | tf_op jit(solution)/shard_map/ppermute | solution.py:15
  8.7 4.5 %collective-permute-done.1.x_ref = bf16[128,1024]{1,0:T(8,128)(2,1)S(1)} collective-permute-done((bf16[128,1024]{1,0:T(8,128)(2,1)}, bf16[128,1024]{1,0:T(8,128)(2,1)S(1)}, u32[]{:S(2)}, u32[]{:S(2)}) %collective-permute-start.1) | collective-permute-done | bytes 262176 | tf_op jit(solution)/shard_map/ppermute | solution.py:15
  13.2 4.8 %collective-permute-done.x_ref = bf16[128,1024]{1,0:T(8,128)(2,1)S(1)} collective-permute-done((bf16[128,1024]{1,0:T(8,128)(2,1)}, bf16[128,1024]{1,0:T(8,128)(2,1)S(1)}, u32[]{:S(2)}, u32[]{:S(2)}) %collective-permute-start) | collective-permute-done | bytes 262176 | tf_op jit(solution)/shard_map/ppermute | solution.py:15
  21.0 1.7 %collective-permute-start.4 = (bf16[128,1024]{1,0:T(8,128)(2,1)S(1)}, bf16[128,1024]{1,0:T(8,128)(2,1)S(1)}, u32[]{:S(2)}, u32[]{:S(2)}) collective-permute-start(bf16[128,1024]{1,0:T(8,128)(2,1)S(1)} %collective-permute-done.1.x_ref), channel_id=1, source_target_pairs={{0,4},{4,0},{8,12},{12,8},{1,5},{5,1},{9,13},{13,9},{2,6},{6,2},{1... | collective-permute-start | bytes 786440 | tf_op jit(solution)/shard_map/ppermute | solution.py:15
  23.8 5.7 %collective-permute-done.4.x_ref = bf16[128,1024]{1,0:T(8,128)(2,1)S(1)} collective-permute-done((bf16[128,1024]{1,0:T(8,128)(2,1)S(1)}, bf16[128,1024]{1,0:T(8,128)(2,1)S(1)}, u32[]{:S(2)}, u32[]{:S(2)}) %collective-permute-start.4) | collective-permute-done | bytes 262176 | tf_op jit(solution)/shard_map/ppermute | solution.py:15
  30.0 1.4 %collective-permute-done.8 = bf16[3,128,192]{2,1,0:T(8,128)(2,1)S(1)} collective-permute-done((bf16[3,128,192]{2,1,0:T(8,128)(2,1)S(1)}, bf16[3,128,192]{2,1,0:T(8,128)(2,1)S(1)}, u32[]{:S(2)}, u32[]{:S(2)}) %collective-permute-start.8) | collective-permute-done | bytes 147488 | tf_op jit(solution)/shard_map/ppermute | solution.py:15
  32.1 1.8 %collective-permute-start.7 = (bf16[128,1024]{1,0:T(8,128)(2,1)S(1)}, bf16[128,1024]{1,0:T(8,128)(2,1)S(1)}, u32[]{:S(2)}, u32[]{:S(2)}) collective-permute-start(bf16[128,1024]{1,0:T(8,128)(2,1)S(1)} %recon_of.3), channel_id=1, source_target_pairs={{0,4},{4,0},{8,12},{12,8},{1,5},{5,1},{9,13},{13,9},{2,6},{6,2},{1... | collective-permute-start | bytes 786440 | tf_op jit(solution)/shard_map/ppermute | solution.py:15
  33.8 4.6 %collective-permute-done.9 = bf16[3,128,192]{2,1,0:T(8,128)(2,1)S(1)} collective-permute-done((bf16[3,128,192]{2,1,0:T(8,128)(2,1)S(1)}, bf16[3,128,192]{2,1,0:T(8,128)(2,1)S(1)}, u32[]{:S(2)}, u32[]{:S(2)}) %collective-permute-start.9) | collective-permute-done | bytes 147488 | tf_op jit(solution)/shard_map/ppermute | solution.py:15
  38.5 2.2 %collective-permute-done.7.refs_0_ = bf16[128,1024]{1,0:T(8,128)(2,1)S(1)} collective-permute-done((bf16[128,1024]{1,0:T(8,128)(2,1)S(1)}, bf16[128,1024]{1,0:T(8,128)(2,1)S(1)}, u32[]{:S(2)}, u32[]{:S(2)}) %collective-permute-start.7) | collective-permute-done | bytes 262176 | tf_op jit(solution)/shard_map/ppermute | solution.py:15
  41.0 1.7 %collective-permute-start.10 = (bf16[128,1024]{1,0:T(8,128)(2,1)S(1)}, bf16[128,1024]{1,0:T(8,128)(2,1)S(1)}, u32[]{:S(2)}, u32[]{:S(2)}) collective-permute-start(bf16[128,1024]{1,0:T(8,128)(2,1)S(1)} %recon_of.4), channel_id=1, source_target_pairs={{0,4},{4,0},{8,12},{12,8},{1,5},{5,1},{9,13},{13,9},{2,6},{6,2},{1... | collective-permute-start | bytes 786440 | tf_op jit(solution)/shard_map/ppermute | solution.py:15
  43.6 8.3 %collective-permute-done.10.refs_0_ = bf16[128,1024]{1,0:T(8,128)(2,1)S(1)} collective-permute-done((bf16[128,1024]{1,0:T(8,128)(2,1)S(1)}, bf16[128,1024]{1,0:T(8,128)(2,1)S(1)}, u32[]{:S(2)}, u32[]{:S(2)}) %collective-permute-start.10) | collective-permute-done | bytes 262176 | tf_op jit(solution)/shard_map/ppermute | solution.py:15
  52.0 5.1 %collective-permute-done.11.refs_1_ = bf16[128,1024]{1,0:T(8,128)(2,1)S(1)} collective-permute-done((bf16[128,1024]{1,0:T(8,128)(2,1)S(1)}, bf16[128,1024]{1,0:T(8,128)(2,1)S(1)}, u32[]{:S(2)}, u32[]{:S(2)}) %collective-permute-start.11) | collective-permute-done | bytes 262176 | tf_op jit(solution)/shard_map/ppermute | solution.py:15
  60.4 8.2 %collective-permute-done.13.r_ref.refs_6_ = bf16[128,1024]{1,0:T(8,128)(2,1)S(1)} collective-permute-done((bf16[128,1024]{1,0:T(8,128)(2,1)S(1)}, bf16[128,1024]{1,0:T(8,128)(2,1)S(1)}, u32[]{:S(2)}, u32[]{:S(2)}) %collective-permute-start.13) | collective-permute-done | bytes 262176 | tf_op jit(solution)/shard_map/ppermute | solution.py:15
  68.6 1.4 %collective-permute-done.12.r_ref.refs_5_ = bf16[128,1024]{1,0:T(8,128)(2,1)S(1)} collective-permute-done((bf16[128,1024]{1,0:T(8,128)(2,1)S(1)}, bf16[128,1024]{1,0:T(8,128)(2,1)S(1)}, u32[]{:S(2)}, u32[]{:S(2)}) %collective-permute-start.12) | collective-permute-done | bytes 262176 | tf_op jit(solution)/shard_map/ppermute | solution.py:15
  71.0 1.4 %collective-permute-done.14 = bf16[3,128,192]{2,1,0:T(8,128)(2,1)S(1)} collective-permute-done((bf16[3,128,192]{2,1,0:T(8,128)(2,1)S(1)}, bf16[3,128,192]{2,1,0:T(8,128)(2,1)S(1)}, u32[]{:S(2)}, u32[]{:S(2)}) %collective-permute-start.14) | collective-permute-done | bytes 147488 | tf_op jit(solution)/shard_map/ppermute | solution.py:15
  72.4 1.3 %collective-permute-start.15 = (bf16[3,128,192]{2,1,0:T(8,128)(2,1)S(1)}, bf16[3,128,192]{2,1,0:T(8,128)(2,1)S(1)}, u32[]{:S(2)}, u32[]{:S(2)}) collective-permute-start(bf16[3,128,192]{2,1,0:T(8,128)(2,1)S(1)} %fusion.3), channel_id=1, source_target_pairs={{0,3},{1,2},{2,1},{3,0},{4,7},{5,6},{6,5},{7,4},{8,11},{9,10},{10,... | collective-permute-start | bytes 442376 | tf_op jit(solution)/shard_map/ppermute | solution.py:15
  73.7 2.9 %collective-permute-done.16.r_ref.refs_7_ = bf16[128,1024]{1,0:T(8,128)(2,1)S(1)} collective-permute-done((bf16[128,1024]{1,0:T(8,128)(2,1)S(1)}, bf16[128,1024]{1,0:T(8,128)(2,1)S(1)}, u32[]{:S(2)}, u32[]{:S(2)}) %collective-permute-start.16) | collective-permute-done | bytes 262176 | tf_op jit(solution)/shard_map/ppermute | solution.py:15
  77.0 2.3 %collective-permute-done.15 = bf16[3,128,192]{2,1,0:T(8,128)(2,1)S(1)} collective-permute-done((bf16[3,128,192]{2,1,0:T(8,128)(2,1)S(1)}, bf16[3,128,192]{2,1,0:T(8,128)(2,1)S(1)}, u32[]{:S(2)}, u32[]{:S(2)}) %collective-permute-start.15) | collective-permute-done | bytes 147488 | tf_op jit(solution)/shard_map/ppermute | solution.py:15
  79.5 1.3 %collective-permute-start.18 = (bf16[128,192]{1,0:T(8,128)(2,1)S(1)}, bf16[128,192]{1,0:T(8,128)(2,1)S(1)}, u32[]{:S(2)}, u32[]{:S(2)}) collective-permute-start(bf16[128,192]{1,0:T(8,128)(2,1)S(1)} %fusion.15), channel_id=1, source_target_pairs={{0,3},{1,2},{2,1},{3,0},{4,7},{5,6},{6,5},{7,4},{8,11},{9,10},{10,... | collective-permute-start | bytes 147464 | tf_op jit(solution)/shard_map/ppermute | solution.py:15
  80.9 2.8 %collective-permute-done.18 = bf16[128,192]{1,0:T(8,128)(2,1)S(1)} collective-permute-done((bf16[128,192]{1,0:T(8,128)(2,1)S(1)}, bf16[128,192]{1,0:T(8,128)(2,1)S(1)}, u32[]{:S(2)}, u32[]{:S(2)}) %collective-permute-start.18) | collective-permute-done | bytes 49184 | tf_op jit(solution)/shard_map/ppermute | solution.py:15
  84.5 1.8 %collective-permute-start.19 = (f32[1,1024]{1,0:T(1,128)S(1)}, f32[1,1024]{1,0:T(1,128)S(1)}, u32[]{:S(2)}, u32[]{:S(2)}) collective-permute-start(f32[1,1024]{1,0:T(1,128)S(1)} %get-tuple-element.51), channel_id=1, source_target_pairs={{0,4},{4,0},{8,12},{12,8},{1,5},{5,1},{9,13},{13,9},{2,6},{6,2},{1... | collective-permute-start | bytes 12296 | tf_op jit(solution)/shard_map/ppermute | solution.py:15
  86.2 1.8 %collective-permute-done.19 = f32[1,1024]{1,0:T(1,128)S(1)} collective-permute-done((f32[1,1024]{1,0:T(1,128)S(1)}, f32[1,1024]{1,0:T(1,128)S(1)}, u32[]{:S(2)}, u32[]{:S(2)}) %collective-permute-start.19) | collective-permute-done | bytes 4128 | tf_op jit(solution)/shard_map/ppermute | solution.py:15
  88.9 1.5 %dec_add.1 = f32[192,1024]{1,0:T(8,128)} custom-call(f32[192,1024]{1,0:T(8,128)S(1)} %convert_multiply_fusion.total_ref, bf16[128,192]{1,0:T(8,128)(2,1)S(1)} %get-tuple-element.61.c_ref.refs_0_, bf16[128,192]{1,0:T(8,128)(2,1)S(1)} %get-tuple-element.63.c_ref.refs_1_, bf16[128,192]{1,0:T(8,128)(2,1)S(1)} %get-tuple-element.57.c_ref.refs_2_, ...), custom_call_target="tpu_custom_call" | custom-call | flops 1000000 | bytes 1000000 | tf_op jit(solution)/shard_map/dec_add/pallas_call | solution.py:51
  90.3 1.5 %enc_end.1 = f32[192,1024]{1,0:T(8,128)} custom-call(bf16[4,128,192]{2,1,0:T(8,128)(2,1)S(1)} %get-tuple-element.45.g_ref, bf16[128,1024]{1,0:T(8,128)(2,1)S(1)} %get-tuple-element.46.refs_0_, bf16[128,1024]{1,0:T(8,128)(2,1)S(1)} %get-tuple-element.47.refs_1_, bf16[128,1024]{1,0:T(8,128)(2,1)S(1)} %get-tuple-element.48.refs_2_, ...), custom_call_target="tpu_custom_call" | custom-call | flops 1000000 | bytes 1000000 | tf_op jit(solution)/shard_map/enc_end/pallas_call | solution.py:51
  (69 shorter events, 17.1 us)
Async XLA Ops:
  0.6 12.6 %collective-permute-start.1 = (bf16[128,1024]{1,0:T(8,128)(2,1)}, bf16[128,1024]{1,0:T(8,128)(2,1)S(1)}, u32[]{:S(2)}, u32[]{:S(2)}) collective-permute-start(bf16[128,1024]{1,0:T(8,128)(2,1)} %x_ref.3), channel_id=1, source_target_pairs={{0,12},{4,8},{8,4},{12,0},{1,13},{5,9},{9,5},{13,1},{2,14},{6,10},... | collective-permute-start | bytes 786440 | tf_op jit(solution)/shard_map/ppermute | solution.py:15
  5.7 12.2 %collective-permute-start = (bf16[128,1024]{1,0:T(8,128)(2,1)}, bf16[128,1024]{1,0:T(8,128)(2,1)S(1)}, u32[]{:S(2)}, u32[]{:S(2)}) collective-permute-start(bf16[128,1024]{1,0:T(8,128)(2,1)} %x_ref.3), channel_id=1, source_target_pairs={{0,4},{4,0},{8,12},{12,8},{1,5},{5,1},{9,13},{13,9},{2,6},{6,2},{1... | collective-permute-start | bytes 786440 | tf_op jit(solution)/shard_map/ppermute | solution.py:15
  8.4 9.6 %copy-start.2 = (bf16[1024,192]{0,1:T(8,128)(2,1)S(1)}, bf16[1024,192]{0,1:T(8,128)(2,1)}, u32[]{:S(2)}) copy-start(bf16[1024,192]{0,1:T(8,128)(2,1)} %param.8) | copy-start | bytes 1179652
  18.3 1.3 %collective-permute-start.5 = (bf16[1,128,192]{2,1,0:T(8,128)(2,1)S(1)}, bf16[1,128,192]{2,1,0:T(8,128)(2,1)S(1)}, u32[]{:S(2)}, u32[]{:S(2)}) collective-permute-start(bf16[1,128,192]{2,1,0:T(8,128)(2,1)S(1)} %fusion.17), channel_id=1, source_target_pairs={{0,1},{1,0},{2,3},{3,2},{4,5},{5,4},{6,7},{7,6},{8,9},{9,8},{10,11... | collective-permute-start | bytes 147464 | tf_op jit(solution)/shard_map/ppermute | solution.py:15
  19.6 4.1 %collective-permute-start.6 = (bf16[1,128,192]{2,1,0:T(8,128)(2,1)S(1)}, bf16[1,128,192]{2,1,0:T(8,128)(2,1)S(1)}, u32[]{:S(2)}, u32[]{:S(2)}) collective-permute-start(bf16[1,128,192]{2,1,0:T(8,128)(2,1)S(1)} %fusion.16), channel_id=1, source_target_pairs={{0,3},{1,2},{2,1},{3,0},{4,7},{5,6},{6,5},{7,4},{8,11},{9,10},{10,... | collective-permute-start | bytes 147464 | tf_op jit(solution)/shard_map/ppermute | solution.py:15
  21.0 8.6 %collective-permute-start.4 = (bf16[128,1024]{1,0:T(8,128)(2,1)S(1)}, bf16[128,1024]{1,0:T(8,128)(2,1)S(1)}, u32[]{:S(2)}, u32[]{:S(2)}) collective-permute-start(bf16[128,1024]{1,0:T(8,128)(2,1)S(1)} %collective-permute-done.1.x_ref), channel_id=1, source_target_pairs={{0,4},{4,0},{8,12},{12,8},{1,5},{5,1},{9,13},{13,9},{2,6},{6,2},{1... | collective-permute-start | bytes 786440 | tf_op jit(solution)/shard_map/ppermute | solution.py:15
  29.9 1.5 %collective-permute-start.8 = (bf16[3,128,192]{2,1,0:T(8,128)(2,1)S(1)}, bf16[3,128,192]{2,1,0:T(8,128)(2,1)S(1)}, u32[]{:S(2)}, u32[]{:S(2)}) collective-permute-start(bf16[3,128,192]{2,1,0:T(8,128)(2,1)S(1)} %fusion.1), channel_id=1, source_target_pairs={{0,1},{1,0},{2,3},{3,2},{4,5},{5,4},{6,7},{7,6},{8,9},{9,8},{10,11... | collective-permute-start | bytes 442376 | tf_op jit(solution)/shard_map/ppermute | solution.py:15
  31.4 6.9 %collective-permute-start.9 = (bf16[3,128,192]{2,1,0:T(8,128)(2,1)S(1)}, bf16[3,128,192]{2,1,0:T(8,128)(2,1)S(1)}, u32[]{:S(2)}, u32[]{:S(2)}) collective-permute-start(bf16[3,128,192]{2,1,0:T(8,128)(2,1)S(1)} %fusion.2), channel_id=1, source_target_pairs={{0,3},{1,2},{2,1},{3,0},{4,7},{5,6},{6,5},{7,4},{8,11},{9,10},{10,... | collective-permute-start | bytes 442376 | tf_op jit(solution)/shard_map/ppermute | solution.py:15
  32.1 8.6 %collective-permute-start.7 = (bf16[128,1024]{1,0:T(8,128)(2,1)S(1)}, bf16[128,1024]{1,0:T(8,128)(2,1)S(1)}, u32[]{:S(2)}, u32[]{:S(2)}) collective-permute-start(bf16[128,1024]{1,0:T(8,128)(2,1)S(1)} %recon_of.3), channel_id=1, source_target_pairs={{0,4},{4,0},{8,12},{12,8},{1,5},{5,1},{9,13},{13,9},{2,6},{6,2},{1... | collective-permute-start | bytes 786440 | tf_op jit(solution)/shard_map/ppermute | solution.py:15
  41.0 11.0 %collective-permute-start.10 = (bf16[128,1024]{1,0:T(8,128)(2,1)S(1)}, bf16[128,1024]{1,0:T(8,128)(2,1)S(1)}, u32[]{:S(2)}, u32[]{:S(2)}) collective-permute-start(bf16[128,1024]{1,0:T(8,128)(2,1)S(1)} %recon_of.4), channel_id=1, source_target_pairs={{0,4},{4,0},{8,12},{12,8},{1,5},{5,1},{9,13},{13,9},{2,6},{6,2},{1... | collective-permute-start | bytes 786440 | tf_op jit(solution)/shard_map/ppermute | solution.py:15
  42.7 14.3 %copy-start.4 = (bf16[128,1024]{1,0:T(8,128)(2,1)S(1)}, bf16[128,1024]{1,0:T(8,128)(2,1)}, u32[]{:S(2)}) copy-start(bf16[128,1024]{1,0:T(8,128)(2,1)} %x_ref.3) | copy-start | bytes 786436
  42.7 14.3 %copy-start.5 = (bf16[128,1024]{1,0:T(8,128)(2,1)S(1)}, bf16[128,1024]{1,0:T(8,128)(2,1)}, u32[]{:S(2)}) copy-start(bf16[128,1024]{1,0:T(8,128)(2,1)} %r_ref.1) | copy-start | bytes 786436
  43.0 14.1 %collective-permute-start.11 = (bf16[128,1024]{1,0:T(8,128)(2,1)S(1)}, bf16[128,1024]{1,0:T(8,128)(2,1)S(1)}, u32[]{:S(2)}, u32[]{:S(2)}) collective-permute-start(bf16[128,1024]{1,0:T(8,128)(2,1)S(1)} %recon_of.5), channel_id=1, source_target_pairs={{0,8},{4,12},{8,0},{12,4},{1,9},{5,13},{9,1},{13,5},{2,10},{6,14},... | collective-permute-start | bytes 786440 | tf_op jit(solution)/shard_map/ppermute | solution.py:15
  57.5 11.0 %collective-permute-start.13 = (bf16[128,1024]{1,0:T(8,128)(2,1)S(1)}, bf16[128,1024]{1,0:T(8,128)(2,1)S(1)}, u32[]{:S(2)}, u32[]{:S(2)}) collective-permute-start(bf16[128,1024]{1,0:T(8,128)(2,1)S(1)} %get-tuple-element.41.res_ref.refs_4_), channel_id=1, source_target_pairs={{0,8},{4,12},{8,0},{12,4},{1,9},{5,13},{9,1},{13,5},{2,10},{6,14},... | collective-permute-start | bytes 786440 | tf_op jit(solution)/shard_map/ppermute | solution.py:15
  57.6 12.3 %collective-permute-start.12 = (bf16[128,1024]{1,0:T(8,128)(2,1)S(1)}, bf16[128,1024]{1,0:T(8,128)(2,1)S(1)}, u32[]{:S(2)}, u32[]{:S(2)}) collective-permute-start(bf16[128,1024]{1,0:T(8,128)(2,1)S(1)} %get-tuple-element.41.res_ref.refs_4_), channel_id=1, source_target_pairs={{0,4},{4,0},{8,12},{12,8},{1,5},{5,1},{9,13},{13,9},{2,6},{6,2},{1... | collective-permute-start | bytes 786440 | tf_op jit(solution)/shard_map/ppermute | solution.py:15
  57.9 1.2 %collective-permute-start.2 = (f32[192]{0:T(256)S(1)}, f32[192]{0:T(256)S(1)}, u32[]{:S(2)}, u32[]{:S(2)}) collective-permute-start(f32[192]{0:T(256)S(1)} %multiply_reduce_fusion), channel_id=1, source_target_pairs={{0,1},{1,0},{2,3},{3,2},{4,5},{5,4},{6,7},{7,6},{8,9},{9,8},{10,11... | collective-permute-start | bytes 2312 | tf_op jit(solution)/shard_map/ppermute | solution.py:15
  59.1 11.9 %collective-permute-start.3 = (f32[192]{0:T(256)S(1)}, f32[192]{0:T(256)S(1)}, u32[]{:S(2)}, u32[]{:S(2)}) collective-permute-start(f32[192]{0:T(256)S(1)} %add.77), channel_id=1, source_target_pairs={{0,3},{1,2},{2,1},{3,0},{4,7},{5,6},{6,5},{7,4},{8,11},{9,10},{10,... | collective-permute-start | bytes 2312 | tf_op jit(solution)/shard_map/ppermute | solution.py:15
  70.2 6.4 %collective-permute-start.16 = (bf16[128,1024]{1,0:T(8,128)(2,1)S(1)}, bf16[128,1024]{1,0:T(8,128)(2,1)S(1)}, u32[]{:S(2)}, u32[]{:S(2)}) collective-permute-start(bf16[128,1024]{1,0:T(8,128)(2,1)S(1)} %collective-permute-done.13.r_ref.refs_6_), channel_id=1, source_target_pairs={{0,4},{4,0},{8,12},{12,8},{1,5},{5,1},{9,13},{13,9},{2,6},{6,2},{1... | collective-permute-start | bytes 786440 | tf_op jit(solution)/shard_map/ppermute | solution.py:15
  70.8 1.5 %collective-permute-start.14 = (bf16[3,128,192]{2,1,0:T(8,128)(2,1)S(1)}, bf16[3,128,192]{2,1,0:T(8,128)(2,1)S(1)}, u32[]{:S(2)}, u32[]{:S(2)}) collective-permute-start(bf16[3,128,192]{2,1,0:T(8,128)(2,1)S(1)} %fusion), channel_id=1, source_target_pairs={{0,1},{1,0},{2,3},{3,2},{4,5},{5,4},{6,7},{7,6},{8,9},{9,8},{10,11... | collective-permute-start | bytes 442376 | tf_op jit(solution)/shard_map/ppermute | solution.py:15
  72.4 6.9 %collective-permute-start.15 = (bf16[3,128,192]{2,1,0:T(8,128)(2,1)S(1)}, bf16[3,128,192]{2,1,0:T(8,128)(2,1)S(1)}, u32[]{:S(2)}, u32[]{:S(2)}) collective-permute-start(bf16[3,128,192]{2,1,0:T(8,128)(2,1)S(1)} %fusion.3), channel_id=1, source_target_pairs={{0,3},{1,2},{2,1},{3,0},{4,7},{5,6},{6,5},{7,4},{8,11},{9,10},{10,... | collective-permute-start | bytes 442376 | tf_op jit(solution)/shard_map/ppermute | solution.py:15
  76.9 2.5 %collective-permute-start.17 = (bf16[128,192]{1,0:T(8,128)(2,1)S(1)}, bf16[128,192]{1,0:T(8,128)(2,1)S(1)}, u32[]{:S(2)}, u32[]{:S(2)}) collective-permute-start(bf16[128,192]{1,0:T(8,128)(2,1)S(1)} %fusion.13), channel_id=1, source_target_pairs={{0,1},{1,0},{2,3},{3,2},{4,5},{5,4},{6,7},{7,6},{8,9},{9,8},{10,11... | collective-permute-start | bytes 147464 | tf_op jit(solution)/shard_map/ppermute | solution.py:15
  79.5 4.1 %collective-permute-start.18 = (bf16[128,192]{1,0:T(8,128)(2,1)S(1)}, bf16[128,192]{1,0:T(8,128)(2,1)S(1)}, u32[]{:S(2)}, u32[]{:S(2)}) collective-permute-start(bf16[128,192]{1,0:T(8,128)(2,1)S(1)} %fusion.15), channel_id=1, source_target_pairs={{0,3},{1,2},{2,1},{3,0},{4,7},{5,6},{6,5},{7,4},{8,11},{9,10},{10,... | collective-permute-start | bytes 147464 | tf_op jit(solution)/shard_map/ppermute | solution.py:15
  84.5 3.6 %collective-permute-start.19 = (f32[1,1024]{1,0:T(1,128)S(1)}, f32[1,1024]{1,0:T(1,128)S(1)}, u32[]{:S(2)}, u32[]{:S(2)}) collective-permute-start(f32[1,1024]{1,0:T(1,128)S(1)} %get-tuple-element.51), channel_id=1, source_target_pairs={{0,4},{4,0},{8,12},{12,8},{1,5},{5,1},{9,13},{13,9},{2,6},{6,2},{1... | collective-permute-start | bytes 12296 | tf_op jit(solution)/shard_map/ppermute | solution.py:15
  88.1 4.5 %collective-permute-start.20 = (f32[1,1024]{1,0:T(1,128)S(1)}, f32[1,1024]{1,0:T(1,128)S(1)}, u32[]{:S(2)}, u32[]{:S(2)}) collective-permute-start(f32[1,1024]{1,0:T(1,128)S(1)} %add.97), channel_id=1, source_target_pairs={{0,8},{4,12},{8,0},{12,4},{1,9},{5,13},{9,1},{13,5},{2,10},{6,14},... | collective-permute-start | bytes 12296 | tf_op jit(solution)/shard_map/ppermute | solution.py:15
  (5 other events, 6.5 us)

commit v5 on v4

--- a/solution.py
+++ b/solution.py
@@ -38,6 +38,30 @@
         value = value + swap(value, axis, step)
         step *= 2
     return value
+
+
+def keeps_low():
+    index, odd = lax.axis_index("width"), 0
+    for bit in range((lax.axis_size("width") - 1).bit_length()):
+        odd = odd ^ ((index >> bit) & 1)
+    return odd == 0
+
+
+def half_sum(part):
+    rows, low = part.shape[0] // 2, keeps_low()
+    keep = jnp.where(low, part[:rows], part[rows:])
+    send = jnp.where(low, part[rows:], part[:rows])
+    total, step = keep.astype(f32) + swap(send, "width", 1).astype(f32), 3
+    while step < lax.axis_size("width") * 3 // 2:
+        sent = lax.reduce_precision(total, 8, 7)
+        total = sent + swap(sent.astype(bf16), "width", step).astype(f32)
+        step *= 2
+    return total
+
+
+def join(kept):
+    low, other = keeps_low(), swap(kept, "width", 1)
+    return jnp.concatenate([jnp.where(low, kept, other), jnp.where(low, other, kept)])
 
 
 def mm(a, b, contract):
@@ -188,19 +212,18 @@
 
     add_parts([0])
     if line:
-        xs[1], xs[3], centered[0], parts[0] = stage(xs[1], xs[3], centered[0], parts[0])
+        xs[3], xs[1], centered[0], parts[0] = stage(xs[3], xs[1], centered[0], parts[0])
         xs[2] = lat_swap(xs[3], 1)
         add_parts([1, 3])
-        xs[2], total = stage(xs[2], sum_parts([3]))
-        add_codes([3], total)
+        kept = jnp.maximum(half_sum(parts[3]) + b_enc, 0.0).astype(bf16)
+        xs[2], kept = stage(xs[2], kept)
+        codes[3] = join(kept)
         passed = lat_swap(recon_of(codes[3], w_dec), 1)
         add_parts([2])
         passed, total = stage(passed, sum_parts([0, 1, 2]))
         add_codes([0, 1, 2], total)
-        sums = [
-            lat_swap(recon_of(codes[1], w_dec), 1),
-            lat_swap(recon_of(codes[2], w_dec, passed), 2),
-        ]
+        onward = recon_of(codes[2], w_dec, passed)
+        sums = [lat_swap(recon_of(after(codes[1], onward), w_dec), 1), lat_swap(onward, 2)]
     else:
         add_parts(others)
         add_codes(range(count), sum_parts(range(count)))
@@ -211,25 +234,29 @@
 
     res = [res_grad] + [lat_swap(res_grad, k) if k != 3 or not line else None for k in others]
     if line:
-        res[1], res[2] = stage(res[1], res[2])
+        res[2], res[1] = stage(res[2], res[1])
         res[3] = lat_swap(res[2], 1)
     parts = [part] + [code_part(res[k], w_dec) for k in others]
     early = width_sum(jnp.stack(parts[:-1]))
     code_sums = [early[k] for k in range(count - 1)] + [width_sum(parts[-1])]
+    code_total = sum(jnp.sum(c.astype(f32), axis=0) for c in codes)
     squares = square_sums(after(w_dec, xs[1]))
     norms = jnp.sqrt(squares + 1e-06)
+    sparsity = (sparsity_coef * row_scale * code_total / norms)[:, None] * w_dec.astype(f32)
+    (grad_dec,) = dec_add(sparsity, codes, res)
+    code_sums[-1], grad_dec = stage(code_sums[-1], grad_dec)
     grads, grad_benc, share = pre_grads(
         codes, code_sums, sparsity_coef * row_scale * norms, w_enc_t, res_grad
     )
-    step = 1
-    while 2 * step < count:
-        share = share + lat_swap(share, step)
-        step *= 2
     grad_enc = enc_end(centered, grads).T
-    code_total = sum(jnp.sum(c.astype(f32), axis=0) for c in codes)
-    sparsity = (sparsity_coef * row_scale * code_total / norms)[:, None] * w_dec.astype(f32)
-    (grad_dec,) = dec_add(sparsity, codes, res)
-    grad_bdec = share + lat_swap(share, step)
+    if line:
+        near, far, cross = (lat_swap(share, k) for k in others)
+        grad_bdec = (share + near) + (far + cross)
+    else:
+        grad_bdec, step = share, 1
+        while step < count:
+            grad_bdec = grad_bdec + lat_swap(grad_bdec, step)
+            step *= 2
     return (grad_enc, grad_benc, grad_dec, grad_bdec[0])
 
 

time: 93.4 us -> 91 us (0.974)
  waiting for transfers between devices: 61.5 us -> 58.5 us
    ppermute x21 -> x23, waiting for transfers between devices: 61.5 us -> 58.5 us  [swap(): return lax.ppermute(value, axis, [(i, i ^ distance) for i in range(count)])]
    ppermute x21 -> x23, starting transfers between devices: 19.8 us -> 20.4 us  [swap(): return lax.ppermute(value, axis, [(i, i ^ distance) for i in range(count)])]
  transfers between devices with their start and end apart: 21 -> 23, of which waited for: 19 -> 19; matrix products, arithmetic and copies ran while one was open for 1% -> 1% of each run, Pallas kernels for 5% -> 5%
where the time goes in v5:
time: 91 us; the launch traced here: 90.8 us
  waiting for transfers between devices  58.5 us (64%)
  starting transfers between devices  20.4 us (22%)
  Pallas kernels  6.81 us (7%)
  local copies, waits for them, and re-layouts  2.69 us (3%)
  other arithmetic  1.49 us (2%)
    ppermute x23, waiting for transfers between devices, swap(): return lax.ppermute(value, axis, [(i, i ^ distance) for i in range(count)])  58.5 us
    ppermute x23, starting transfers between devices, swap(): return lax.ppermute(value, axis, [(i, i ^ distance) for i in range(count)])  20.4 us
    pallas_call x14, Pallas kernels, call(): pl.pallas_call(kernel, out_shape=[jax.ShapeDtypeStruct(shape, kind) for s...  6.81 us
    unnamed x16, local copies, waits for them, and re-layouts  2.66 us
  transfers between devices with their start and end apart: 23, of which 19 were waited for; matrix products, arithmetic and copies ran while one was open for 1% of the time, Pallas kernels for 5%

profile of v5, /device:TPU:0, one launch (start us, length us, event | category | flops | bytes accessed | tf_op | source)
XLA Modules:
  0.0 90.8 jit_solution(10276420479551275887)
XLA Ops:
  0.6 5.1 %collective-permute-start = (bf16[128,1024]{1,0:T(8,128)(2,1)}, bf16[128,1024]{1,0:T(8,128)(2,1)S(1)}, u32[]{:S(2)}, u32[]{:S(2)}) collective-permute-start(bf16[128,1024]{1,0:T(8,128)(2,1)} %x_ref.3), channel_id=1, source_target_pairs={{0,12},{4,8},{8,4},{12,0},{1,13},{5,9},{9,5},{13,1},{2,14},{6,10},... | collective-permute-start | bytes 786440 | tf_op jit(solution)/shard_map/ppermute | solution.py:15
  8.7 4.5 %collective-permute-done.x_ref = bf16[128,1024]{1,0:T(8,128)(2,1)S(1)} collective-permute-done((bf16[128,1024]{1,0:T(8,128)(2,1)}, bf16[128,1024]{1,0:T(8,128)(2,1)S(1)}, u32[]{:S(2)}, u32[]{:S(2)}) %collective-permute-start) | collective-permute-done | bytes 262176 | tf_op jit(solution)/shard_map/ppermute | solution.py:15
  13.2 4.8 %collective-permute-done.1.x_ref = bf16[128,1024]{1,0:T(8,128)(2,1)S(1)} collective-permute-done((bf16[128,1024]{1,0:T(8,128)(2,1)}, bf16[128,1024]{1,0:T(8,128)(2,1)S(1)}, u32[]{:S(2)}, u32[]{:S(2)}) %collective-permute-start.1) | collective-permute-done | bytes 262176 | tf_op jit(solution)/shard_map/ppermute | solution.py:15
  18.4 1.7 %collective-permute-start.4 = (bf16[128,1024]{1,0:T(8,128)(2,1)S(1)}, bf16[128,1024]{1,0:T(8,128)(2,1)S(1)}, u32[]{:S(2)}, u32[]{:S(2)}) collective-permute-start(bf16[128,1024]{1,0:T(8,128)(2,1)S(1)} %collective-permute-done.x_ref), channel_id=1, source_target_pairs={{0,4},{4,0},{8,12},{12,8},{1,5},{5,1},{9,13},{13,9},{2,6},{6,2},{1... | collective-permute-start | bytes 786440 | tf_op jit(solution)/shard_map/ppermute | solution.py:15
  20.2 1.3 %collective-permute-start.6 = (bf16[64,192]{1,0:T(8,128)(2,1)S(1)}, bf16[64,192]{1,0:T(8,128)(2,1)S(1)}, u32[]{:S(2)}, u32[]{:S(2)}) collective-permute-start(bf16[64,192]{1,0:T(8,128)(2,1)S(1)} %fusion.12), channel_id=1, source_target_pairs={{0,3},{1,2},{2,1},{3,0},{4,7},{5,6},{6,5},{7,4},{8,11},{9,10},{10,... | collective-permute-start | bytes 73736 | tf_op jit(solution)/shard_map/ppermute | solution.py:15
  21.8 1.8 %collective-permute-done.6 = bf16[64,192]{1,0:T(8,128)(2,1)S(1)} collective-permute-done((bf16[64,192]{1,0:T(8,128)(2,1)S(1)}, bf16[64,192]{1,0:T(8,128)(2,1)S(1)}, u32[]{:S(2)}, u32[]{:S(2)}) %collective-permute-start.6) | collective-permute-done | bytes 24608 | tf_op jit(solution)/shard_map/ppermute | solution.py:15
  23.6 3.5 %collective-permute-done.4.x_ref = bf16[128,1024]{1,0:T(8,128)(2,1)S(1)} collective-permute-done((bf16[128,1024]{1,0:T(8,128)(2,1)S(1)}, bf16[128,1024]{1,0:T(8,128)(2,1)S(1)}, u32[]{:S(2)}, u32[]{:S(2)}) %collective-permute-start.4) | collective-permute-done | bytes 262176 | tf_op jit(solution)/shard_map/ppermute | solution.py:15
  29.0 1.3 %collective-permute-start.10 = (bf16[3,128,192]{2,1,0:T(8,128)(2,1)S(1)}, bf16[3,128,192]{2,1,0:T(8,128)(2,1)S(1)}, u32[]{:S(2)}, u32[]{:S(2)}) collective-permute-start(bf16[3,128,192]{2,1,0:T(8,128)(2,1)S(1)} %fusion.2), channel_id=1, source_target_pairs={{0,3},{1,2},{2,1},{3,0},{4,7},{5,6},{6,5},{7,4},{8,11},{9,10},{10,... | collective-permute-start | bytes 442376 | tf_op jit(solution)/shard_map/ppermute | solution.py:15
  30.6 1.8 %collective-permute-start.8 = (bf16[128,1024]{1,0:T(8,128)(2,1)S(1)}, bf16[128,1024]{1,0:T(8,128)(2,1)S(1)}, u32[]{:S(2)}, u32[]{:S(2)}) collective-permute-start(bf16[128,1024]{1,0:T(8,128)(2,1)S(1)} %recon_of.3), channel_id=1, source_target_pairs={{0,4},{4,0},{8,12},{12,8},{1,5},{5,1},{9,13},{13,9},{2,6},{6,2},{1... | collective-permute-start | bytes 786440 | tf_op jit(solution)/shard_map/ppermute | solution.py:15
  32.3 3.6 %collective-permute-done.10 = bf16[3,128,192]{2,1,0:T(8,128)(2,1)S(1)} collective-permute-done((bf16[3,128,192]{2,1,0:T(8,128)(2,1)S(1)}, bf16[3,128,192]{2,1,0:T(8,128)(2,1)S(1)}, u32[]{:S(2)}, u32[]{:S(2)}) %collective-permute-start.10) | collective-permute-done | bytes 147488 | tf_op jit(solution)/shard_map/ppermute | solution.py:15
  36.0 3.2 %collective-permute-done.8.refs_0_ = bf16[128,1024]{1,0:T(8,128)(2,1)S(1)} collective-permute-done((bf16[128,1024]{1,0:T(8,128)(2,1)S(1)}, bf16[128,1024]{1,0:T(8,128)(2,1)S(1)}, u32[]{:S(2)}, u32[]{:S(2)}) %collective-permute-start.8) | collective-permute-done | bytes 262176 | tf_op jit(solution)/shard_map/ppermute | solution.py:15
  39.8 1.7 %collective-permute-start.11 = (bf16[128,1024]{1,0:T(8,128)(2,1)S(1)}, bf16[128,1024]{1,0:T(8,128)(2,1)S(1)}, u32[]{:S(2)}, u32[]{:S(2)}) collective-permute-start(bf16[128,1024]{1,0:T(8,128)(2,1)S(1)} %recon_of.5), channel_id=1, source_target_pairs={{0,4},{4,0},{8,12},{12,8},{1,5},{5,1},{9,13},{13,9},{2,6},{6,2},{1... | collective-permute-start | bytes 786440 | tf_op jit(solution)/shard_map/ppermute | solution.py:15
  42.1 8.9 %collective-permute-done.11.refs_0_ = bf16[128,1024]{1,0:T(8,128)(2,1)S(1)} collective-permute-done((bf16[128,1024]{1,0:T(8,128)(2,1)S(1)}, bf16[128,1024]{1,0:T(8,128)(2,1)S(1)}, u32[]{:S(2)}, u32[]{:S(2)}) %collective-permute-start.11) | collective-permute-done | bytes 262176 | tf_op jit(solution)/shard_map/ppermute | solution.py:15
  51.0 4.5 %collective-permute-done.12.refs_1_ = bf16[128,1024]{1,0:T(8,128)(2,1)S(1)} collective-permute-done((bf16[128,1024]{1,0:T(8,128)(2,1)S(1)}, bf16[128,1024]{1,0:T(8,128)(2,1)S(1)}, u32[]{:S(2)}, u32[]{:S(2)}) %collective-permute-start.12) | collective-permute-done | bytes 262176 | tf_op jit(solution)/shard_map/ppermute | solution.py:15
  58.1 2.6 %collective-permute-done.3 = f32[192]{0:T(256)S(1)} collective-permute-done((f32[192]{0:T(256)S(1)}, f32[192]{0:T(256)S(1)}, u32[]{:S(2)}, u32[]{:S(2)}) %collective-permute-start.3) | collective-permute-done | bytes 800 | tf_op jit(solution)/shard_map/ppermute | solution.py:15
  60.7 6.6 %collective-permute-done.13.r_ref.refs_6_ = bf16[128,1024]{1,0:T(8,128)(2,1)S(1)} collective-permute-done((bf16[128,1024]{1,0:T(8,128)(2,1)S(1)}, bf16[128,1024]{1,0:T(8,128)(2,1)S(1)}, u32[]{:S(2)}, u32[]{:S(2)}) %collective-permute-start.13) | collective-permute-done | bytes 262176 | tf_op jit(solution)/shard_map/ppermute | solution.py:15
  69.6 1.3 %collective-permute-done.15 = bf16[3,128,192]{2,1,0:T(8,128)(2,1)S(1)} collective-permute-done((bf16[3,128,192]{2,1,0:T(8,128)(2,1)S(1)}, bf16[3,128,192]{2,1,0:T(8,128)(2,1)S(1)}, u32[]{:S(2)}, u32[]{:S(2)}) %collective-permute-start.15) | collective-permute-done | bytes 147488 | tf_op jit(solution)/shard_map/ppermute | solution.py:15
  71.3 3.6 %collective-permute-done.17.r_ref.refs_7_ = bf16[128,1024]{1,0:T(8,128)(2,1)S(1)} collective-permute-done((bf16[128,1024]{1,0:T(8,128)(2,1)S(1)}, bf16[128,1024]{1,0:T(8,128)(2,1)S(1)}, u32[]{:S(2)}, u32[]{:S(2)}) %collective-permute-start.17) | collective-permute-done | bytes 262176 | tf_op jit(solution)/shard_map/ppermute | solution.py:15
  75.3 1.5 %dec_add.1 = f32[192,1024]{1,0:T(8,128)} custom-call(f32[192,1024]{1,0:T(8,128)S(1)} %convert_multiply_fusion.total_ref, bf16[128,192]{1,0:T(8,128)(2,1)S(1)} %get-tuple-element.67.c_ref.refs_0_, bf16[128,192]{1,0:T(8,128)(2,1)S(1)} %get-tuple-element.44.c_ref.refs_1_, bf16[128,192]{1,0:T(8,128)(2,1)S(1)} %get-tuple-element.63.c_ref.refs_2_, ...), custom_call_target="tpu_custom_call" | custom-call | flops 1000000 | bytes 1000000 | tf_op jit(solution)/shard_map/dec_add/pallas_call | solution.py:75
  76.8 1.2 %collective-permute-done.16 = bf16[3,128,192]{2,1,0:T(8,128)(2,1)S(1)} collective-permute-done((bf16[3,128,192]{2,1,0:T(8,128)(2,1)S(1)}, bf16[3,128,192]{2,1,0:T(8,128)(2,1)S(1)}, u32[]{:S(2)}, u32[]{:S(2)}) %collective-permute-start.16) | collective-permute-done | bytes 147488 | tf_op jit(solution)/shard_map/ppermute | solution.py:15
  78.5 3.8 %collective-permute-done.19 = bf16[128,192]{1,0:T(8,128)(2,1)S(1)} collective-permute-done((bf16[128,192]{1,0:T(8,128)(2,1)S(1)}, bf16[128,192]{1,0:T(8,128)(2,1)S(1)}, u32[]{:S(2)}, u32[]{:S(2)}) %collective-permute-start.19) | collective-permute-done | bytes 49184 | tf_op jit(solution)/shard_map/ppermute | solution.py:15
  83.1 1.7 %collective-permute-start.20 = (f32[1,1024]{1,0:T(1,128)S(1)}, f32[1,1024]{1,0:T(1,128)S(1)}, u32[]{:S(2)}, u32[]{:S(2)}) collective-permute-start(f32[1,1024]{1,0:T(1,128)S(1)} %get-tuple-element.57), channel_id=1, source_target_pairs={{0,4},{4,0},{8,12},{12,8},{1,5},{5,1},{9,13},{13,9},{2,6},{6,2},{1... | collective-permute-start | bytes 12296 | tf_op jit(solution)/shard_map/ppermute | solution.py:15
  84.8 2.7 %collective-permute-start.22 = (f32[1,1024]{1,0:T(1,128)S(1)}, f32[1,1024]{1,0:T(1,128)S(1)}, u32[]{:S(2)}, u32[]{:S(2)}) collective-permute-start(f32[1,1024]{1,0:T(1,128)S(1)} %get-tuple-element.57), channel_id=1, source_target_pairs={{0,12},{4,8},{8,4},{12,0},{1,13},{5,9},{9,5},{13,1},{2,14},{6,10},... | collective-permute-start | bytes 12296 | tf_op jit(solution)/shard_map/ppermute | solution.py:15
  87.5 1.5 %enc_end.1 = f32[192,1024]{1,0:T(8,128)} custom-call(bf16[4,128,192]{2,1,0:T(8,128)(2,1)S(1)} %get-tuple-element.50.g_ref, bf16[128,1024]{1,0:T(8,128)(2,1)S(1)} %get-tuple-element.51.refs_0_, bf16[128,1024]{1,0:T(8,128)(2,1)S(1)} %get-tuple-element.52.refs_1_, bf16[128,1024]{1,0:T(8,128)(2,1)S(1)} %get-tuple-element.53.refs_2_, ...), custom_call_target="tpu_custom_call" | custom-call | flops 1000000 | bytes 1000000 | tf_op jit(solution)/shard_map/enc_end/pallas_call | solution.py:75
  (74 shorter events, 15.6 us)
Async XLA Ops:
  0.6 12.6 %collective-permute-start = (bf16[128,1024]{1,0:T(8,128)(2,1)}, bf16[128,1024]{1,0:T(8,128)(2,1)S(1)}, u32[]{:S(2)}, u32[]{:S(2)}) collective-permute-start(bf16[128,1024]{1,0:T(8,128)(2,1)} %x_ref.3), channel_id=1, source_target_pairs={{0,12},{4,8},{8,4},{12,0},{1,13},{5,9},{9,5},{13,1},{2,14},{6,10},... | collective-permute-start | bytes 786440 | tf_op jit(solution)/shard_map/ppermute | solution.py:15
  5.7 12.2 %collective-permute-start.1 = (bf16[128,1024]{1,0:T(8,128)(2,1)}, bf16[128,1024]{1,0:T(8,128)(2,1)S(1)}, u32[]{:S(2)}, u32[]{:S(2)}) collective-permute-start(bf16[128,1024]{1,0:T(8,128)(2,1)} %x_ref.3), channel_id=1, source_target_pairs={{0,4},{4,0},{8,12},{12,8},{1,5},{5,1},{9,13},{13,9},{2,6},{6,2},{1... | collective-permute-start | bytes 786440 | tf_op jit(solution)/shard_map/ppermute | solution.py:15
  18.3 1.8 %collective-permute-start.5 = (bf16[64,192]{1,0:T(8,128)(2,1)S(1)}, bf16[64,192]{1,0:T(8,128)(2,1)S(1)}, u32[]{:S(2)}, u32[]{:S(2)}) collective-permute-start(bf16[64,192]{1,0:T(8,128)(2,1)S(1)} %broadcast_select_fusion.2), channel_id=1, source_target_pairs={{0,1},{1,0},{2,3},{3,2},{4,5},{5,4},{6,7},{7,6},{8,9},{9,8},{10,11... | collective-permute-start | bytes 73736 | tf_op jit(solution)/shard_map/ppermute | solution.py:15
  18.4 8.7 %collective-permute-start.4 = (bf16[128,1024]{1,0:T(8,128)(2,1)S(1)}, bf16[128,1024]{1,0:T(8,128)(2,1)S(1)}, u32[]{:S(2)}, u32[]{:S(2)}) collective-permute-start(bf16[128,1024]{1,0:T(8,128)(2,1)S(1)} %collective-permute-done.x_ref), channel_id=1, source_target_pairs={{0,4},{4,0},{8,12},{12,8},{1,5},{5,1},{9,13},{13,9},{2,6},{6,2},{1... | collective-permute-start | bytes 786440 | tf_op jit(solution)/shard_map/ppermute | solution.py:15
  20.2 3.4 %collective-permute-start.6 = (bf16[64,192]{1,0:T(8,128)(2,1)S(1)}, bf16[64,192]{1,0:T(8,128)(2,1)S(1)}, u32[]{:S(2)}, u32[]{:S(2)}) collective-permute-start(bf16[64,192]{1,0:T(8,128)(2,1)S(1)} %fusion.12), channel_id=1, source_target_pairs={{0,3},{1,2},{2,1},{3,0},{4,7},{5,6},{6,5},{7,4},{8,11},{9,10},{10,... | collective-permute-start | bytes 73736 | tf_op jit(solution)/shard_map/ppermute | solution.py:15
  27.4 1.5 %collective-permute-start.9 = (bf16[3,128,192]{2,1,0:T(8,128)(2,1)S(1)}, bf16[3,128,192]{2,1,0:T(8,128)(2,1)S(1)}, u32[]{:S(2)}, u32[]{:S(2)}) collective-permute-start(bf16[3,128,192]{2,1,0:T(8,128)(2,1)S(1)} %fusion.1), channel_id=1, source_target_pairs={{0,1},{1,0},{2,3},{3,2},{4,5},{5,4},{6,7},{7,6},{8,9},{9,8},{10,11... | collective-permute-start | bytes 442376 | tf_op jit(solution)/shard_map/ppermute | solution.py:15
  27.5 2.8 %collective-permute-start.7 = (bf16[64,192]{1,0:T(8,128)(2,1)S(1)}, bf16[64,192]{1,0:T(8,128)(2,1)S(1)}, u32[]{:S(2)}, u32[]{:S(2)}) collective-permute-start(bf16[64,192]{1,0:T(8,128)(2,1)S(1)} %maximum_convert_fusion), channel_id=1, source_target_pairs={{0,1},{1,0},{2,3},{3,2},{4,5},{5,4},{6,7},{7,6},{8,9},{9,8},{10,11... | collective-permute-start | bytes 73736 | tf_op jit(solution)/shard_map/ppermute | solution.py:15
  29.0 6.9 %collective-permute-start.10 = (bf16[3,128,192]{2,1,0:T(8,128)(2,1)S(1)}, bf16[3,128,192]{2,1,0:T(8,128)(2,1)S(1)}, u32[]{:S(2)}, u32[]{:S(2)}) collective-permute-start(bf16[3,128,192]{2,1,0:T(8,128)(2,1)S(1)} %fusion.2), channel_id=1, source_target_pairs={{0,3},{1,2},{2,1},{3,0},{4,7},{5,6},{6,5},{7,4},{8,11},{9,10},{10,... | collective-permute-start | bytes 442376 | tf_op jit(solution)/shard_map/ppermute | solution.py:15
  30.6 8.6 %collective-permute-start.8 = (bf16[128,1024]{1,0:T(8,128)(2,1)S(1)}, bf16[128,1024]{1,0:T(8,128)(2,1)S(1)}, u32[]{:S(2)}, u32[]{:S(2)}) collective-permute-start(bf16[128,1024]{1,0:T(8,128)(2,1)S(1)} %recon_of.3), channel_id=1, source_target_pairs={{0,4},{4,0},{8,12},{12,8},{1,5},{5,1},{9,13},{13,9},{2,6},{6,2},{1... | collective-permute-start | bytes 786440 | tf_op jit(solution)/shard_map/ppermute | solution.py:15
  39.5 16.1 %copy-start.4 = (bf16[128,1024]{1,0:T(8,128)(2,1)S(1)}, bf16[128,1024]{1,0:T(8,128)(2,1)}, u32[]{:S(2)}) copy-start(bf16[128,1024]{1,0:T(8,128)(2,1)} %x_ref.3) | copy-start | bytes 786436
  39.8 11.3 %collective-permute-start.11 = (bf16[128,1024]{1,0:T(8,128)(2,1)S(1)}, bf16[128,1024]{1,0:T(8,128)(2,1)S(1)}, u32[]{:S(2)}, u32[]{:S(2)}) collective-permute-start(bf16[128,1024]{1,0:T(8,128)(2,1)S(1)} %recon_of.5), channel_id=1, source_target_pairs={{0,4},{4,0},{8,12},{12,8},{1,5},{5,1},{9,13},{13,9},{2,6},{6,2},{1... | collective-permute-start | bytes 786440 | tf_op jit(solution)/shard_map/ppermute | solution.py:15
  41.5 14.1 %collective-permute-start.12 = (bf16[128,1024]{1,0:T(8,128)(2,1)S(1)}, bf16[128,1024]{1,0:T(8,128)(2,1)S(1)}, u32[]{:S(2)}, u32[]{:S(2)}) collective-permute-start(bf16[128,1024]{1,0:T(8,128)(2,1)S(1)} %recon_of.4), channel_id=1, source_target_pairs={{0,8},{4,12},{8,0},{12,4},{1,9},{5,13},{9,1},{13,5},{2,10},{6,14},... | collective-permute-start | bytes 786440 | tf_op jit(solution)/shard_map/ppermute | solution.py:15
  56.0 11.3 %collective-permute-start.13 = (bf16[128,1024]{1,0:T(8,128)(2,1)S(1)}, bf16[128,1024]{1,0:T(8,128)(2,1)S(1)}, u32[]{:S(2)}, u32[]{:S(2)}) collective-permute-start(bf16[128,1024]{1,0:T(8,128)(2,1)S(1)} %get-tuple-element.45.refs_4_.res_ref), channel_id=1, source_target_pairs={{0,8},{4,12},{8,0},{12,4},{1,9},{5,13},{9,1},{13,5},{2,10},{6,14},... | collective-permute-start | bytes 786440 | tf_op jit(solution)/shard_map/ppermute | solution.py:15
  56.3 12.2 %collective-permute-start.14 = (bf16[128,1024]{1,0:T(8,128)(2,1)S(1)}, bf16[128,1024]{1,0:T(8,128)(2,1)S(1)}, u32[]{:S(2)}, u32[]{:S(2)}) collective-permute-start(bf16[128,1024]{1,0:T(8,128)(2,1)S(1)} %get-tuple-element.45.refs_4_.res_ref), channel_id=1, source_target_pairs={{0,4},{4,0},{8,12},{12,8},{1,5},{5,1},{9,13},{13,9},{2,6},{6,2},{1... | collective-permute-start | bytes 786440 | tf_op jit(solution)/shard_map/ppermute | solution.py:15
  56.5 1.2 %collective-permute-start.2 = (f32[192]{0:T(256)S(1)}, f32[192]{0:T(256)S(1)}, u32[]{:S(2)}, u32[]{:S(2)}) collective-permute-start(f32[192]{0:T(256)S(1)} %multiply_reduce_fusion), channel_id=1, source_target_pairs={{0,1},{1,0},{2,3},{3,2},{4,5},{5,4},{6,7},{7,6},{8,9},{9,8},{10,11... | collective-permute-start | bytes 2312 | tf_op jit(solution)/shard_map/ppermute | solution.py:15
  57.7 3.0 %collective-permute-start.3 = (f32[192]{0:T(256)S(1)}, f32[192]{0:T(256)S(1)}, u32[]{:S(2)}, u32[]{:S(2)}) collective-permute-start(f32[192]{0:T(256)S(1)} %add.82), channel_id=1, source_target_pairs={{0,3},{1,2},{2,1},{3,0},{4,7},{5,6},{6,5},{7,4},{8,11},{9,10},{10,... | collective-permute-start | bytes 2312 | tf_op jit(solution)/shard_map/ppermute | solution.py:15
  68.5 6.4 %collective-permute-start.17 = (bf16[128,1024]{1,0:T(8,128)(2,1)S(1)}, bf16[128,1024]{1,0:T(8,128)(2,1)S(1)}, u32[]{:S(2)}, u32[]{:S(2)}) collective-permute-start(bf16[128,1024]{1,0:T(8,128)(2,1)S(1)} %collective-permute-done.13.r_ref.refs_6_), channel_id=1, source_target_pairs={{0,4},{4,0},{8,12},{12,8},{1,5},{5,1},{9,13},{13,9},{2,6},{6,2},{1... | collective-permute-start | bytes 786440 | tf_op jit(solution)/shard_map/ppermute | solution.py:15
  69.4 1.5 %collective-permute-start.15 = (bf16[3,128,192]{2,1,0:T(8,128)(2,1)S(1)}, bf16[3,128,192]{2,1,0:T(8,128)(2,1)S(1)}, u32[]{:S(2)}, u32[]{:S(2)}) collective-permute-start(bf16[3,128,192]{2,1,0:T(8,128)(2,1)S(1)} %fusion), channel_id=1, source_target_pairs={{0,1},{1,0},{2,3},{3,2},{4,5},{5,4},{6,7},{7,6},{8,9},{9,8},{10,11... | collective-permute-start | bytes 442376 | tf_op jit(solution)/shard_map/ppermute | solution.py:15
  71.0 6.9 %collective-permute-start.16 = (bf16[3,128,192]{2,1,0:T(8,128)(2,1)S(1)}, bf16[3,128,192]{2,1,0:T(8,128)(2,1)S(1)}, u32[]{:S(2)}, u32[]{:S(2)}) collective-permute-start(bf16[3,128,192]{2,1,0:T(8,128)(2,1)S(1)} %fusion.3), channel_id=1, source_target_pairs={{0,3},{1,2},{2,1},{3,0},{4,7},{5,6},{6,5},{7,4},{8,11},{9,10},{10,... | collective-permute-start | bytes 442376 | tf_op jit(solution)/shard_map/ppermute | solution.py:15
  75.2 2.9 %collective-permute-start.18 = (bf16[128,192]{1,0:T(8,128)(2,1)S(1)}, bf16[128,192]{1,0:T(8,128)(2,1)S(1)}, u32[]{:S(2)}, u32[]{:S(2)}) collective-permute-start(bf16[128,192]{1,0:T(8,128)(2,1)S(1)} %fusion.10), channel_id=1, source_target_pairs={{0,1},{1,0},{2,3},{3,2},{4,5},{5,4},{6,7},{7,6},{8,9},{9,8},{10,11... | collective-permute-start | bytes 147464 | tf_op jit(solution)/shard_map/ppermute | solution.py:15
  78.1 4.1 %collective-permute-start.19 = (bf16[128,192]{1,0:T(8,128)(2,1)S(1)}, bf16[128,192]{1,0:T(8,128)(2,1)S(1)}, u32[]{:S(2)}, u32[]{:S(2)}) collective-permute-start(bf16[128,192]{1,0:T(8,128)(2,1)S(1)} %fusion.11), channel_id=1, source_target_pairs={{0,3},{1,2},{2,1},{3,0},{4,7},{5,6},{6,5},{7,4},{8,11},{9,10},{10,... | collective-permute-start | bytes 147464 | tf_op jit(solution)/shard_map/ppermute | solution.py:15
  83.1 5.9 %collective-permute-start.20 = (f32[1,1024]{1,0:T(1,128)S(1)}, f32[1,1024]{1,0:T(1,128)S(1)}, u32[]{:S(2)}, u32[]{:S(2)}) collective-permute-start(f32[1,1024]{1,0:T(1,128)S(1)} %get-tuple-element.57), channel_id=1, source_target_pairs={{0,4},{4,0},{8,12},{12,8},{1,5},{5,1},{9,13},{13,9},{2,6},{6,2},{1... | collective-permute-start | bytes 12296 | tf_op jit(solution)/shard_map/ppermute | solution.py:15
  84.8 4.5 %collective-permute-start.21 = (f32[1,1024]{1,0:T(1,128)S(1)}, f32[1,1024]{1,0:T(1,128)S(1)}, u32[]{:S(2)}, u32[]{:S(2)}) collective-permute-start(f32[1,1024]{1,0:T(1,128)S(1)} %get-tuple-element.57), channel_id=1, source_target_pairs={{0,8},{4,12},{8,0},{12,4},{1,9},{5,13},{9,1},{13,5},{2,10},{6,14},... | collective-permute-start | bytes 12296 | tf_op jit(solution)/shard_map/ppermute | solution.py:15
  84.8 5.4 %collective-permute-start.22 = (f32[1,1024]{1,0:T(1,128)S(1)}, f32[1,1024]{1,0:T(1,128)S(1)}, u32[]{:S(2)}, u32[]{:S(2)}) collective-permute-start(f32[1,1024]{1,0:T(1,128)S(1)} %get-tuple-element.57), channel_id=1, source_target_pairs={{0,12},{4,8},{8,4},{12,0},{1,13},{5,9},{9,5},{13,1},{2,14},{6,10},... | collective-permute-start | bytes 12296 | tf_op jit(solution)/shard_map/ppermute | solution.py:15
  (7 other events, 34.6 us)

commit v6 on v5

--- a/solution.py
+++ b/solution.py
@@ -216,7 +216,6 @@
         xs[2] = lat_swap(xs[3], 1)
         add_parts([1, 3])
         kept = jnp.maximum(half_sum(parts[3]) + b_enc, 0.0).astype(bf16)
-        xs[2], kept = stage(xs[2], kept)
         codes[3] = join(kept)
         passed = lat_swap(recon_of(codes[3], w_dec), 1)
         add_parts([2])

time: 91 us -> 89.1 us (0.979)
  starting transfers between devices: 20.4 us -> 17.6 us
    ppermute x23, starting transfers between devices: 20.4 us -> 17.6 us  [swap(): return lax.ppermute(value, axis, [(i, i ^ distance) for i in range(count)])]
  transfers between devices with their start and end apart: 23 -> 23, of which waited for: 19 -> 19; matrix products, arithmetic and copies ran while one was open for 1% -> 1% of each run, Pallas kernels for 5% -> 6%
where the time goes in v6:
time: 89.1 us; the launch traced here: 88.9 us
  waiting for transfers between devices  58.9 us (66%)
  starting transfers between devices  17.6 us (20%)
  Pallas kernels  6.81 us (8%)
  local copies, waits for them, and re-layouts  3.23 us (4%)
  other arithmetic  1.49 us (2%)
  between operations  0.93 us (1%)
    ppermute x23, waiting for transfers between devices, swap(): return lax.ppermute(value, axis, [(i, i ^ distance) for i in range(count)])  58.9 us
    ppermute x23, starting transfers between devices, swap(): return lax.ppermute(value, axis, [(i, i ^ distance) for i in range(count)])  17.6 us
    pallas_call x14, Pallas kernels, call(): pl.pallas_call(kernel, out_shape=[jax.ShapeDtypeStruct(shape, kind) for s...  6.81 us
    unnamed x16, local copies, waits for them, and re-layouts  3.2 us
  transfers between devices with their start and end apart: 23, of which 19 were waited for; matrix products, arithmetic and copies ran while one was open for 1% of the time, Pallas kernels for 6%

profile of v6, /device:TPU:0, one launch (start us, length us, event | category | flops | bytes accessed | tf_op | source)
XLA Modules:
  0.0 88.9 jit_solution(5746134787107140011)
XLA Ops:
  0.6 5.1 %collective-permute-start = (bf16[128,1024]{1,0:T(8,128)(2,1)}, bf16[128,1024]{1,0:T(8,128)(2,1)S(1)}, u32[]{:S(2)}, u32[]{:S(2)}) collective-permute-start(bf16[128,1024]{1,0:T(8,128)(2,1)} %x_ref.3), channel_id=1, source_target_pairs={{0,12},{4,8},{8,4},{12,0},{1,13},{5,9},{9,5},{13,1},{2,14},{6,10},... | collective-permute-start | bytes 786440 | tf_op jit(solution)/shard_map/ppermute | solution.py:15
  6.4 1.0 %copy-done.1 = bf16[1024,192]{0,1:T(8,128)(2,1)S(1)} copy-done((bf16[1024,192]{0,1:T(8,128)(2,1)S(1)}, bf16[1024,192]{0,1:T(8,128)(2,1)}, u32[]{:S(2)}) %copy-start.1) | copy-done | bytes 393240
  8.7 4.5 %collective-permute-done.x_ref = bf16[128,1024]{1,0:T(8,128)(2,1)S(1)} collective-permute-done((bf16[128,1024]{1,0:T(8,128)(2,1)}, bf16[128,1024]{1,0:T(8,128)(2,1)S(1)}, u32[]{:S(2)}, u32[]{:S(2)}) %collective-permute-start) | collective-permute-done | bytes 262176 | tf_op jit(solution)/shard_map/ppermute | solution.py:15
  13.2 4.8 %collective-permute-done.1.x_ref = bf16[128,1024]{1,0:T(8,128)(2,1)S(1)} collective-permute-done((bf16[128,1024]{1,0:T(8,128)(2,1)}, bf16[128,1024]{1,0:T(8,128)(2,1)S(1)}, u32[]{:S(2)}, u32[]{:S(2)}) %collective-permute-start.1) | collective-permute-done | bytes 262176 | tf_op jit(solution)/shard_map/ppermute | solution.py:15
  18.0 1.7 %collective-permute-start.8 = (bf16[128,1024]{1,0:T(8,128)(2,1)S(1)}, bf16[128,1024]{1,0:T(8,128)(2,1)S(1)}, u32[]{:S(2)}, u32[]{:S(2)}) collective-permute-start(bf16[128,1024]{1,0:T(8,128)(2,1)S(1)} %collective-permute-done.x_ref), channel_id=1, source_target_pairs={{0,4},{4,0},{8,12},{12,8},{1,5},{5,1},{9,13},{13,9},{2,6},{6,2},{1... | collective-permute-start | bytes 786440 | tf_op jit(solution)/shard_map/ppermute | solution.py:15
  21.3 1.3 %collective-permute-start.5 = (bf16[64,192]{1,0:T(8,128)(2,1)S(1)}, bf16[64,192]{1,0:T(8,128)(2,1)S(1)}, u32[]{:S(2)}, u32[]{:S(2)}) collective-permute-start(bf16[64,192]{1,0:T(8,128)(2,1)S(1)} %fusion.12), channel_id=1, source_target_pairs={{0,3},{1,2},{2,1},{3,0},{4,7},{5,6},{6,5},{7,4},{8,11},{9,10},{10,... | collective-permute-start | bytes 73736 | tf_op jit(solution)/shard_map/ppermute | solution.py:15
  22.6 3.6 %collective-permute-done.8.x_ref = bf16[128,1024]{1,0:T(8,128)(2,1)S(1)} collective-permute-done((bf16[128,1024]{1,0:T(8,128)(2,1)S(1)}, bf16[128,1024]{1,0:T(8,128)(2,1)S(1)}, u32[]{:S(2)}, u32[]{:S(2)}) %collective-permute-start.8) | collective-permute-done | bytes 262176 | tf_op jit(solution)/shard_map/ppermute | solution.py:15
  28.1 1.3 %collective-permute-start.10 = (bf16[3,128,192]{2,1,0:T(8,128)(2,1)S(1)}, bf16[3,128,192]{2,1,0:T(8,128)(2,1)S(1)}, u32[]{:S(2)}, u32[]{:S(2)}) collective-permute-start(bf16[3,128,192]{2,1,0:T(8,128)(2,1)S(1)} %fusion.2), channel_id=1, source_target_pairs={{0,3},{1,2},{2,1},{3,0},{4,7},{5,6},{6,5},{7,4},{8,11},{9,10},{10,... | collective-permute-start | bytes 442376 | tf_op jit(solution)/shard_map/ppermute | solution.py:15
  30.4 4.6 %collective-permute-done.10 = bf16[3,128,192]{2,1,0:T(8,128)(2,1)S(1)} collective-permute-done((bf16[3,128,192]{2,1,0:T(8,128)(2,1)S(1)}, bf16[3,128,192]{2,1,0:T(8,128)(2,1)S(1)}, u32[]{:S(2)}, u32[]{:S(2)}) %collective-permute-start.10) | collective-permute-done | bytes 147488 | tf_op jit(solution)/shard_map/ppermute | solution.py:15
  35.2 3.2 %collective-permute-done.7.refs_0_ = bf16[128,1024]{1,0:T(8,128)(2,1)S(1)} collective-permute-done((bf16[128,1024]{1,0:T(8,128)(2,1)S(1)}, bf16[128,1024]{1,0:T(8,128)(2,1)S(1)}, u32[]{:S(2)}, u32[]{:S(2)}) %collective-permute-start.7) | collective-permute-done | bytes 262176 | tf_op jit(solution)/shard_map/ppermute | solution.py:15
  40.0 10.1 %collective-permute-done.11.refs_0_ = bf16[128,1024]{1,0:T(8,128)(2,1)S(1)} collective-permute-done((bf16[128,1024]{1,0:T(8,128)(2,1)S(1)}, bf16[128,1024]{1,0:T(8,128)(2,1)S(1)}, u32[]{:S(2)}, u32[]{:S(2)}) %collective-permute-start.11) | collective-permute-done | bytes 262176 | tf_op jit(solution)/shard_map/ppermute | solution.py:15
  50.2 3.5 %collective-permute-done.12.refs_1_ = bf16[128,1024]{1,0:T(8,128)(2,1)S(1)} collective-permute-done((bf16[128,1024]{1,0:T(8,128)(2,1)S(1)}, bf16[128,1024]{1,0:T(8,128)(2,1)S(1)}, u32[]{:S(2)}, u32[]{:S(2)}) %collective-permute-start.12) | collective-permute-done | bytes 262176 | tf_op jit(solution)/shard_map/ppermute | solution.py:15
  54.7 1.1 %collective-permute-done.2 = f32[192]{0:T(256)S(1)} collective-permute-done((f32[192]{0:T(256)S(1)}, f32[192]{0:T(256)S(1)}, u32[]{:S(2)}, u32[]{:S(2)}) %collective-permute-start.2) | collective-permute-done | bytes 800 | tf_op jit(solution)/shard_map/ppermute | solution.py:15
  56.2 2.7 %collective-permute-done.3 = f32[192]{0:T(256)S(1)} collective-permute-done((f32[192]{0:T(256)S(1)}, f32[192]{0:T(256)S(1)}, u32[]{:S(2)}, u32[]{:S(2)}) %collective-permute-start.3) | collective-permute-done | bytes 800 | tf_op jit(solution)/shard_map/ppermute | solution.py:15
  58.8 6.6 %collective-permute-done.13.r_ref.refs_6_ = bf16[128,1024]{1,0:T(8,128)(2,1)S(1)} collective-permute-done((bf16[128,1024]{1,0:T(8,128)(2,1)S(1)}, bf16[128,1024]{1,0:T(8,128)(2,1)S(1)}, u32[]{:S(2)}, u32[]{:S(2)}) %collective-permute-start.13) | collective-permute-done | bytes 262176 | tf_op jit(solution)/shard_map/ppermute | solution.py:15
  65.5 1.2 %collective-permute-done.14.r_ref.refs_5_ = bf16[128,1024]{1,0:T(8,128)(2,1)S(1)} collective-permute-done((bf16[128,1024]{1,0:T(8,128)(2,1)S(1)}, bf16[128,1024]{1,0:T(8,128)(2,1)S(1)}, u32[]{:S(2)}, u32[]{:S(2)}) %collective-permute-start.14) | collective-permute-done | bytes 262176 | tf_op jit(solution)/shard_map/ppermute | solution.py:15
  67.8 1.3 %collective-permute-done.15 = bf16[3,128,192]{2,1,0:T(8,128)(2,1)S(1)} collective-permute-done((bf16[3,128,192]{2,1,0:T(8,128)(2,1)S(1)}, bf16[3,128,192]{2,1,0:T(8,128)(2,1)S(1)}, u32[]{:S(2)}, u32[]{:S(2)}) %collective-permute-start.15) | collective-permute-done | bytes 147488 | tf_op jit(solution)/shard_map/ppermute | solution.py:15
  69.4 3.6 %collective-permute-done.17.r_ref.refs_7_ = bf16[128,1024]{1,0:T(8,128)(2,1)S(1)} collective-permute-done((bf16[128,1024]{1,0:T(8,128)(2,1)S(1)}, bf16[128,1024]{1,0:T(8,128)(2,1)S(1)}, u32[]{:S(2)}, u32[]{:S(2)}) %collective-permute-start.17) | collective-permute-done | bytes 262176 | tf_op jit(solution)/shard_map/ppermute | solution.py:15
  73.4 1.5 %dec_add.1 = f32[192,1024]{1,0:T(8,128)} custom-call(f32[192,1024]{1,0:T(8,128)S(1)} %convert_multiply_fusion.total_ref, bf16[128,192]{1,0:T(8,128)(2,1)S(1)} %get-tuple-element.63.c_ref.refs_0_, bf16[128,192]{1,0:T(8,128)(2,1)S(1)} %get-tuple-element.40.c_ref.refs_1_, bf16[128,192]{1,0:T(8,128)(2,1)S(1)} %get-tuple-element.59.c_ref.refs_2_, ...), custom_call_target="tpu_custom_call" | custom-call | flops 1000000 | bytes 1000000 | tf_op jit(solution)/shard_map/dec_add/pallas_call | solution.py:75
  74.9 1.2 %collective-permute-done.16 = bf16[3,128,192]{2,1,0:T(8,128)(2,1)S(1)} collective-permute-done((bf16[3,128,192]{2,1,0:T(8,128)(2,1)S(1)}, bf16[3,128,192]{2,1,0:T(8,128)(2,1)S(1)}, u32[]{:S(2)}, u32[]{:S(2)}) %collective-permute-start.16) | collective-permute-done | bytes 147488 | tf_op jit(solution)/shard_map/ppermute | solution.py:15
  76.5 3.8 %collective-permute-done.19 = bf16[128,192]{1,0:T(8,128)(2,1)S(1)} collective-permute-done((bf16[128,192]{1,0:T(8,128)(2,1)S(1)}, bf16[128,192]{1,0:T(8,128)(2,1)S(1)}, u32[]{:S(2)}, u32[]{:S(2)}) %collective-permute-start.19) | collective-permute-done | bytes 49184 | tf_op jit(solution)/shard_map/ppermute | solution.py:15
  81.2 1.7 %collective-permute-start.20 = (f32[1,1024]{1,0:T(1,128)S(1)}, f32[1,1024]{1,0:T(1,128)S(1)}, u32[]{:S(2)}, u32[]{:S(2)}) collective-permute-start(f32[1,1024]{1,0:T(1,128)S(1)} %get-tuple-element.53), channel_id=1, source_target_pairs={{0,4},{4,0},{8,12},{12,8},{1,5},{5,1},{9,13},{13,9},{2,6},{6,2},{1... | collective-permute-start | bytes 12296 | tf_op jit(solution)/shard_map/ppermute | solution.py:15
  82.9 2.7 %collective-permute-start.22 = (f32[1,1024]{1,0:T(1,128)S(1)}, f32[1,1024]{1,0:T(1,128)S(1)}, u32[]{:S(2)}, u32[]{:S(2)}) collective-permute-start(f32[1,1024]{1,0:T(1,128)S(1)} %get-tuple-element.53), channel_id=1, source_target_pairs={{0,12},{4,8},{8,4},{12,0},{1,13},{5,9},{9,5},{13,1},{2,14},{6,10},... | collective-permute-start | bytes 12296 | tf_op jit(solution)/shard_map/ppermute | solution.py:15
  85.6 1.5 %enc_end.1 = f32[192,1024]{1,0:T(8,128)} custom-call(bf16[4,128,192]{2,1,0:T(8,128)(2,1)S(1)} %get-tuple-element.46.g_ref, bf16[128,1024]{1,0:T(8,128)(2,1)S(1)} %get-tuple-element.47.refs_0_, bf16[128,1024]{1,0:T(8,128)(2,1)S(1)} %get-tuple-element.48.refs_1_, bf16[128,1024]{1,0:T(8,128)(2,1)S(1)} %get-tuple-element.49.refs_2_, ...), custom_call_target="tpu_custom_call" | custom-call | flops 1000000 | bytes 1000000 | tf_op jit(solution)/shard_map/enc_end/pallas_call | solution.py:75
  (74 shorter events, 14.3 us)
Async XLA Ops:
  0.6 12.6 %collective-permute-start = (bf16[128,1024]{1,0:T(8,128)(2,1)}, bf16[128,1024]{1,0:T(8,128)(2,1)S(1)}, u32[]{:S(2)}, u32[]{:S(2)}) collective-permute-start(bf16[128,1024]{1,0:T(8,128)(2,1)} %x_ref.3), channel_id=1, source_target_pairs={{0,12},{4,8},{8,4},{12,0},{1,13},{5,9},{9,5},{13,1},{2,14},{6,10},... | collective-permute-start | bytes 786440 | tf_op jit(solution)/shard_map/ppermute | solution.py:15
  5.7 12.2 %collective-permute-start.1 = (bf16[128,1024]{1,0:T(8,128)(2,1)}, bf16[128,1024]{1,0:T(8,128)(2,1)S(1)}, u32[]{:S(2)}, u32[]{:S(2)}) collective-permute-start(bf16[128,1024]{1,0:T(8,128)(2,1)} %x_ref.3), channel_id=1, source_target_pairs={{0,4},{4,0},{8,12},{12,8},{1,5},{5,1},{9,13},{13,9},{2,6},{6,2},{1... | collective-permute-start | bytes 786440 | tf_op jit(solution)/shard_map/ppermute | solution.py:15
  18.0 8.2 %collective-permute-start.8 = (bf16[128,1024]{1,0:T(8,128)(2,1)S(1)}, bf16[128,1024]{1,0:T(8,128)(2,1)S(1)}, u32[]{:S(2)}, u32[]{:S(2)}) collective-permute-start(bf16[128,1024]{1,0:T(8,128)(2,1)S(1)} %collective-permute-done.x_ref), channel_id=1, source_target_pairs={{0,4},{4,0},{8,12},{12,8},{1,5},{5,1},{9,13},{13,9},{2,6},{6,2},{1... | collective-permute-start | bytes 786440 | tf_op jit(solution)/shard_map/ppermute | solution.py:15
  20.0 1.3 %collective-permute-start.4 = (bf16[64,192]{1,0:T(8,128)(2,1)S(1)}, bf16[64,192]{1,0:T(8,128)(2,1)S(1)}, u32[]{:S(2)}, u32[]{:S(2)}) collective-permute-start(bf16[64,192]{1,0:T(8,128)(2,1)S(1)} %broadcast_select_fusion.2), channel_id=1, source_target_pairs={{0,1},{1,0},{2,3},{3,2},{4,5},{5,4},{6,7},{7,6},{8,9},{9,8},{10,11... | collective-permute-start | bytes 73736 | tf_op jit(solution)/shard_map/ppermute | solution.py:15
  21.3 5.4 %collective-permute-start.5 = (bf16[64,192]{1,0:T(8,128)(2,1)S(1)}, bf16[64,192]{1,0:T(8,128)(2,1)S(1)}, u32[]{:S(2)}, u32[]{:S(2)}) collective-permute-start(bf16[64,192]{1,0:T(8,128)(2,1)S(1)} %fusion.12), channel_id=1, source_target_pairs={{0,3},{1,2},{2,1},{3,0},{4,7},{5,6},{6,5},{7,4},{8,11},{9,10},{10,... | collective-permute-start | bytes 73736 | tf_op jit(solution)/shard_map/ppermute | solution.py:15
  26.6 1.5 %collective-permute-start.9 = (bf16[3,128,192]{2,1,0:T(8,128)(2,1)S(1)}, bf16[3,128,192]{2,1,0:T(8,128)(2,1)S(1)}, u32[]{:S(2)}, u32[]{:S(2)}) collective-permute-start(bf16[3,128,192]{2,1,0:T(8,128)(2,1)S(1)} %fusion.1), channel_id=1, source_target_pairs={{0,1},{1,0},{2,3},{3,2},{4,5},{5,4},{6,7},{7,6},{8,9},{9,8},{10,11... | collective-permute-start | bytes 442376 | tf_op jit(solution)/shard_map/ppermute | solution.py:15
  27.2 2.2 %collective-permute-start.6 = (bf16[64,192]{1,0:T(8,128)(2,1)S(1)}, bf16[64,192]{1,0:T(8,128)(2,1)S(1)}, u32[]{:S(2)}, u32[]{:S(2)}) collective-permute-start(bf16[64,192]{1,0:T(8,128)(2,1)S(1)} %maximum_convert_fusion), channel_id=1, source_target_pairs={{0,1},{1,0},{2,3},{3,2},{4,5},{5,4},{6,7},{7,6},{8,9},{9,8},{10,11... | collective-permute-start | bytes 73736 | tf_op jit(solution)/shard_map/ppermute | solution.py:15
  28.1 6.9 %collective-permute-start.10 = (bf16[3,128,192]{2,1,0:T(8,128)(2,1)S(1)}, bf16[3,128,192]{2,1,0:T(8,128)(2,1)S(1)}, u32[]{:S(2)}, u32[]{:S(2)}) collective-permute-start(bf16[3,128,192]{2,1,0:T(8,128)(2,1)S(1)} %fusion.2), channel_id=1, source_target_pairs={{0,3},{1,2},{2,1},{3,0},{4,7},{5,6},{6,5},{7,4},{8,11},{9,10},{10,... | collective-permute-start | bytes 442376 | tf_op jit(solution)/shard_map/ppermute | solution.py:15
  29.7 8.6 %collective-permute-start.7 = (bf16[128,1024]{1,0:T(8,128)(2,1)S(1)}, bf16[128,1024]{1,0:T(8,128)(2,1)S(1)}, u32[]{:S(2)}, u32[]{:S(2)}) collective-permute-start(bf16[128,1024]{1,0:T(8,128)(2,1)S(1)} %recon_of.3), channel_id=1, source_target_pairs={{0,4},{4,0},{8,12},{12,8},{1,5},{5,1},{9,13},{13,9},{2,6},{6,2},{1... | collective-permute-start | bytes 786440 | tf_op jit(solution)/shard_map/ppermute | solution.py:15
  38.6 15.0 %copy-start.4 = (bf16[128,1024]{1,0:T(8,128)(2,1)S(1)}, bf16[128,1024]{1,0:T(8,128)(2,1)}, u32[]{:S(2)}) copy-start(bf16[128,1024]{1,0:T(8,128)(2,1)} %x_ref.3) | copy-start | bytes 786436
  38.9 11.3 %collective-permute-start.11 = (bf16[128,1024]{1,0:T(8,128)(2,1)S(1)}, bf16[128,1024]{1,0:T(8,128)(2,1)S(1)}, u32[]{:S(2)}, u32[]{:S(2)}) collective-permute-start(bf16[128,1024]{1,0:T(8,128)(2,1)S(1)} %recon_of.5), channel_id=1, source_target_pairs={{0,4},{4,0},{8,12},{12,8},{1,5},{5,1},{9,13},{13,9},{2,6},{6,2},{1... | collective-permute-start | bytes 786440 | tf_op jit(solution)/shard_map/ppermute | solution.py:15
  39.6 14.1 %collective-permute-start.12 = (bf16[128,1024]{1,0:T(8,128)(2,1)S(1)}, bf16[128,1024]{1,0:T(8,128)(2,1)S(1)}, u32[]{:S(2)}, u32[]{:S(2)}) collective-permute-start(bf16[128,1024]{1,0:T(8,128)(2,1)S(1)} %recon_of.4), channel_id=1, source_target_pairs={{0,8},{4,12},{8,0},{12,4},{1,9},{5,13},{9,1},{13,5},{2,10},{6,14},... | collective-permute-start | bytes 786440 | tf_op jit(solution)/shard_map/ppermute | solution.py:15
  54.1 11.3 %collective-permute-start.13 = (bf16[128,1024]{1,0:T(8,128)(2,1)S(1)}, bf16[128,1024]{1,0:T(8,128)(2,1)S(1)}, u32[]{:S(2)}, u32[]{:S(2)}) collective-permute-start(bf16[128,1024]{1,0:T(8,128)(2,1)S(1)} %get-tuple-element.41.refs_4_.res_ref), channel_id=1, source_target_pairs={{0,8},{4,12},{8,0},{12,4},{1,9},{5,13},{9,1},{13,5},{2,10},{6,14},... | collective-permute-start | bytes 786440 | tf_op jit(solution)/shard_map/ppermute | solution.py:15
  54.5 12.2 %collective-permute-start.14 = (bf16[128,1024]{1,0:T(8,128)(2,1)S(1)}, bf16[128,1024]{1,0:T(8,128)(2,1)S(1)}, u32[]{:S(2)}, u32[]{:S(2)}) collective-permute-start(bf16[128,1024]{1,0:T(8,128)(2,1)S(1)} %get-tuple-element.41.refs_4_.res_ref), channel_id=1, source_target_pairs={{0,4},{4,0},{8,12},{12,8},{1,5},{5,1},{9,13},{13,9},{2,6},{6,2},{1... | collective-permute-start | bytes 786440 | tf_op jit(solution)/shard_map/ppermute | solution.py:15
  54.6 1.2 %collective-permute-start.2 = (f32[192]{0:T(256)S(1)}, f32[192]{0:T(256)S(1)}, u32[]{:S(2)}, u32[]{:S(2)}) collective-permute-start(f32[192]{0:T(256)S(1)} %multiply_reduce_fusion), channel_id=1, source_target_pairs={{0,1},{1,0},{2,3},{3,2},{4,5},{5,4},{6,7},{7,6},{8,9},{9,8},{10,11... | collective-permute-start | bytes 2312 | tf_op jit(solution)/shard_map/ppermute | solution.py:15
  55.8 3.0 %collective-permute-start.3 = (f32[192]{0:T(256)S(1)}, f32[192]{0:T(256)S(1)}, u32[]{:S(2)}, u32[]{:S(2)}) collective-permute-start(f32[192]{0:T(256)S(1)} %add.82), channel_id=1, source_target_pairs={{0,3},{1,2},{2,1},{3,0},{4,7},{5,6},{6,5},{7,4},{8,11},{9,10},{10,... | collective-permute-start | bytes 2312 | tf_op jit(solution)/shard_map/ppermute | solution.py:15
  66.6 6.4 %collective-permute-start.17 = (bf16[128,1024]{1,0:T(8,128)(2,1)S(1)}, bf16[128,1024]{1,0:T(8,128)(2,1)S(1)}, u32[]{:S(2)}, u32[]{:S(2)}) collective-permute-start(bf16[128,1024]{1,0:T(8,128)(2,1)S(1)} %collective-permute-done.13.r_ref.refs_6_), channel_id=1, source_target_pairs={{0,4},{4,0},{8,12},{12,8},{1,5},{5,1},{9,13},{13,9},{2,6},{6,2},{1... | collective-permute-start | bytes 786440 | tf_op jit(solution)/shard_map/ppermute | solution.py:15
  67.6 1.5 %collective-permute-start.15 = (bf16[3,128,192]{2,1,0:T(8,128)(2,1)S(1)}, bf16[3,128,192]{2,1,0:T(8,128)(2,1)S(1)}, u32[]{:S(2)}, u32[]{:S(2)}) collective-permute-start(bf16[3,128,192]{2,1,0:T(8,128)(2,1)S(1)} %fusion), channel_id=1, source_target_pairs={{0,1},{1,0},{2,3},{3,2},{4,5},{5,4},{6,7},{7,6},{8,9},{9,8},{10,11... | collective-permute-start | bytes 442376 | tf_op jit(solution)/shard_map/ppermute | solution.py:15
  69.1 6.9 %collective-permute-start.16 = (bf16[3,128,192]{2,1,0:T(8,128)(2,1)S(1)}, bf16[3,128,192]{2,1,0:T(8,128)(2,1)S(1)}, u32[]{:S(2)}, u32[]{:S(2)}) collective-permute-start(bf16[3,128,192]{2,1,0:T(8,128)(2,1)S(1)} %fusion.3), channel_id=1, source_target_pairs={{0,3},{1,2},{2,1},{3,0},{4,7},{5,6},{6,5},{7,4},{8,11},{9,10},{10,... | collective-permute-start | bytes 442376 | tf_op jit(solution)/shard_map/ppermute | solution.py:15
  73.3 2.9 %collective-permute-start.18 = (bf16[128,192]{1,0:T(8,128)(2,1)S(1)}, bf16[128,192]{1,0:T(8,128)(2,1)S(1)}, u32[]{:S(2)}, u32[]{:S(2)}) collective-permute-start(bf16[128,192]{1,0:T(8,128)(2,1)S(1)} %fusion.10), channel_id=1, source_target_pairs={{0,1},{1,0},{2,3},{3,2},{4,5},{5,4},{6,7},{7,6},{8,9},{9,8},{10,11... | collective-permute-start | bytes 147464 | tf_op jit(solution)/shard_map/ppermute | solution.py:15
  76.2 4.1 %collective-permute-start.19 = (bf16[128,192]{1,0:T(8,128)(2,1)S(1)}, bf16[128,192]{1,0:T(8,128)(2,1)S(1)}, u32[]{:S(2)}, u32[]{:S(2)}) collective-permute-start(bf16[128,192]{1,0:T(8,128)(2,1)S(1)} %fusion.11), channel_id=1, source_target_pairs={{0,3},{1,2},{2,1},{3,0},{4,7},{5,6},{6,5},{7,4},{8,11},{9,10},{10,... | collective-permute-start | bytes 147464 | tf_op jit(solution)/shard_map/ppermute | solution.py:15
  81.2 5.9 %collective-permute-start.20 = (f32[1,1024]{1,0:T(1,128)S(1)}, f32[1,1024]{1,0:T(1,128)S(1)}, u32[]{:S(2)}, u32[]{:S(2)}) collective-permute-start(f32[1,1024]{1,0:T(1,128)S(1)} %get-tuple-element.53), channel_id=1, source_target_pairs={{0,4},{4,0},{8,12},{12,8},{1,5},{5,1},{9,13},{13,9},{2,6},{6,2},{1... | collective-permute-start | bytes 12296 | tf_op jit(solution)/shard_map/ppermute | solution.py:15
  82.9 4.5 %collective-permute-start.21 = (f32[1,1024]{1,0:T(1,128)S(1)}, f32[1,1024]{1,0:T(1,128)S(1)}, u32[]{:S(2)}, u32[]{:S(2)}) collective-permute-start(f32[1,1024]{1,0:T(1,128)S(1)} %get-tuple-element.53), channel_id=1, source_target_pairs={{0,8},{4,12},{8,0},{12,4},{1,9},{5,13},{9,1},{13,5},{2,10},{6,14},... | collective-permute-start | bytes 12296 | tf_op jit(solution)/shard_map/ppermute | solution.py:15
  82.9 5.4 %collective-permute-start.22 = (f32[1,1024]{1,0:T(1,128)S(1)}, f32[1,1024]{1,0:T(1,128)S(1)}, u32[]{:S(2)}, u32[]{:S(2)}) collective-permute-start(f32[1,1024]{1,0:T(1,128)S(1)} %get-tuple-element.53), channel_id=1, source_target_pairs={{0,12},{4,8},{8,4},{12,0},{1,13},{5,9},{9,5},{13,1},{2,14},{6,10},... | collective-permute-start | bytes 12296 | tf_op jit(solution)/shard_map/ppermute | solution.py:15
  (7 other events, 31.9 us)

commit v7 on v6

--- a/solution.py
+++ b/solution.py
@@ -249,7 +249,7 @@
     )
     grad_enc = enc_end(centered, grads).T
     if line:
-        near, far, cross = (lat_swap(share, k) for k in others)
+        cross, far, near = stage(*(lat_swap(share, k) for k in (3, 2, 1)))
         grad_bdec = (share + near) + (far + cross)
     else:
         grad_bdec, step = share, 1

time: 89.1 us -> 88.8 us (level)
  transfers between devices with their start and end apart: 23 -> 23, of which waited for: 19 -> 18; matrix products, arithmetic and copies ran while one was open for 1% -> 1% of each run, Pallas kernels for 6% -> 6%
where the time goes in v7:
time: 88.8 us; the launch traced here: 88.6 us
  waiting for transfers between devices  58.5 us (66%)
  starting transfers between devices  17.6 us (20%)
  Pallas kernels  6.82 us (8%)
  local copies, waits for them, and re-layouts  3.23 us (4%)
  other arithmetic  1.49 us (2%)
  between operations  0.93 us (1%)
    ppermute x23, waiting for transfers between devices, swap(): return lax.ppermute(value, axis, [(i, i ^ distance) for i in range(count)])  58.5 us
    ppermute x23, starting transfers between devices, swap(): return lax.ppermute(value, axis, [(i, i ^ distance) for i in range(count)])  17.6 us
    pallas_call x14, Pallas kernels, call(): pl.pallas_call(kernel, out_shape=[jax.ShapeDtypeStruct(shape, kind) for s...  6.82 us
    unnamed x16, local copies, waits for them, and re-layouts  3.2 us
  transfers between devices with their start and end apart: 23, of which 18 were waited for; matrix products, arithmetic and copies ran while one was open for 1% of the time, Pallas kernels for 6%

profile of v7, /device:TPU:0, one launch (start us, length us, event | category | flops | bytes accessed | tf_op | source)
XLA Modules:
  0.0 88.6 jit_solution(6626674040607324317)
XLA Ops:
  0.6 5.1 %collective-permute-start = (bf16[128,1024]{1,0:T(8,128)(2,1)}, bf16[128,1024]{1,0:T(8,128)(2,1)S(1)}, u32[]{:S(2)}, u32[]{:S(2)}) collective-permute-start(bf16[128,1024]{1,0:T(8,128)(2,1)} %x_ref.3), channel_id=1, source_target_pairs={{0,12},{4,8},{8,4},{12,0},{1,13},{5,9},{9,5},{13,1},{2,14},{6,10},... | collective-permute-start | bytes 786440 | tf_op jit(solution)/shard_map/ppermute | solution.py:15
  6.4 1.0 %copy-done.1 = bf16[1024,192]{0,1:T(8,128)(2,1)S(1)} copy-done((bf16[1024,192]{0,1:T(8,128)(2,1)S(1)}, bf16[1024,192]{0,1:T(8,128)(2,1)}, u32[]{:S(2)}) %copy-start.1) | copy-done | bytes 393240
  8.7 4.5 %collective-permute-done.x_ref = bf16[128,1024]{1,0:T(8,128)(2,1)S(1)} collective-permute-done((bf16[128,1024]{1,0:T(8,128)(2,1)}, bf16[128,1024]{1,0:T(8,128)(2,1)S(1)}, u32[]{:S(2)}, u32[]{:S(2)}) %collective-permute-start) | collective-permute-done | bytes 262176 | tf_op jit(solution)/shard_map/ppermute | solution.py:15
  13.2 4.8 %collective-permute-done.1.x_ref = bf16[128,1024]{1,0:T(8,128)(2,1)S(1)} collective-permute-done((bf16[128,1024]{1,0:T(8,128)(2,1)}, bf16[128,1024]{1,0:T(8,128)(2,1)S(1)}, u32[]{:S(2)}, u32[]{:S(2)}) %collective-permute-start.1) | collective-permute-done | bytes 262176 | tf_op jit(solution)/shard_map/ppermute | solution.py:15
  18.0 1.7 %collective-permute-start.8 = (bf16[128,1024]{1,0:T(8,128)(2,1)S(1)}, bf16[128,1024]{1,0:T(8,128)(2,1)S(1)}, u32[]{:S(2)}, u32[]{:S(2)}) collective-permute-start(bf16[128,1024]{1,0:T(8,128)(2,1)S(1)} %collective-permute-done.x_ref), channel_id=1, source_target_pairs={{0,4},{4,0},{8,12},{12,8},{1,5},{5,1},{9,13},{13,9},{2,6},{6,2},{1... | collective-permute-start | bytes 786440 | tf_op jit(solution)/shard_map/ppermute | solution.py:15
  21.3 1.3 %collective-permute-start.5 = (bf16[64,192]{1,0:T(8,128)(2,1)S(1)}, bf16[64,192]{1,0:T(8,128)(2,1)S(1)}, u32[]{:S(2)}, u32[]{:S(2)}) collective-permute-start(bf16[64,192]{1,0:T(8,128)(2,1)S(1)} %fusion.12), channel_id=1, source_target_pairs={{0,3},{1,2},{2,1},{3,0},{4,7},{5,6},{6,5},{7,4},{8,11},{9,10},{10,... | collective-permute-start | bytes 73736 | tf_op jit(solution)/shard_map/ppermute | solution.py:15
  22.6 3.6 %collective-permute-done.8.x_ref = bf16[128,1024]{1,0:T(8,128)(2,1)S(1)} collective-permute-done((bf16[128,1024]{1,0:T(8,128)(2,1)S(1)}, bf16[128,1024]{1,0:T(8,128)(2,1)S(1)}, u32[]{:S(2)}, u32[]{:S(2)}) %collective-permute-start.8) | collective-permute-done | bytes 262176 | tf_op jit(solution)/shard_map/ppermute | solution.py:15
  28.1 1.3 %collective-permute-start.10 = (bf16[3,128,192]{2,1,0:T(8,128)(2,1)S(1)}, bf16[3,128,192]{2,1,0:T(8,128)(2,1)S(1)}, u32[]{:S(2)}, u32[]{:S(2)}) collective-permute-start(bf16[3,128,192]{2,1,0:T(8,128)(2,1)S(1)} %fusion.2), channel_id=1, source_target_pairs={{0,3},{1,2},{2,1},{3,0},{4,7},{5,6},{6,5},{7,4},{8,11},{9,10},{10,... | collective-permute-start | bytes 442376 | tf_op jit(solution)/shard_map/ppermute | solution.py:15
  30.4 4.6 %collective-permute-done.10 = bf16[3,128,192]{2,1,0:T(8,128)(2,1)S(1)} collective-permute-done((bf16[3,128,192]{2,1,0:T(8,128)(2,1)S(1)}, bf16[3,128,192]{2,1,0:T(8,128)(2,1)S(1)}, u32[]{:S(2)}, u32[]{:S(2)}) %collective-permute-start.10) | collective-permute-done | bytes 147488 | tf_op jit(solution)/shard_map/ppermute | solution.py:15
  35.2 3.2 %collective-permute-done.7.refs_0_ = bf16[128,1024]{1,0:T(8,128)(2,1)S(1)} collective-permute-done((bf16[128,1024]{1,0:T(8,128)(2,1)S(1)}, bf16[128,1024]{1,0:T(8,128)(2,1)S(1)}, u32[]{:S(2)}, u32[]{:S(2)}) %collective-permute-start.7) | collective-permute-done | bytes 262176 | tf_op jit(solution)/shard_map/ppermute | solution.py:15
  40.0 10.1 %collective-permute-done.11.refs_0_ = bf16[128,1024]{1,0:T(8,128)(2,1)S(1)} collective-permute-done((bf16[128,1024]{1,0:T(8,128)(2,1)S(1)}, bf16[128,1024]{1,0:T(8,128)(2,1)S(1)}, u32[]{:S(2)}, u32[]{:S(2)}) %collective-permute-start.11) | collective-permute-done | bytes 262176 | tf_op jit(solution)/shard_map/ppermute | solution.py:15
  50.2 3.5 %collective-permute-done.12.refs_1_ = bf16[128,1024]{1,0:T(8,128)(2,1)S(1)} collective-permute-done((bf16[128,1024]{1,0:T(8,128)(2,1)S(1)}, bf16[128,1024]{1,0:T(8,128)(2,1)S(1)}, u32[]{:S(2)}, u32[]{:S(2)}) %collective-permute-start.12) | collective-permute-done | bytes 262176 | tf_op jit(solution)/shard_map/ppermute | solution.py:15
  54.7 1.1 %collective-permute-done.2 = f32[192]{0:T(256)S(1)} collective-permute-done((f32[192]{0:T(256)S(1)}, f32[192]{0:T(256)S(1)}, u32[]{:S(2)}, u32[]{:S(2)}) %collective-permute-start.2) | collective-permute-done | bytes 800 | tf_op jit(solution)/shard_map/ppermute | solution.py:15
  56.2 2.7 %collective-permute-done.3 = f32[192]{0:T(256)S(1)} collective-permute-done((f32[192]{0:T(256)S(1)}, f32[192]{0:T(256)S(1)}, u32[]{:S(2)}, u32[]{:S(2)}) %collective-permute-start.3) | collective-permute-done | bytes 800 | tf_op jit(solution)/shard_map/ppermute | solution.py:15
  58.8 6.6 %collective-permute-done.13.r_ref.refs_6_ = bf16[128,1024]{1,0:T(8,128)(2,1)S(1)} collective-permute-done((bf16[128,1024]{1,0:T(8,128)(2,1)S(1)}, bf16[128,1024]{1,0:T(8,128)(2,1)S(1)}, u32[]{:S(2)}, u32[]{:S(2)}) %collective-permute-start.13) | collective-permute-done | bytes 262176 | tf_op jit(solution)/shard_map/ppermute | solution.py:15
  65.5 1.2 %collective-permute-done.14.r_ref.refs_5_ = bf16[128,1024]{1,0:T(8,128)(2,1)S(1)} collective-permute-done((bf16[128,1024]{1,0:T(8,128)(2,1)S(1)}, bf16[128,1024]{1,0:T(8,128)(2,1)S(1)}, u32[]{:S(2)}, u32[]{:S(2)}) %collective-permute-start.14) | collective-permute-done | bytes 262176 | tf_op jit(solution)/shard_map/ppermute | solution.py:15
  67.8 1.3 %collective-permute-done.15 = bf16[3,128,192]{2,1,0:T(8,128)(2,1)S(1)} collective-permute-done((bf16[3,128,192]{2,1,0:T(8,128)(2,1)S(1)}, bf16[3,128,192]{2,1,0:T(8,128)(2,1)S(1)}, u32[]{:S(2)}, u32[]{:S(2)}) %collective-permute-start.15) | collective-permute-done | bytes 147488 | tf_op jit(solution)/shard_map/ppermute | solution.py:15
  69.4 3.6 %collective-permute-done.17.r_ref.refs_7_ = bf16[128,1024]{1,0:T(8,128)(2,1)S(1)} collective-permute-done((bf16[128,1024]{1,0:T(8,128)(2,1)S(1)}, bf16[128,1024]{1,0:T(8,128)(2,1)S(1)}, u32[]{:S(2)}, u32[]{:S(2)}) %collective-permute-start.17) | collective-permute-done | bytes 262176 | tf_op jit(solution)/shard_map/ppermute | solution.py:15
  73.4 1.5 %dec_add.1 = f32[192,1024]{1,0:T(8,128)} custom-call(f32[192,1024]{1,0:T(8,128)S(1)} %convert_multiply_fusion.total_ref, bf16[128,192]{1,0:T(8,128)(2,1)S(1)} %get-tuple-element.69.c_ref.refs_0_, bf16[128,192]{1,0:T(8,128)(2,1)S(1)} %get-tuple-element.43.c_ref.refs_1_, bf16[128,192]{1,0:T(8,128)(2,1)S(1)} %get-tuple-element.65.c_ref.refs_2_, ...), custom_call_target="tpu_custom_call" | custom-call | flops 1000000 | bytes 1000000 | tf_op jit(solution)/shard_map/dec_add/pallas_call | solution.py:75
  74.9 1.2 %collective-permute-done.16 = bf16[3,128,192]{2,1,0:T(8,128)(2,1)S(1)} collective-permute-done((bf16[3,128,192]{2,1,0:T(8,128)(2,1)S(1)}, bf16[3,128,192]{2,1,0:T(8,128)(2,1)S(1)}, u32[]{:S(2)}, u32[]{:S(2)}) %collective-permute-start.16) | collective-permute-done | bytes 147488 | tf_op jit(solution)/shard_map/ppermute | solution.py:15
  76.5 3.8 %collective-permute-done.19 = bf16[128,192]{1,0:T(8,128)(2,1)S(1)} collective-permute-done((bf16[128,192]{1,0:T(8,128)(2,1)S(1)}, bf16[128,192]{1,0:T(8,128)(2,1)S(1)}, u32[]{:S(2)}, u32[]{:S(2)}) %collective-permute-start.19) | collective-permute-done | bytes 49184 | tf_op jit(solution)/shard_map/ppermute | solution.py:15
  81.6 2.8 %collective-permute-start.21 = (f32[1,1024]{1,0:T(1,128)S(1)}, f32[1,1024]{1,0:T(1,128)S(1)}, u32[]{:S(2)}, u32[]{:S(2)}) collective-permute-start(f32[1,1024]{1,0:T(1,128)S(1)} %get-tuple-element.56), channel_id=1, source_target_pairs={{0,8},{4,12},{8,0},{12,4},{1,9},{5,13},{9,1},{13,5},{2,10},{6,14},... | collective-permute-start | bytes 12296 | tf_op jit(solution)/shard_map/ppermute | solution.py:15
  84.4 1.2 %collective-permute-start.22 = (f32[1,1024]{1,0:T(1,128)S(1)}, f32[1,1024]{1,0:T(1,128)S(1)}, u32[]{:S(2)}, u32[]{:S(2)}) collective-permute-start(f32[1,1024]{1,0:T(1,128)S(1)} %get-tuple-element.56), channel_id=1, source_target_pairs={{0,4},{4,0},{8,12},{12,8},{1,5},{5,1},{9,13},{13,9},{2,6},{6,2},{1... | collective-permute-start | bytes 12296 | tf_op jit(solution)/shard_map/ppermute | solution.py:15
  85.6 1.5 %enc_end.1 = f32[192,1024]{1,0:T(8,128)} custom-call(bf16[4,128,192]{2,1,0:T(8,128)(2,1)S(1)} %get-tuple-element.49.g_ref, bf16[128,1024]{1,0:T(8,128)(2,1)S(1)} %get-tuple-element.50.refs_0_, bf16[128,1024]{1,0:T(8,128)(2,1)S(1)} %get-tuple-element.51.refs_1_, bf16[128,1024]{1,0:T(8,128)(2,1)S(1)} %get-tuple-element.52.refs_2_, ...), custom_call_target="tpu_custom_call" | custom-call | flops 1000000 | bytes 1000000 | tf_op jit(solution)/shard_map/enc_end/pallas_call | solution.py:75
  (74 shorter events, 14.4 us)
Async XLA Ops:
  0.6 12.6 %collective-permute-start = (bf16[128,1024]{1,0:T(8,128)(2,1)}, bf16[128,1024]{1,0:T(8,128)(2,1)S(1)}, u32[]{:S(2)}, u32[]{:S(2)}) collective-permute-start(bf16[128,1024]{1,0:T(8,128)(2,1)} %x_ref.3), channel_id=1, source_target_pairs={{0,12},{4,8},{8,4},{12,0},{1,13},{5,9},{9,5},{13,1},{2,14},{6,10},... | collective-permute-start | bytes 786440 | tf_op jit(solution)/shard_map/ppermute | solution.py:15
  5.7 12.2 %collective-permute-start.1 = (bf16[128,1024]{1,0:T(8,128)(2,1)}, bf16[128,1024]{1,0:T(8,128)(2,1)S(1)}, u32[]{:S(2)}, u32[]{:S(2)}) collective-permute-start(bf16[128,1024]{1,0:T(8,128)(2,1)} %x_ref.3), channel_id=1, source_target_pairs={{0,4},{4,0},{8,12},{12,8},{1,5},{5,1},{9,13},{13,9},{2,6},{6,2},{1... | collective-permute-start | bytes 786440 | tf_op jit(solution)/shard_map/ppermute | solution.py:15
  18.0 8.2 %collective-permute-start.8 = (bf16[128,1024]{1,0:T(8,128)(2,1)S(1)}, bf16[128,1024]{1,0:T(8,128)(2,1)S(1)}, u32[]{:S(2)}, u32[]{:S(2)}) collective-permute-start(bf16[128,1024]{1,0:T(8,128)(2,1)S(1)} %collective-permute-done.x_ref), channel_id=1, source_target_pairs={{0,4},{4,0},{8,12},{12,8},{1,5},{5,1},{9,13},{13,9},{2,6},{6,2},{1... | collective-permute-start | bytes 786440 | tf_op jit(solution)/shard_map/ppermute | solution.py:15
  20.0 1.3 %collective-permute-start.4 = (bf16[64,192]{1,0:T(8,128)(2,1)S(1)}, bf16[64,192]{1,0:T(8,128)(2,1)S(1)}, u32[]{:S(2)}, u32[]{:S(2)}) collective-permute-start(bf16[64,192]{1,0:T(8,128)(2,1)S(1)} %broadcast_select_fusion.2), channel_id=1, source_target_pairs={{0,1},{1,0},{2,3},{3,2},{4,5},{5,4},{6,7},{7,6},{8,9},{9,8},{10,11... | collective-permute-start | bytes 73736 | tf_op jit(solution)/shard_map/ppermute | solution.py:15
  21.3 5.4 %collective-permute-start.5 = (bf16[64,192]{1,0:T(8,128)(2,1)S(1)}, bf16[64,192]{1,0:T(8,128)(2,1)S(1)}, u32[]{:S(2)}, u32[]{:S(2)}) collective-permute-start(bf16[64,192]{1,0:T(8,128)(2,1)S(1)} %fusion.12), channel_id=1, source_target_pairs={{0,3},{1,2},{2,1},{3,0},{4,7},{5,6},{6,5},{7,4},{8,11},{9,10},{10,... | collective-permute-start | bytes 73736 | tf_op jit(solution)/shard_map/ppermute | solution.py:15
  26.6 1.5 %collective-permute-start.9 = (bf16[3,128,192]{2,1,0:T(8,128)(2,1)S(1)}, bf16[3,128,192]{2,1,0:T(8,128)(2,1)S(1)}, u32[]{:S(2)}, u32[]{:S(2)}) collective-permute-start(bf16[3,128,192]{2,1,0:T(8,128)(2,1)S(1)} %fusion.1), channel_id=1, source_target_pairs={{0,1},{1,0},{2,3},{3,2},{4,5},{5,4},{6,7},{7,6},{8,9},{9,8},{10,11... | collective-permute-start | bytes 442376 | tf_op jit(solution)/shard_map/ppermute | solution.py:15
  27.2 2.2 %collective-permute-start.6 = (bf16[64,192]{1,0:T(8,128)(2,1)S(1)}, bf16[64,192]{1,0:T(8,128)(2,1)S(1)}, u32[]{:S(2)}, u32[]{:S(2)}) collective-permute-start(bf16[64,192]{1,0:T(8,128)(2,1)S(1)} %maximum_convert_fusion), channel_id=1, source_target_pairs={{0,1},{1,0},{2,3},{3,2},{4,5},{5,4},{6,7},{7,6},{8,9},{9,8},{10,11... | collective-permute-start | bytes 73736 | tf_op jit(solution)/shard_map/ppermute | solution.py:15
  28.1 6.9 %collective-permute-start.10 = (bf16[3,128,192]{2,1,0:T(8,128)(2,1)S(1)}, bf16[3,128,192]{2,1,0:T(8,128)(2,1)S(1)}, u32[]{:S(2)}, u32[]{:S(2)}) collective-permute-start(bf16[3,128,192]{2,1,0:T(8,128)(2,1)S(1)} %fusion.2), channel_id=1, source_target_pairs={{0,3},{1,2},{2,1},{3,0},{4,7},{5,6},{6,5},{7,4},{8,11},{9,10},{10,... | collective-permute-start | bytes 442376 | tf_op jit(solution)/shard_map/ppermute | solution.py:15
  29.7 8.6 %collective-permute-start.7 = (bf16[128,1024]{1,0:T(8,128)(2,1)S(1)}, bf16[128,1024]{1,0:T(8,128)(2,1)S(1)}, u32[]{:S(2)}, u32[]{:S(2)}) collective-permute-start(bf16[128,1024]{1,0:T(8,128)(2,1)S(1)} %recon_of.3), channel_id=1, source_target_pairs={{0,4},{4,0},{8,12},{12,8},{1,5},{5,1},{9,13},{13,9},{2,6},{6,2},{1... | collective-permute-start | bytes 786440 | tf_op jit(solution)/shard_map/ppermute | solution.py:15
  38.6 15.0 %copy-start.4 = (bf16[128,1024]{1,0:T(8,128)(2,1)S(1)}, bf16[128,1024]{1,0:T(8,128)(2,1)}, u32[]{:S(2)}) copy-start(bf16[128,1024]{1,0:T(8,128)(2,1)} %x_ref.3) | copy-start | bytes 786436
  38.9 11.3 %collective-permute-start.11 = (bf16[128,1024]{1,0:T(8,128)(2,1)S(1)}, bf16[128,1024]{1,0:T(8,128)(2,1)S(1)}, u32[]{:S(2)}, u32[]{:S(2)}) collective-permute-start(bf16[128,1024]{1,0:T(8,128)(2,1)S(1)} %recon_of.5), channel_id=1, source_target_pairs={{0,4},{4,0},{8,12},{12,8},{1,5},{5,1},{9,13},{13,9},{2,6},{6,2},{1... | collective-permute-start | bytes 786440 | tf_op jit(solution)/shard_map/ppermute | solution.py:15
  39.6 14.1 %collective-permute-start.12 = (bf16[128,1024]{1,0:T(8,128)(2,1)S(1)}, bf16[128,1024]{1,0:T(8,128)(2,1)S(1)}, u32[]{:S(2)}, u32[]{:S(2)}) collective-permute-start(bf16[128,1024]{1,0:T(8,128)(2,1)S(1)} %recon_of.4), channel_id=1, source_target_pairs={{0,8},{4,12},{8,0},{12,4},{1,9},{5,13},{9,1},{13,5},{2,10},{6,14},... | collective-permute-start | bytes 786440 | tf_op jit(solution)/shard_map/ppermute | solution.py:15
  54.1 11.3 %collective-permute-start.13 = (bf16[128,1024]{1,0:T(8,128)(2,1)S(1)}, bf16[128,1024]{1,0:T(8,128)(2,1)S(1)}, u32[]{:S(2)}, u32[]{:S(2)}) collective-permute-start(bf16[128,1024]{1,0:T(8,128)(2,1)S(1)} %get-tuple-element.44.refs_4_.res_ref), channel_id=1, source_target_pairs={{0,8},{4,12},{8,0},{12,4},{1,9},{5,13},{9,1},{13,5},{2,10},{6,14},... | collective-permute-start | bytes 786440 | tf_op jit(solution)/shard_map/ppermute | solution.py:15
  54.5 12.2 %collective-permute-start.14 = (bf16[128,1024]{1,0:T(8,128)(2,1)S(1)}, bf16[128,1024]{1,0:T(8,128)(2,1)S(1)}, u32[]{:S(2)}, u32[]{:S(2)}) collective-permute-start(bf16[128,1024]{1,0:T(8,128)(2,1)S(1)} %get-tuple-element.44.refs_4_.res_ref), channel_id=1, source_target_pairs={{0,4},{4,0},{8,12},{12,8},{1,5},{5,1},{9,13},{13,9},{2,6},{6,2},{1... | collective-permute-start | bytes 786440 | tf_op jit(solution)/shard_map/ppermute | solution.py:15
  54.6 1.2 %collective-permute-start.2 = (f32[192]{0:T(256)S(1)}, f32[192]{0:T(256)S(1)}, u32[]{:S(2)}, u32[]{:S(2)}) collective-permute-start(f32[192]{0:T(256)S(1)} %multiply_reduce_fusion), channel_id=1, source_target_pairs={{0,1},{1,0},{2,3},{3,2},{4,5},{5,4},{6,7},{7,6},{8,9},{9,8},{10,11... | collective-permute-start | bytes 2312 | tf_op jit(solution)/shard_map/ppermute | solution.py:15
  55.8 3.0 %collective-permute-start.3 = (f32[192]{0:T(256)S(1)}, f32[192]{0:T(256)S(1)}, u32[]{:S(2)}, u32[]{:S(2)}) collective-permute-start(f32[192]{0:T(256)S(1)} %add.82), channel_id=1, source_target_pairs={{0,3},{1,2},{2,1},{3,0},{4,7},{5,6},{6,5},{7,4},{8,11},{9,10},{10,... | collective-permute-start | bytes 2312 | tf_op jit(solution)/shard_map/ppermute | solution.py:15
  66.6 6.4 %collective-permute-start.17 = (bf16[128,1024]{1,0:T(8,128)(2,1)S(1)}, bf16[128,1024]{1,0:T(8,128)(2,1)S(1)}, u32[]{:S(2)}, u32[]{:S(2)}) collective-permute-start(bf16[128,1024]{1,0:T(8,128)(2,1)S(1)} %collective-permute-done.13.r_ref.refs_6_), channel_id=1, source_target_pairs={{0,4},{4,0},{8,12},{12,8},{1,5},{5,1},{9,13},{13,9},{2,6},{6,2},{1... | collective-permute-start | bytes 786440 | tf_op jit(solution)/shard_map/ppermute | solution.py:15
  67.6 1.5 %collective-permute-start.15 = (bf16[3,128,192]{2,1,0:T(8,128)(2,1)S(1)}, bf16[3,128,192]{2,1,0:T(8,128)(2,1)S(1)}, u32[]{:S(2)}, u32[]{:S(2)}) collective-permute-start(bf16[3,128,192]{2,1,0:T(8,128)(2,1)S(1)} %fusion), channel_id=1, source_target_pairs={{0,1},{1,0},{2,3},{3,2},{4,5},{5,4},{6,7},{7,6},{8,9},{9,8},{10,11... | collective-permute-start | bytes 442376 | tf_op jit(solution)/shard_map/ppermute | solution.py:15
  69.1 6.9 %collective-permute-start.16 = (bf16[3,128,192]{2,1,0:T(8,128)(2,1)S(1)}, bf16[3,128,192]{2,1,0:T(8,128)(2,1)S(1)}, u32[]{:S(2)}, u32[]{:S(2)}) collective-permute-start(bf16[3,128,192]{2,1,0:T(8,128)(2,1)S(1)} %fusion.3), channel_id=1, source_target_pairs={{0,3},{1,2},{2,1},{3,0},{4,7},{5,6},{6,5},{7,4},{8,11},{9,10},{10,... | collective-permute-start | bytes 442376 | tf_op jit(solution)/shard_map/ppermute | solution.py:15
  73.3 2.9 %collective-permute-start.18 = (bf16[128,192]{1,0:T(8,128)(2,1)S(1)}, bf16[128,192]{1,0:T(8,128)(2,1)S(1)}, u32[]{:S(2)}, u32[]{:S(2)}) collective-permute-start(bf16[128,192]{1,0:T(8,128)(2,1)S(1)} %fusion.10), channel_id=1, source_target_pairs={{0,1},{1,0},{2,3},{3,2},{4,5},{5,4},{6,7},{7,6},{8,9},{9,8},{10,11... | collective-permute-start | bytes 147464 | tf_op jit(solution)/shard_map/ppermute | solution.py:15
  76.2 4.1 %collective-permute-start.19 = (bf16[128,192]{1,0:T(8,128)(2,1)S(1)}, bf16[128,192]{1,0:T(8,128)(2,1)S(1)}, u32[]{:S(2)}, u32[]{:S(2)}) collective-permute-start(bf16[128,192]{1,0:T(8,128)(2,1)S(1)} %fusion.11), channel_id=1, source_target_pairs={{0,3},{1,2},{2,1},{3,0},{4,7},{5,6},{6,5},{7,4},{8,11},{9,10},{10,... | collective-permute-start | bytes 147464 | tf_op jit(solution)/shard_map/ppermute | solution.py:15
  81.2 5.9 %collective-permute-start.20 = (f32[1,1024]{1,0:T(1,128)S(1)}, f32[1,1024]{1,0:T(1,128)S(1)}, u32[]{:S(2)}, u32[]{:S(2)}) collective-permute-start(f32[1,1024]{1,0:T(1,128)S(1)} %get-tuple-element.56), channel_id=1, source_target_pairs={{0,12},{4,8},{8,4},{12,0},{1,13},{5,9},{9,5},{13,1},{2,14},{6,10},... | collective-permute-start | bytes 12296 | tf_op jit(solution)/shard_map/ppermute | solution.py:15
  81.6 5.5 %collective-permute-start.21 = (f32[1,1024]{1,0:T(1,128)S(1)}, f32[1,1024]{1,0:T(1,128)S(1)}, u32[]{:S(2)}, u32[]{:S(2)}) collective-permute-start(f32[1,1024]{1,0:T(1,128)S(1)} %get-tuple-element.56), channel_id=1, source_target_pairs={{0,8},{4,12},{8,0},{12,4},{1,9},{5,13},{9,1},{13,5},{2,10},{6,14},... | collective-permute-start | bytes 12296 | tf_op jit(solution)/shard_map/ppermute | solution.py:15
  84.4 3.6 %collective-permute-start.22 = (f32[1,1024]{1,0:T(1,128)S(1)}, f32[1,1024]{1,0:T(1,128)S(1)}, u32[]{:S(2)}, u32[]{:S(2)}) collective-permute-start(f32[1,1024]{1,0:T(1,128)S(1)} %get-tuple-element.56), channel_id=1, source_target_pairs={{0,4},{4,0},{8,12},{12,8},{1,5},{5,1},{9,13},{13,9},{2,6},{6,2},{1... | collective-permute-start | bytes 12296 | tf_op jit(solution)/shard_map/ppermute | solution.py:15
  (7 other events, 31.9 us)

commit v8 on v7

--- a/solution.py
+++ b/solution.py
@@ -137,7 +137,7 @@
     return call(kernel, "dec_add", outs, total, *codes, *res, *shares)
 
 
-def pre_grads(codes, sums, threshold, w_enc_t, res):
+def pre_grads(codes, sums, threshold, w_enc_t, res_sum):
     count = len(codes)
 
     def kernel(n_ref, w_ref, res_ref, *refs):
@@ -157,12 +157,12 @@
         pieces = jnp.where(row == 0, high.astype(f32), jnp.where(row == 1, mid.astype(f32), 0.0))
         pieces = jnp.where(row == 2, low.astype(f32), pieces).astype(bf16)
         product = jnp.sum(mm(pieces, w_ref[...], (1, 0)), axis=0, keepdims=True)
-        share[...] = jnp.sum(res_ref[...].astype(f32), axis=0, keepdims=True) - product
+        share[...] = res_ref[...] - product
 
     lat, cols = w_enc_t.shape
     outs = [((count, *codes[0].shape), bf16), ((1, lat), f32), ((1, cols), f32)]
     grads, bias, share = call(
-        kernel, "pre_grads", outs, threshold[None], w_enc_t, res, *codes, *sums
+        kernel, "pre_grads", outs, threshold[None], w_enc_t, res_sum, *codes, *sums
     )
     return grads, bias[0], share
 
@@ -243,9 +243,10 @@
     norms = jnp.sqrt(squares + 1e-06)
     sparsity = (sparsity_coef * row_scale * code_total / norms)[:, None] * w_dec.astype(f32)
     (grad_dec,) = dec_add(sparsity, codes, res)
-    code_sums[-1], grad_dec = stage(code_sums[-1], grad_dec)
+    res_sum = jnp.sum(res_grad.astype(f32), axis=0, keepdims=True)
+    code_sums[-1], grad_dec, res_sum = stage(code_sums[-1], grad_dec, res_sum)
     grads, grad_benc, share = pre_grads(
-        codes, code_sums, sparsity_coef * row_scale * norms, w_enc_t, res_grad
+        codes, code_sums, sparsity_coef * row_scale * norms, w_enc_t, res_sum
     )
     grad_enc = enc_end(centered, grads).T
     if line:

time: 88.8 us -> 90 us (1.014)
  transfers between devices with their start and end apart: 23 -> 23, of which waited for: 18 -> 17; matrix products, arithmetic and copies ran while one was open for 1% -> 1% of each run, Pallas kernels for 6% -> 5%
where the time goes in v8:
time: 90 us; the launch traced here: 89.8 us
  waiting for transfers between devices  59.2 us (66%)
  starting transfers between devices  18.1 us (20%)
  Pallas kernels  6.8 us (8%)
  local copies, waits for them, and re-layouts  3.23 us (4%)
  other arithmetic  1.54 us (2%)
  between operations  0.91 us (1%)
    ppermute x23, waiting for transfers between devices, swap(): return lax.ppermute(value, axis, [(i, i ^ distance) for i in range(count)])  59.2 us
    ppermute x23, starting transfers between devices, swap(): return lax.ppermute(value, axis, [(i, i ^ distance) for i in range(count)])  18.1 us
    pallas_call x14, Pallas kernels, call(): pl.pallas_call(kernel, out_shape=[jax.ShapeDtypeStruct(shape, kind) for s...  6.8 us
    unnamed x16, local copies, waits for them, and re-layouts  3.2 us
  transfers between devices with their start and end apart: 23, of which 17 were waited for; matrix products, arithmetic and copies ran while one was open for 1% of the time, Pallas kernels for 5%

profile of v8, /device:TPU:0, one launch (start us, length us, event | category | flops | bytes accessed | tf_op | source)
XLA Modules:
  0.0 89.8 jit_solution(157431896875685555)
XLA Ops:
  0.6 5.1 %collective-permute-start = (bf16[128,1024]{1,0:T(8,128)(2,1)}, bf16[128,1024]{1,0:T(8,128)(2,1)S(1)}, u32[]{:S(2)}, u32[]{:S(2)}) collective-permute-start(bf16[128,1024]{1,0:T(8,128)(2,1)} %x_ref.3), channel_id=1, source_target_pairs={{0,12},{4,8},{8,4},{12,0},{1,13},{5,9},{9,5},{13,1},{2,14},{6,10},... | collective-permute-start | bytes 786440 | tf_op jit(solution)/shard_map/ppermute | solution.py:15
  6.4 1.0 %copy-done.1 = bf16[1024,192]{0,1:T(8,128)(2,1)S(1)} copy-done((bf16[1024,192]{0,1:T(8,128)(2,1)S(1)}, bf16[1024,192]{0,1:T(8,128)(2,1)}, u32[]{:S(2)}) %copy-start.1) | copy-done | bytes 393240
  7.4 0.9 %copy-done.3 = bf16[128,1024]{1,0:T(8,128)(2,1)S(1)} copy-done((bf16[128,1024]{1,0:T(8,128)(2,1)S(1)}, bf16[128,1024]{1,0:T(8,128)(2,1)}, u32[]{:S(2)}) %copy-start.3) | copy-done | bytes 262168
  8.7 4.5 %collective-permute-done.x_ref = bf16[128,1024]{1,0:T(8,128)(2,1)S(1)} collective-permute-done((bf16[128,1024]{1,0:T(8,128)(2,1)}, bf16[128,1024]{1,0:T(8,128)(2,1)S(1)}, u32[]{:S(2)}, u32[]{:S(2)}) %collective-permute-start) | collective-permute-done | bytes 262176 | tf_op jit(solution)/shard_map/ppermute | solution.py:15
  13.2 4.8 %collective-permute-done.1.x_ref = bf16[128,1024]{1,0:T(8,128)(2,1)S(1)} collective-permute-done((bf16[128,1024]{1,0:T(8,128)(2,1)}, bf16[128,1024]{1,0:T(8,128)(2,1)S(1)}, u32[]{:S(2)}, u32[]{:S(2)}) %collective-permute-start.1) | collective-permute-done | bytes 262176 | tf_op jit(solution)/shard_map/ppermute | solution.py:15
  18.3 1.7 %collective-permute-start.8 = (bf16[128,1024]{1,0:T(8,128)(2,1)S(1)}, bf16[128,1024]{1,0:T(8,128)(2,1)S(1)}, u32[]{:S(2)}, u32[]{:S(2)}) collective-permute-start(bf16[128,1024]{1,0:T(8,128)(2,1)S(1)} %collective-permute-done.x_ref), channel_id=1, source_target_pairs={{0,4},{4,0},{8,12},{12,8},{1,5},{5,1},{9,13},{13,9},{2,6},{6,2},{1... | collective-permute-start | bytes 786440 | tf_op jit(solution)/shard_map/ppermute | solution.py:15
  20.3 0.9 %collective-permute-done.4 = bf16[64,192]{1,0:T(8,128)(2,1)S(1)} collective-permute-done((bf16[64,192]{1,0:T(8,128)(2,1)S(1)}, bf16[64,192]{1,0:T(8,128)(2,1)S(1)}, u32[]{:S(2)}, u32[]{:S(2)}) %collective-permute-start.4) | collective-permute-done | bytes 24608 | tf_op jit(solution)/shard_map/ppermute | solution.py:15
  21.3 1.3 %collective-permute-start.5 = (bf16[64,192]{1,0:T(8,128)(2,1)S(1)}, bf16[64,192]{1,0:T(8,128)(2,1)S(1)}, u32[]{:S(2)}, u32[]{:S(2)}) collective-permute-start(bf16[64,192]{1,0:T(8,128)(2,1)S(1)} %fusion.12), channel_id=1, source_target_pairs={{0,3},{1,2},{2,1},{3,0},{4,7},{5,6},{6,5},{7,4},{8,11},{9,10},{10,... | collective-permute-start | bytes 73736 | tf_op jit(solution)/shard_map/ppermute | solution.py:15
  22.6 4.0 %collective-permute-done.8.x_ref = bf16[128,1024]{1,0:T(8,128)(2,1)S(1)} collective-permute-done((bf16[128,1024]{1,0:T(8,128)(2,1)S(1)}, bf16[128,1024]{1,0:T(8,128)(2,1)S(1)}, u32[]{:S(2)}, u32[]{:S(2)}) %collective-permute-start.8) | collective-permute-done | bytes 262176 | tf_op jit(solution)/shard_map/ppermute | solution.py:15
  28.5 1.3 %collective-permute-start.10 = (bf16[3,128,192]{2,1,0:T(8,128)(2,1)S(1)}, bf16[3,128,192]{2,1,0:T(8,128)(2,1)S(1)}, u32[]{:S(2)}, u32[]{:S(2)}) collective-permute-start(bf16[3,128,192]{2,1,0:T(8,128)(2,1)S(1)} %fusion.2), channel_id=1, source_target_pairs={{0,3},{1,2},{2,1},{3,0},{4,7},{5,6},{6,5},{7,4},{8,11},{9,10},{10,... | collective-permute-start | bytes 442376 | tf_op jit(solution)/shard_map/ppermute | solution.py:15
  30.8 4.6 %collective-permute-done.10 = bf16[3,128,192]{2,1,0:T(8,128)(2,1)S(1)} collective-permute-done((bf16[3,128,192]{2,1,0:T(8,128)(2,1)S(1)}, bf16[3,128,192]{2,1,0:T(8,128)(2,1)S(1)}, u32[]{:S(2)}, u32[]{:S(2)}) %collective-permute-start.10) | collective-permute-done | bytes 147488 | tf_op jit(solution)/shard_map/ppermute | solution.py:15
  35.5 3.2 %collective-permute-done.7.refs_0_ = bf16[128,1024]{1,0:T(8,128)(2,1)S(1)} collective-permute-done((bf16[128,1024]{1,0:T(8,128)(2,1)S(1)}, bf16[128,1024]{1,0:T(8,128)(2,1)S(1)}, u32[]{:S(2)}, u32[]{:S(2)}) %collective-permute-start.7) | collective-permute-done | bytes 262176 | tf_op jit(solution)/shard_map/ppermute | solution.py:15
  40.4 10.1 %collective-permute-done.11.refs_0_ = bf16[128,1024]{1,0:T(8,128)(2,1)S(1)} collective-permute-done((bf16[128,1024]{1,0:T(8,128)(2,1)S(1)}, bf16[128,1024]{1,0:T(8,128)(2,1)S(1)}, u32[]{:S(2)}, u32[]{:S(2)}) %collective-permute-start.11) | collective-permute-done | bytes 262176 | tf_op jit(solution)/shard_map/ppermute | solution.py:15
  50.5 3.5 %collective-permute-done.12.refs_1_ = bf16[128,1024]{1,0:T(8,128)(2,1)S(1)} collective-permute-done((bf16[128,1024]{1,0:T(8,128)(2,1)S(1)}, bf16[128,1024]{1,0:T(8,128)(2,1)S(1)}, u32[]{:S(2)}, u32[]{:S(2)}) %collective-permute-start.12) | collective-permute-done | bytes 262176 | tf_op jit(solution)/shard_map/ppermute | solution.py:15
  55.0 1.1 %collective-permute-done.2 = f32[192]{0:T(256)S(1)} collective-permute-done((f32[192]{0:T(256)S(1)}, f32[192]{0:T(256)S(1)}, u32[]{:S(2)}, u32[]{:S(2)}) %collective-permute-start.2) | collective-permute-done | bytes 800 | tf_op jit(solution)/shard_map/ppermute | solution.py:15
  56.5 2.6 %collective-permute-done.3 = f32[192]{0:T(256)S(1)} collective-permute-done((f32[192]{0:T(256)S(1)}, f32[192]{0:T(256)S(1)}, u32[]{:S(2)}, u32[]{:S(2)}) %collective-permute-start.3) | collective-permute-done | bytes 800 | tf_op jit(solution)/shard_map/ppermute | solution.py:15
  59.2 6.6 %collective-permute-done.13.refs_6_.r_ref = bf16[128,1024]{1,0:T(8,128)(2,1)S(1)} collective-permute-done((bf16[128,1024]{1,0:T(8,128)(2,1)S(1)}, bf16[128,1024]{1,0:T(8,128)(2,1)S(1)}, u32[]{:S(2)}, u32[]{:S(2)}) %collective-permute-start.13) | collective-permute-done | bytes 262176 | tf_op jit(solution)/shard_map/ppermute | solution.py:15
  65.8 1.2 %collective-permute-done.14.refs_5_.r_ref = bf16[128,1024]{1,0:T(8,128)(2,1)S(1)} collective-permute-done((bf16[128,1024]{1,0:T(8,128)(2,1)S(1)}, bf16[128,1024]{1,0:T(8,128)(2,1)S(1)}, u32[]{:S(2)}, u32[]{:S(2)}) %collective-permute-start.14) | collective-permute-done | bytes 262176 | tf_op jit(solution)/shard_map/ppermute | solution.py:15
  69.5 7.1 %collective-permute-done.15.r_ref.refs_7_ = bf16[128,1024]{1,0:T(8,128)(2,1)S(1)} collective-permute-done((bf16[128,1024]{1,0:T(8,128)(2,1)S(1)}, bf16[128,1024]{1,0:T(8,128)(2,1)S(1)}, u32[]{:S(2)}, u32[]{:S(2)}) %collective-permute-start.15) | collective-permute-done | bytes 262176 | tf_op jit(solution)/shard_map/ppermute | solution.py:15
  76.9 1.5 %dec_add.1 = f32[192,1024]{1,0:T(8,128)} custom-call(f32[192,1024]{1,0:T(8,128)S(1)} %convert_multiply_fusion.total_ref, bf16[128,192]{1,0:T(8,128)(2,1)S(1)} %get-tuple-element.71.c_ref.refs_0_, bf16[128,192]{1,0:T(8,128)(2,1)S(1)} %get-tuple-element.44.c_ref.refs_1_, bf16[128,192]{1,0:T(8,128)(2,1)S(1)} %get-tuple-element.67.c_ref.refs_2_, ...), custom_call_target="tpu_custom_call" | custom-call | flops 1000000 | bytes 1000000 | tf_op jit(solution)/shard_map/dec_add/pallas_call | solution.py:75
  79.2 3.1 %collective-permute-done.17 = bf16[128,192]{1,0:T(8,128)(2,1)S(1)} collective-permute-done((bf16[128,192]{1,0:T(8,128)(2,1)S(1)}, bf16[128,192]{1,0:T(8,128)(2,1)S(1)}, u32[]{:S(2)}, u32[]{:S(2)}) %collective-permute-start.17) | collective-permute-done | bytes 49184 | tf_op jit(solution)/shard_map/ppermute | solution.py:15
  83.3 1.7 %collective-permute-start.21 = (f32[1,1024]{1,0:T(1,128)S(1)}, f32[1,1024]{1,0:T(1,128)S(1)}, u32[]{:S(2)}, u32[]{:S(2)}) collective-permute-start(f32[1,1024]{1,0:T(1,128)S(1)} %get-tuple-element.58), channel_id=1, source_target_pairs={{0,8},{4,12},{8,0},{12,4},{1,9},{5,13},{9,1},{13,5},{2,10},{6,14},... | collective-permute-start | bytes 12296 | tf_op jit(solution)/shard_map/ppermute | solution.py:15
  85.0 2.6 %collective-permute-start.22 = (f32[1,1024]{1,0:T(1,128)S(1)}, f32[1,1024]{1,0:T(1,128)S(1)}, u32[]{:S(2)}, u32[]{:S(2)}) collective-permute-start(f32[1,1024]{1,0:T(1,128)S(1)} %get-tuple-element.58), channel_id=1, source_target_pairs={{0,4},{4,0},{8,12},{12,8},{1,5},{5,1},{9,13},{13,9},{2,6},{6,2},{1... | collective-permute-start | bytes 12296 | tf_op jit(solution)/shard_map/ppermute | solution.py:15
  87.6 1.5 %enc_end.1 = f32[192,1024]{1,0:T(8,128)} custom-call(bf16[4,128,192]{2,1,0:T(8,128)(2,1)S(1)} %get-tuple-element.51.g_ref, bf16[128,1024]{1,0:T(8,128)(2,1)S(1)} %get-tuple-element.52.refs_0_, bf16[128,1024]{1,0:T(8,128)(2,1)S(1)} %get-tuple-element.53.refs_1_, bf16[128,1024]{1,0:T(8,128)(2,1)S(1)} %get-tuple-element.54.refs_2_, ...), custom_call_target="tpu_custom_call" | custom-call | flops 1000000 | bytes 1000000 | tf_op jit(solution)/shard_map/enc_end/pallas_call | solution.py:75
  (75 shorter events, 12.7 us)
Async XLA Ops:
  0.6 12.6 %collective-permute-start = (bf16[128,1024]{1,0:T(8,128)(2,1)}, bf16[128,1024]{1,0:T(8,128)(2,1)S(1)}, u32[]{:S(2)}, u32[]{:S(2)}) collective-permute-start(bf16[128,1024]{1,0:T(8,128)(2,1)} %x_ref.3), channel_id=1, source_target_pairs={{0,12},{4,8},{8,4},{12,0},{1,13},{5,9},{9,5},{13,1},{2,14},{6,10},... | collective-permute-start | bytes 786440 | tf_op jit(solution)/shard_map/ppermute | solution.py:15
  5.7 12.2 %collective-permute-start.1 = (bf16[128,1024]{1,0:T(8,128)(2,1)}, bf16[128,1024]{1,0:T(8,128)(2,1)S(1)}, u32[]{:S(2)}, u32[]{:S(2)}) collective-permute-start(bf16[128,1024]{1,0:T(8,128)(2,1)} %x_ref.3), channel_id=1, source_target_pairs={{0,4},{4,0},{8,12},{12,8},{1,5},{5,1},{9,13},{13,9},{2,6},{6,2},{1... | collective-permute-start | bytes 786440 | tf_op jit(solution)/shard_map/ppermute | solution.py:15
  18.3 8.3 %collective-permute-start.8 = (bf16[128,1024]{1,0:T(8,128)(2,1)S(1)}, bf16[128,1024]{1,0:T(8,128)(2,1)S(1)}, u32[]{:S(2)}, u32[]{:S(2)}) collective-permute-start(bf16[128,1024]{1,0:T(8,128)(2,1)S(1)} %collective-permute-done.x_ref), channel_id=1, source_target_pairs={{0,4},{4,0},{8,12},{12,8},{1,5},{5,1},{9,13},{13,9},{2,6},{6,2},{1... | collective-permute-start | bytes 786440 | tf_op jit(solution)/shard_map/ppermute | solution.py:15
  20.0 1.2 %collective-permute-start.4 = (bf16[64,192]{1,0:T(8,128)(2,1)S(1)}, bf16[64,192]{1,0:T(8,128)(2,1)S(1)}, u32[]{:S(2)}, u32[]{:S(2)}) collective-permute-start(bf16[64,192]{1,0:T(8,128)(2,1)S(1)} %broadcast_select_fusion.2), channel_id=1, source_target_pairs={{0,1},{1,0},{2,3},{3,2},{4,5},{5,4},{6,7},{7,6},{8,9},{9,8},{10,11... | collective-permute-start | bytes 73736 | tf_op jit(solution)/shard_map/ppermute | solution.py:15
  21.3 5.7 %collective-permute-start.5 = (bf16[64,192]{1,0:T(8,128)(2,1)S(1)}, bf16[64,192]{1,0:T(8,128)(2,1)S(1)}, u32[]{:S(2)}, u32[]{:S(2)}) collective-permute-start(bf16[64,192]{1,0:T(8,128)(2,1)S(1)} %fusion.12), channel_id=1, source_target_pairs={{0,3},{1,2},{2,1},{3,0},{4,7},{5,6},{6,5},{7,4},{8,11},{9,10},{10,... | collective-permute-start | bytes 73736 | tf_op jit(solution)/shard_map/ppermute | solution.py:15
  26.9 1.5 %collective-permute-start.9 = (bf16[3,128,192]{2,1,0:T(8,128)(2,1)S(1)}, bf16[3,128,192]{2,1,0:T(8,128)(2,1)S(1)}, u32[]{:S(2)}, u32[]{:S(2)}) collective-permute-start(bf16[3,128,192]{2,1,0:T(8,128)(2,1)S(1)} %fusion.1), channel_id=1, source_target_pairs={{0,1},{1,0},{2,3},{3,2},{4,5},{5,4},{6,7},{7,6},{8,9},{9,8},{10,11... | collective-permute-start | bytes 442376 | tf_op jit(solution)/shard_map/ppermute | solution.py:15
  27.6 2.2 %collective-permute-start.6 = (bf16[64,192]{1,0:T(8,128)(2,1)S(1)}, bf16[64,192]{1,0:T(8,128)(2,1)S(1)}, u32[]{:S(2)}, u32[]{:S(2)}) collective-permute-start(bf16[64,192]{1,0:T(8,128)(2,1)S(1)} %maximum_convert_fusion), channel_id=1, source_target_pairs={{0,1},{1,0},{2,3},{3,2},{4,5},{5,4},{6,7},{7,6},{8,9},{9,8},{10,11... | collective-permute-start | bytes 73736 | tf_op jit(solution)/shard_map/ppermute | solution.py:15
  28.5 6.9 %collective-permute-start.10 = (bf16[3,128,192]{2,1,0:T(8,128)(2,1)S(1)}, bf16[3,128,192]{2,1,0:T(8,128)(2,1)S(1)}, u32[]{:S(2)}, u32[]{:S(2)}) collective-permute-start(bf16[3,128,192]{2,1,0:T(8,128)(2,1)S(1)} %fusion.2), channel_id=1, source_target_pairs={{0,3},{1,2},{2,1},{3,0},{4,7},{5,6},{6,5},{7,4},{8,11},{9,10},{10,... | collective-permute-start | bytes 442376 | tf_op jit(solution)/shard_map/ppermute | solution.py:15
  30.1 8.6 %collective-permute-start.7 = (bf16[128,1024]{1,0:T(8,128)(2,1)S(1)}, bf16[128,1024]{1,0:T(8,128)(2,1)S(1)}, u32[]{:S(2)}, u32[]{:S(2)}) collective-permute-start(bf16[128,1024]{1,0:T(8,128)(2,1)S(1)} %recon_of.3), channel_id=1, source_target_pairs={{0,4},{4,0},{8,12},{12,8},{1,5},{5,1},{9,13},{13,9},{2,6},{6,2},{1... | collective-permute-start | bytes 786440 | tf_op jit(solution)/shard_map/ppermute | solution.py:15
  39.0 15.0 %copy-start.4 = (bf16[128,1024]{1,0:T(8,128)(2,1)S(1)}, bf16[128,1024]{1,0:T(8,128)(2,1)}, u32[]{:S(2)}) copy-start(bf16[128,1024]{1,0:T(8,128)(2,1)} %x_ref.3) | copy-start | bytes 786436
  39.3 11.3 %collective-permute-start.11 = (bf16[128,1024]{1,0:T(8,128)(2,1)S(1)}, bf16[128,1024]{1,0:T(8,128)(2,1)S(1)}, u32[]{:S(2)}, u32[]{:S(2)}) collective-permute-start(bf16[128,1024]{1,0:T(8,128)(2,1)S(1)} %recon_of.5), channel_id=1, source_target_pairs={{0,4},{4,0},{8,12},{12,8},{1,5},{5,1},{9,13},{13,9},{2,6},{6,2},{1... | collective-permute-start | bytes 786440 | tf_op jit(solution)/shard_map/ppermute | solution.py:15
  40.0 14.0 %collective-permute-start.12 = (bf16[128,1024]{1,0:T(8,128)(2,1)S(1)}, bf16[128,1024]{1,0:T(8,128)(2,1)S(1)}, u32[]{:S(2)}, u32[]{:S(2)}) collective-permute-start(bf16[128,1024]{1,0:T(8,128)(2,1)S(1)} %recon_of.4), channel_id=1, source_target_pairs={{0,8},{4,12},{8,0},{12,4},{1,9},{5,13},{9,1},{13,5},{2,10},{6,14},... | collective-permute-start | bytes 786440 | tf_op jit(solution)/shard_map/ppermute | solution.py:15
  54.5 11.3 %collective-permute-start.13 = (bf16[128,1024]{1,0:T(8,128)(2,1)S(1)}, bf16[128,1024]{1,0:T(8,128)(2,1)S(1)}, u32[]{:S(2)}, u32[]{:S(2)}) collective-permute-start(bf16[128,1024]{1,0:T(8,128)(2,1)S(1)} %get-tuple-element.45.refs_4_), channel_id=1, source_target_pairs={{0,8},{4,12},{8,0},{12,4},{1,9},{5,13},{9,1},{13,5},{2,10},{6,14},... | collective-permute-start | bytes 786440 | tf_op jit(solution)/shard_map/ppermute | solution.py:15
  54.8 12.2 %collective-permute-start.14 = (bf16[128,1024]{1,0:T(8,128)(2,1)S(1)}, bf16[128,1024]{1,0:T(8,128)(2,1)S(1)}, u32[]{:S(2)}, u32[]{:S(2)}) collective-permute-start(bf16[128,1024]{1,0:T(8,128)(2,1)S(1)} %get-tuple-element.45.refs_4_), channel_id=1, source_target_pairs={{0,4},{4,0},{8,12},{12,8},{1,5},{5,1},{9,13},{13,9},{2,6},{6,2},{1... | collective-permute-start | bytes 786440 | tf_op jit(solution)/shard_map/ppermute | solution.py:15
  55.0 1.2 %collective-permute-start.2 = (f32[192]{0:T(256)S(1)}, f32[192]{0:T(256)S(1)}, u32[]{:S(2)}, u32[]{:S(2)}) collective-permute-start(f32[192]{0:T(256)S(1)} %multiply_reduce_fusion), channel_id=1, source_target_pairs={{0,1},{1,0},{2,3},{3,2},{4,5},{5,4},{6,7},{7,6},{8,9},{9,8},{10,11... | collective-permute-start | bytes 2312 | tf_op jit(solution)/shard_map/ppermute | solution.py:15
  56.2 3.0 %collective-permute-start.3 = (f32[192]{0:T(256)S(1)}, f32[192]{0:T(256)S(1)}, u32[]{:S(2)}, u32[]{:S(2)}) collective-permute-start(f32[192]{0:T(256)S(1)} %add.82), channel_id=1, source_target_pairs={{0,3},{1,2},{2,1},{3,0},{4,7},{5,6},{6,5},{7,4},{8,11},{9,10},{10,... | collective-permute-start | bytes 2312 | tf_op jit(solution)/shard_map/ppermute | solution.py:15
  67.6 1.5 %collective-permute-start.18 = (bf16[3,128,192]{2,1,0:T(8,128)(2,1)S(1)}, bf16[3,128,192]{2,1,0:T(8,128)(2,1)S(1)}, u32[]{:S(2)}, u32[]{:S(2)}) collective-permute-start(bf16[3,128,192]{2,1,0:T(8,128)(2,1)S(1)} %fusion), channel_id=1, source_target_pairs={{0,1},{1,0},{2,3},{3,2},{4,5},{5,4},{6,7},{7,6},{8,9},{9,8},{10,11... | collective-permute-start | bytes 442376 | tf_op jit(solution)/shard_map/ppermute | solution.py:15
  67.8 8.8 %collective-permute-start.15 = (bf16[128,1024]{1,0:T(8,128)(2,1)S(1)}, bf16[128,1024]{1,0:T(8,128)(2,1)S(1)}, u32[]{:S(2)}, u32[]{:S(2)}) collective-permute-start(bf16[128,1024]{1,0:T(8,128)(2,1)S(1)} %collective-permute-done.13.refs_6_.r_ref), channel_id=1, source_target_pairs={{0,4},{4,0},{8,12},{12,8},{1,5},{5,1},{9,13},{13,9},{2,6},{6,2},{1... | collective-permute-start | bytes 786440 | tf_op jit(solution)/shard_map/ppermute | solution.py:15
  69.1 9.3 %collective-permute-start.19 = (bf16[3,128,192]{2,1,0:T(8,128)(2,1)S(1)}, bf16[3,128,192]{2,1,0:T(8,128)(2,1)S(1)}, u32[]{:S(2)}, u32[]{:S(2)}) collective-permute-start(bf16[3,128,192]{2,1,0:T(8,128)(2,1)S(1)} %fusion.3), channel_id=1, source_target_pairs={{0,3},{1,2},{2,1},{3,0},{4,7},{5,6},{6,5},{7,4},{8,11},{9,10},{10,... | collective-permute-start | bytes 442376 | tf_op jit(solution)/shard_map/ppermute | solution.py:15
  76.8 1.7 %collective-permute-start.16 = (bf16[128,192]{1,0:T(8,128)(2,1)S(1)}, bf16[128,192]{1,0:T(8,128)(2,1)S(1)}, u32[]{:S(2)}, u32[]{:S(2)}) collective-permute-start(bf16[128,192]{1,0:T(8,128)(2,1)S(1)} %fusion.10), channel_id=1, source_target_pairs={{0,1},{1,0},{2,3},{3,2},{4,5},{5,4},{6,7},{7,6},{8,9},{9,8},{10,11... | collective-permute-start | bytes 147464 | tf_op jit(solution)/shard_map/ppermute | solution.py:15
  78.5 3.8 %collective-permute-start.17 = (bf16[128,192]{1,0:T(8,128)(2,1)S(1)}, bf16[128,192]{1,0:T(8,128)(2,1)S(1)}, u32[]{:S(2)}, u32[]{:S(2)}) collective-permute-start(bf16[128,192]{1,0:T(8,128)(2,1)S(1)} %fusion.11), channel_id=1, source_target_pairs={{0,3},{1,2},{2,1},{3,0},{4,7},{5,6},{6,5},{7,4},{8,11},{9,10},{10,... | collective-permute-start | bytes 147464 | tf_op jit(solution)/shard_map/ppermute | solution.py:15
  83.2 5.9 %collective-permute-start.20 = (f32[1,1024]{1,0:T(1,128)S(1)}, f32[1,1024]{1,0:T(1,128)S(1)}, u32[]{:S(2)}, u32[]{:S(2)}) collective-permute-start(f32[1,1024]{1,0:T(1,128)S(1)} %get-tuple-element.58), channel_id=1, source_target_pairs={{0,12},{4,8},{8,4},{12,0},{1,13},{5,9},{9,5},{13,1},{2,14},{6,10},... | collective-permute-start | bytes 12296 | tf_op jit(solution)/shard_map/ppermute | solution.py:15
  83.3 5.7 %collective-permute-start.21 = (f32[1,1024]{1,0:T(1,128)S(1)}, f32[1,1024]{1,0:T(1,128)S(1)}, u32[]{:S(2)}, u32[]{:S(2)}) collective-permute-start(f32[1,1024]{1,0:T(1,128)S(1)} %get-tuple-element.58), channel_id=1, source_target_pairs={{0,8},{4,12},{8,0},{12,4},{1,9},{5,13},{9,1},{13,5},{2,10},{6,14},... | collective-permute-start | bytes 12296 | tf_op jit(solution)/shard_map/ppermute | solution.py:15
  85.0 4.2 %collective-permute-start.22 = (f32[1,1024]{1,0:T(1,128)S(1)}, f32[1,1024]{1,0:T(1,128)S(1)}, u32[]{:S(2)}, u32[]{:S(2)}) collective-permute-start(f32[1,1024]{1,0:T(1,128)S(1)} %get-tuple-element.58), channel_id=1, source_target_pairs={{0,4},{4,0},{8,12},{12,8},{1,5},{5,1},{9,13},{13,9},{2,6},{6,2},{1... | collective-permute-start | bytes 12296 | tf_op jit(solution)/shard_map/ppermute | solution.py:15
  (7 other events, 30.2 us)
